TPU v7x, 512 devices: a whole 4x4x16 slice. The times are simulated.
512 devices in a mesh: grp: 8 (over y, core), mem: 64 (over x, z).
Axes of the slice: x: 4, y: 4, z: 16, core: 2. Of those that a mesh axis runs over, the one named last changes fastest.
Arguments:
- tokens: bfloat16 [65536, 1024], P(('grp', 'mem')), may hold values from -6 to 6
- cotangent: bfloat16 [65536, 1024], P(('grp', 'mem')), may hold values from -6 to 6
- path: int32 [512, 3], P(('grp', 'mem')), may hold values from 0 to 1023, as said below
- coarse_weights: bfloat16 [4, 1024, 512], P(None, 'mem'), may hold values from -0.1875 to 0.1875
- middle_weights: bfloat16 [64, 1024, 256], P(None, 'mem'), may hold values from -0.1875 to 0.1875
- fine_weights: bfloat16 [1024, 1024, 128], P('grp', 'mem'), may hold values from -0.1875 to 0.1875
Outputs:
- tokens_grad: bfloat16 [65536, 1024], P(('grp', 'mem'))
- coarse_grad: bfloat16 [4, 1024, 512], P(None, 'mem')
- middle_grad: bfloat16 [64, 1024, 256], P(None, 'mem')
- fine_grad: bfloat16 [1024, 1024, 128], P('grp', 'mem')
Inputs may be any that keep to these rules, and one draw needn't show every extreme that they name: Row d is the path of document d: column 0 its coarse block, column 1 its middle block, column 2 its fine block, with middle = fine * 64 // 1024 and coarse = middle * 4 // 64. Some fine blocks are chosen by many documents.
All inputs are finite; a program needn't handle non-finite values.
Results may differ from a plain program's by a relative error of at most 0.005.
Values may be sent and summed in bfloat16 or wider, within the bound.
No kernel may reach another device: no remote copies, remote signals or barrier semaphores. Data moves between devices by JAX's collectives and lax.ppermute only.
A program may use at most 64 MiB of HBM per device.

v0:
```python
from functools import partial

import jax
import jax.numpy as jnp
from jax import lax
from jax.sharding import PartitionSpec as P


def contract_rows(left, right):
    return lax.dot_general(
        left, right, (((0,), (0,)), ((), ())), preferred_element_type=jnp.float32
    )


def level_terms(inputs, upstream, weights):
    hidden_width = weights.shape[1] // 2
    up_half = weights[:, :hidden_width]
    down_half = weights[:, hidden_width:]
    before = jnp.dot(inputs, up_half, preferred_element_type=jnp.float32)
    hidden, pullback = jax.vjp(partial(jax.nn.gelu, approximate=True), before)
    hidden_low = hidden.astype(jnp.bfloat16)
    hidden_grad = jnp.dot(upstream, down_half, preferred_element_type=jnp.float32)
    before_grad = pullback(hidden_grad)[0].astype(jnp.bfloat16)
    up_grad = contract_rows(inputs, before_grad)
    down_grad = contract_rows(upstream, hidden_low)
    input_part = lax.dot_general(
        before_grad, up_half, (((1,), (1,)), ((), ())), preferred_element_type=jnp.float32
    )
    return (jnp.concatenate([up_grad, down_grad], axis=1), input_part)


def one_hot_rows(identity, count):
    return (identity[:, None] == jnp.arange(count, dtype=jnp.int32)[None, :]).astype(jnp.bfloat16)


def select_blocks(picker, blocks):
    return jnp.einsum("mk,krh->mrh", picker, blocks, preferred_element_type=jnp.float32).astype(
        jnp.bfloat16
    )


def collect_blocks(picker, pieces):
    return jnp.einsum(
        "mk,mrh->krh", picker.astype(jnp.float32), pieces, precision=lax.Precision.HIGHEST
    )


def on_device(tokens, cotangent, path, coarse_weights, middle_weights, fine_weights):
    member_count = lax.axis_size("mem")
    group_count = lax.axis_size("grp")
    group = lax.axis_index("grp")
    row_count = coarse_weights.shape[1]
    fine_owned = fine_weights.shape[0]
    route = path[0]
    all_paths = lax.all_gather(path, ("grp", "mem"), axis=0, tiled=True)
    group_paths = lax.dynamic_slice_in_dim(all_paths, group * member_count, member_count, 0)
    coarse_pick = one_hot_rows(group_paths[:, 0], coarse_weights.shape[0])
    middle_pick = one_hot_rows(group_paths[:, 1], middle_weights.shape[0])
    middle_send = select_blocks(middle_pick, middle_weights)
    every_block = lax.all_gather(coarse_weights, "mem", axis=1, tiled=True)
    coarse_block = lax.dynamic_index_in_dim(every_block, route[0], 0, keepdims=False)
    middle_block = lax.all_to_all(middle_send, "mem", split_axis=0, concat_axis=1, tiled=True)[0]
    offsets = all_paths[:, 2] - group * fine_owned
    fine_pick = one_hot_rows(offsets, fine_owned)
    fine_send = select_blocks(fine_pick, fine_weights).reshape(
        group_count, member_count, row_count, fine_weights.shape[2]
    )
    arrived = lax.all_to_all(fine_send, "grp", split_axis=0, concat_axis=0, tiled=True)
    merged = jnp.sum(arrived, axis=0, dtype=jnp.float32).astype(jnp.bfloat16)
    fine_block = lax.all_to_all(merged, "mem", split_axis=0, concat_axis=1, tiled=True)[0]
    coarse_term, coarse_back = level_terms(tokens, cotangent, coarse_block)
    middle_term, middle_back = level_terms(tokens, cotangent, middle_block)
    fine_term, fine_back = level_terms(tokens, cotangent, fine_block)
    tokens_grad = (coarse_back + middle_back + fine_back).astype(jnp.bfloat16)
    coarse_parts, middle_parts = (
        lax.all_to_all(
            coarse_term.reshape(member_count, row_count, -1),
            "mem",
            split_axis=0,
            concat_axis=0,
            tiled=True,
        ),
        lax.all_to_all(
            middle_term.reshape(member_count, row_count, -1),
            "mem",
            split_axis=0,
            concat_axis=0,
            tiled=True,
        ),
    )
    coarse_local = collect_blocks(coarse_pick, coarse_parts)
    middle_local = collect_blocks(middle_pick, middle_parts)
    coarse_total, middle_total = lax.psum((coarse_local, middle_local), "grp")
    fine_parts = lax.all_to_all(
        fine_term.reshape(member_count, row_count, -1),
        "mem",
        split_axis=0,
        concat_axis=0,
        tiled=True,
    )
    owner_group = group_paths[:, 2] // fine_owned
    destined = (jnp.arange(group_count, dtype=jnp.int32)[:, None] == owner_group[None, :]).astype(
        jnp.float32
    )
    outgoing = destined[:, :, None, None] * fine_parts[None]
    returned = lax.all_to_all(outgoing, "grp", split_axis=0, concat_axis=0, tiled=True)
    fine_local = collect_blocks(
        fine_pick, returned.reshape(group_count * member_count, row_count, -1)
    )
    return (
        tokens_grad,
        coarse_total.astype(jnp.bfloat16),
        middle_total.astype(jnp.bfloat16),
        fine_local.astype(jnp.bfloat16),
    )


def solution(mesh):
    return jax.shard_map(
        on_device,
        mesh=mesh,
        in_specs=(
            P(("grp", "mem"), None),
            P(("grp", "mem"), None),
            P(("grp", "mem"), None),
            P(None, "mem", None),
            P(None, "mem", None),
            P("grp", "mem", None),
        ),
        out_specs=(
            P(("grp", "mem"), None),
            P(None, "mem", None),
            P(None, "mem", None),
            P("grp", "mem", None),
        ),
        check_vma=False,
    )
```

profile of v0, /device:TPU:1, one launch (start us, length us, event | category | flops | bytes accessed | tf_op | source)
XLA Modules:
  0.0 553.8 jit_solution(7141725121758117286)
XLA Ops:
  7.2 108.2 %all-gather = s32[512,1,3]{2,1,0:T(1,128)S(1)} all-gather(s32[1,1,3]{2,1,0:T(1,128)} %bitcast.100), channel_id=1, replica_groups=mesh['grp'=8,'mem'=64] {'grp','mem'}, dimensions={0}, use_global_device_ids=true | all-gather | bytes 6156 | tf_op jit(solution)/shard_map/all_gather | solution.py:55
  116.7 34.8 %all_to_all.43 = bf16[8,64,16,128]{3,1,2,0:T(8,128)(2,1)S(1)} all-to-all(bf16[8,64,16,128]{3,1,2,0:T(8,128)(2,1)S(1)} %copy.78), channel_id=1, replica_groups=mesh['grp'=8,'mem'=64] {'grp'}, dimensions={0} | all-to-all | bytes 4194304 | tf_op jit(solution)/shard_map/all_to_all | solution.py:68
  152.7 10.4 %all-to-all-start.2 = ((bf16[64,16,128]{2,1,0:T(8,128)(2,1)}), bf16[64,16,128]{2,1,0:T(8,128)(2,1)S(1)}, u32[]{:S(2)}, u32[]{:S(2)}) async-start(bf16[64,16,128]{2,1,0:T(8,128)(2,1)} %copy.80), calls=%async_computation.2 | async-start | bytes 524288 | tf_op jit(solution)/shard_map/all_to_all | solution.py:70
  163.2 1.4 convolution_convert_fusion.1
  165.6 16.0 %all-to-all-done.2 = bf16[64,16,128]{2,1,0:T(8,128)(2,1)S(1)} async-done(((bf16[64,16,128]{2,1,0:T(8,128)(2,1)}), bf16[64,16,128]{2,1,0:T(8,128)(2,1)S(1)}, u32[]{:S(2)}, u32[]{:S(2)}) %all-to-all-start.2) | async-done | bytes 262176 | tf_op jit(solution)/shard_map/all_to_all | solution.py:70
  181.7 8.1 %all-to-all-start = ((bf16[64,16,256]{2,1,0:T(8,128)(2,1)}), bf16[64,16,256]{2,1,0:T(8,128)(2,1)S(1)}, u32[]{:S(2)}, u32[]{:S(2)}) async-start(bf16[64,16,256]{2,1,0:T(8,128)(2,1)} %copy.75), calls=%async_computation | async-start | bytes 1048576 | tf_op jit(solution)/shard_map/all_to_all | solution.py:62
  191.8 26.9 %all-to-all-done = bf16[64,16,256]{2,1,0:T(8,128)(2,1)S(1)} async-done(((bf16[64,16,256]{2,1,0:T(8,128)(2,1)}), bf16[64,16,256]{2,1,0:T(8,128)(2,1)S(1)}, u32[]{:S(2)}, u32[]{:S(2)}) %all-to-all-start) | async-done | bytes 524320 | tf_op jit(solution)/shard_map/all_to_all | solution.py:62
  218.7 9.3 %all-to-all-start.5 = ((f32[64,16,128]{2,1,0:T(8,128)}), f32[64,16,128]{2,1,0:T(8,128)}, u32[]{:S(2)}, u32[]{:S(2)}) async-start(f32[64,16,128]{2,1,0:T(8,128)} %bitcast.30), calls=%async_computation.5 | async-start | bytes 1048576 | tf_op jit(solution)/shard_map/all_to_all | solution.py:94
  229.9 1.3 copy.83
  231.2 25.7 %all-to-all-done.5 = f32[64,16,128]{2,1,0:T(8,128)} async-done(((f32[64,16,128]{2,1,0:T(8,128)}), f32[64,16,128]{2,1,0:T(8,128)}, u32[]{:S(2)}, u32[]{:S(2)}) %all-to-all-start.5) | async-done | bytes 524320 | tf_op jit(solution)/shard_map/all_to_all | solution.py:94
  256.9 9.2 %all-to-all-start.4 = ((f32[64,16,256]{2,1,0:T(8,128)}), f32[64,16,256]{2,1,0:T(8,128)S(1)}, u32[]{:S(2)}, u32[]{:S(2)}) async-start(f32[64,16,256]{2,1,0:T(8,128)} %bitcast.25), calls=%async_computation.4 | async-start | bytes 2097152 | tf_op jit(solution)/shard_map/all_to_all | solution.py:83
  267.4 2.6 broadcast_multiply_fusion
  270.0 48.8 %all-to-all-done.4 = f32[64,16,256]{2,1,0:T(8,128)S(1)} async-done(((f32[64,16,256]{2,1,0:T(8,128)}), f32[64,16,256]{2,1,0:T(8,128)S(1)}, u32[]{:S(2)}, u32[]{:S(2)}) %all-to-all-start.4) | async-done | bytes 1048608 | tf_op jit(solution)/shard_map/all_to_all | solution.py:83
  319.8 9.6 %all-to-all-start.6 = ((f32[8,64,16,128]{3,1,2,0:T(8,128)}), f32[8,64,16,128]{3,1,2,0:T(8,128)}, u32[]{:S(2)}, u32[]{:S(2)}) async-start(f32[8,64,16,128]{3,1,2,0:T(8,128)} %broadcast_multiply_fusion), calls=%async_computation.6 | async-start | bytes 8388608 | tf_op jit(solution)/shard_map/all_to_all | solution.py:106
  329.6 53.5 %all-gather.3.cloned.1.call-done = bf16[4,1024,512]{2,1,0:T(8,128)(2,1)} async-done(((bf16[4,16,512]{2,1,0:T(8,128)(2,1)}), bf16[4,1024,512]{2,1,0:T(8,128)(2,1)}) %all-gather.3.cloned.1.call-update) | async-done | bytes 4194320 | tf_op jit(solution)/shard_map/all_gather | solution.py:60
  383.1 1.3 dynamic-slice_bitcast_fusion
  385.8 1.9 copy.81
  387.7 8.4 %all-to-all-start.3 = ((f32[64,16,512]{2,1,0:T(8,128)}), f32[64,16,512]{2,1,0:T(8,128)S(1)}, u32[]{:S(2)}, u32[]{:S(2)}) async-start(f32[64,16,512]{2,1,0:T(8,128)} %bitcast.89), calls=%async_computation.3 | async-start | bytes 4194304 | tf_op jit(solution)/shard_map/all_to_all | solution.py:76
  396.2 3.6 fusion.3
  401.3 2.5 copy.87
  403.8 1.7 convolution_convert_fusion.2
  406.6 75.5 %all-to-all-done.3 = f32[64,16,512]{2,1,0:T(8,128)S(1)} async-done(((f32[64,16,512]{2,1,0:T(8,128)}), f32[64,16,512]{2,1,0:T(8,128)S(1)}, u32[]{:S(2)}, u32[]{:S(2)}) %all-to-all-start.3) | async-done | bytes 2097184 | tf_op jit(solution)/shard_map/all_to_all | solution.py:76
  482.1 2.0 fusion
  484.1 61.1 %all-reduce.2 = (bf16[4,16,512]{2,0,1:T(4,128)(2,1)S(1)}, bf16[64,16,256]{2,0,1:T(8,128)(2,1)S(1)}) all-reduce(f32[4,16,512]{2,0,1:T(4,128)S(1)} %fusion, f32[64,16,256]{2,0,1:T(8,128)} %fusion.3), channel_id=1, replica_groups=mesh['grp'=8,'mem'=64] {'grp'}, use_global_device_ids=true, to_apply=%region_1.2 | all-reduce | flops 294912 | bytes 1769472 | tf_op jit(solution)/shard_map/psum | solution.py:93
  (55 shorter events, 15.5 us)
Async XLA Ops:
  7.2 108.5 %copy-start = (bf16[128,16,128]{2,1,0:T(8,128)(2,1)S(1)}, bf16[128,16,128]{2,1,0:T(8,128)(2,1)}, u32[]{:S(2)}) copy-start(bf16[128,16,128]{2,1,0:T(8,128)(2,1)} %param.11) | copy-start | bytes 1572868
  151.8 38.0 %copy-start.1 = (bf16[128,1024]{1,0:T(8,128)(2,1)S(1)}, bf16[128,1024]{1,0:T(8,128)(2,1)}, u32[]{:S(2)}) copy-start(bf16[128,1024]{1,0:T(8,128)(2,1)} %param.6) | copy-start | bytes 786436
  152.7 37.4 %copy-start.5 = (bf16[128,1024]{1,0:T(8,128)(2,1)S(1)}, bf16[128,1024]{1,0:T(8,128)(2,1)}, u32[]{:S(2)}) copy-start(bf16[128,1024]{1,0:T(8,128)(2,1)} %param.7) | copy-start | bytes 786436
  152.7 29.0 %all-to-all-start.2 = ((bf16[64,16,128]{2,1,0:T(8,128)(2,1)}), bf16[64,16,128]{2,1,0:T(8,128)(2,1)S(1)}, u32[]{:S(2)}, u32[]{:S(2)}) async-start(bf16[64,16,128]{2,1,0:T(8,128)(2,1)} %copy.80), calls=%async_computation.2 | async-start | bytes 524288 | tf_op jit(solution)/shard_map/all_to_all | solution.py:70
  181.7 37.1 %all-to-all-start = ((bf16[64,16,256]{2,1,0:T(8,128)(2,1)}), bf16[64,16,256]{2,1,0:T(8,128)(2,1)S(1)}, u32[]{:S(2)}, u32[]{:S(2)}) async-start(bf16[64,16,256]{2,1,0:T(8,128)(2,1)} %copy.75), calls=%async_computation | async-start | bytes 1048576 | tf_op jit(solution)/shard_map/all_to_all | solution.py:62
  218.7 11.1 %copy-start.6 = (bf16[64,16,256]{2,1,0:T(8,128)(2,1)}, bf16[64,16,256]{2,1,0:T(8,128)(2,1)S(1)}, u32[]{:S(2)}) copy-start(bf16[64,16,256]{2,1,0:T(8,128)(2,1)S(1)} %all-to-all-done) | copy-start | bytes 1572868
  218.7 38.2 %all-to-all-start.5 = ((f32[64,16,128]{2,1,0:T(8,128)}), f32[64,16,128]{2,1,0:T(8,128)}, u32[]{:S(2)}, u32[]{:S(2)}) async-start(f32[64,16,128]{2,1,0:T(8,128)} %bitcast.30), calls=%async_computation.5 | async-start | bytes 1048576 | tf_op jit(solution)/shard_map/all_to_all | solution.py:94
  228.1 155.0 %all-gather.3.cloned.1.call-start = ((), (), s32[]{:S(2)}) async-start(), calls=%async_computation.7 | async-start | bytes 4259840 | tf_op jit(solution)/shard_map/all_gather | solution.py:60
  256.9 61.9 %all-to-all-start.4 = ((f32[64,16,256]{2,1,0:T(8,128)}), f32[64,16,256]{2,1,0:T(8,128)S(1)}, u32[]{:S(2)}, u32[]{:S(2)}) async-start(f32[64,16,256]{2,1,0:T(8,128)} %bitcast.25), calls=%async_computation.4 | async-start | bytes 2097152 | tf_op jit(solution)/shard_map/all_to_all | solution.py:83
  270.0 59.5 %copy-start.8 = (s32[1,3]{1,0:T(1,128)S(1)}, s32[1,3]{1,0:T(1,128)}, u32[]{:S(2)}) copy-start(s32[1,3]{1,0:T(1,128)} %param.8) | copy-start | bytes 40
  318.8 1.0 copy-start.2
  319.8 67.9 %all-to-all-start.6 = ((f32[8,64,16,128]{3,1,2,0:T(8,128)}), f32[8,64,16,128]{3,1,2,0:T(8,128)}, u32[]{:S(2)}, u32[]{:S(2)}) async-start(f32[8,64,16,128]{3,1,2,0:T(8,128)} %broadcast_multiply_fusion), calls=%async_computation.6 | async-start | bytes 8388608 | tf_op jit(solution)/shard_map/all_to_all | solution.py:106
  384.4 1.0 copy-start.3
  387.7 94.4 %all-to-all-start.3 = ((f32[64,16,512]{2,1,0:T(8,128)}), f32[64,16,512]{2,1,0:T(8,128)S(1)}, u32[]{:S(2)}, u32[]{:S(2)}) async-start(f32[64,16,512]{2,1,0:T(8,128)} %bitcast.89), calls=%async_computation.3 | async-start | bytes 4194304 | tf_op jit(solution)/shard_map/all_to_all | solution.py:76
  396.1 3.6 copy-start.4
  396.1 3.9 copy-start.7
Sparse Core Ops, SparseCore 0:
  231.9 151.1 all-gather.2
where the time goes:
time: 556 us; the launch traced here: 554 us
  waiting for transfers between devices  247 us (44%)
  blocking collectives  204 us (37%)
  starting transfers between devices  55.2 us (10%)
  local copies, waits for them, and re-layouts  15.4 us (3%)
  between operations  14.5 us (3%)
  matrix products  14.1 us (3%)
    all_gather x1, blocking collectives, on_device(): all_paths = lax.all_gather(path, ('grp', 'mem'), axis=0, tiled=True)  108 us
    all_to_all x1, waiting for transfers between devices, on_device(): lax.all_to_all(coarse_term.reshape(member_count, row_count, -1), 'mem', s...  75.5 us
    psum x1, blocking collectives, on_device(): coarse_total, middle_total = lax.psum((coarse_local, middle_local), 'grp')  61.1 us
    all_gather x1, waiting for transfers between devices, on_device(): every_block = lax.all_gather(coarse_weights, 'mem', axis=1, tiled=True)  53.5 us
    all_to_all x1, waiting for transfers between devices, on_device(): lax.all_to_all(middle_term.reshape(member_count, row_count, -1), 'mem', s...  48.8 us
    all_to_all x1, blocking collectives, on_device(): lax.all_to_all(fine_send, 'grp', split_axis=0, concat_axis=0, tiled=True)  34.8 us
    all_to_all x1, waiting for transfers between devices, on_device(): lax.all_to_all(middle_send, 'mem', split_axis=0, concat_axis=1, tiled=True)  26.9 us
    all_to_all x1, waiting for transfers between devices, on_device(): lax.all_to_all(fine_term.reshape(member_count, row_count, -1), 'mem', spl...  25.7 us
  transfers between devices with their start and end apart: 7, of which 6 were waited for; matrix products, arithmetic and copies ran while one was open for 5% of the time, Pallas kernels for 0%

commit v1 on v0

v1 whole, which is shorter than its diff:
```python
from functools import partial

import jax
import jax.numpy as jnp
from jax import lax
from jax.sharding import Mesh, PartitionSpec as P

F32 = jnp.float32
BF16 = jnp.bfloat16


def contract_rows(left, right):
    return lax.dot_general(
        left, right, (((0,), (0,)), ((), ())), preferred_element_type=F32
    )


def level_terms(inputs, upstream, weights):
    hidden_width = weights.shape[1] // 2
    up_half = weights[:, :hidden_width]
    down_half = weights[:, hidden_width:]
    before = jnp.dot(inputs, up_half, preferred_element_type=F32)
    hidden, pullback = jax.vjp(partial(jax.nn.gelu, approximate=True), before)
    hidden_low = hidden.astype(BF16)
    hidden_grad = jnp.dot(upstream, down_half, preferred_element_type=F32)
    before_grad = pullback(hidden_grad)[0].astype(BF16)
    up_grad = contract_rows(inputs, before_grad).astype(BF16)
    down_grad = contract_rows(upstream, hidden_low).astype(BF16)
    input_part = lax.dot_general(
        before_grad, up_half, (((1,), (1,)), ((), ())), preferred_element_type=F32
    )
    return (up_grad, down_grad, input_part)


def one_hot_rows(identity, count):
    return (identity[:, None] == jnp.arange(count, dtype=jnp.int32)[None, :]).astype(BF16)


def select_blocks(picker, blocks):
    return jnp.einsum("mk,krh->mrh", picker, blocks, preferred_element_type=F32).astype(BF16)


def collect_blocks(picker, pieces):
    return jnp.einsum("mk,mrh->krh", picker, pieces, preferred_element_type=F32)


def exchange(array, axes):
    return lax.all_to_all(array, axes, split_axis=0, concat_axis=0, tiled=True)


def gather(array, axes):
    count = lax.axis_size(axes)
    return exchange(jnp.broadcast_to(array[None], (count,) + array.shape), axes)


def on_device(tokens, cotangent, path, coarse_weights, middle_weights, fine_weights):
    y_count, c_count = lax.axis_size("y"), lax.axis_size("c")
    group_count = y_count * c_count
    member_count = lax.axis_size(("x", "z"))
    y_index, c_index = lax.axis_index("y"), lax.axis_index("c")
    group = y_index * c_count + c_index
    row_count = coarse_weights.shape[1]
    fine_owned, _, fine_width = fine_weights.shape
    coarse_count, _, coarse_width = coarse_weights.shape
    middle_count, _, middle_width = middle_weights.shape

    ids = gather(path[0], ("y", "c", "x", "z"))
    ids = ids.reshape(group_count, member_count, 3)
    own = lax.dynamic_index_in_dim(ids, group, 0, keepdims=False)
    coarse_pick = one_hot_rows(own[:, 0], coarse_count)
    middle_pick = one_hot_rows(own[:, 1], middle_count)
    fine_all = ids[:, :, 2].reshape(y_count, c_count, member_count)

    offsets = jnp.swapaxes(fine_all, 0, 1).reshape(-1) - group * fine_owned
    fine_send = select_blocks(one_hot_rows(offsets, fine_owned), fine_weights)
    fine_send = fine_send.reshape(c_count, y_count * member_count, row_count, fine_width)
    arrived = exchange(fine_send, "c")
    arrived = (arrived[0] + arrived[1]).reshape(y_count, member_count, row_count, fine_width)
    arrived = exchange(arrived, "y")
    fine_rows = (arrived[0] + arrived[1]) + (arrived[2] + arrived[3])

    blocks = jnp.concatenate(
        [
            select_blocks(coarse_pick, coarse_weights),
            select_blocks(middle_pick, middle_weights),
            fine_rows,
        ],
        axis=2,
    )
    mine = exchange(blocks, ("x", "z")).reshape(member_count * row_count, -1)

    low, high = coarse_width, coarse_width + middle_width
    c_up, c_down, c_back = level_terms(tokens, cotangent, mine[:, :low])
    m_up, m_down, m_back = level_terms(tokens, cotangent, mine[:, low:high])
    f_up, f_down, f_back = level_terms(tokens, cotangent, mine[:, high:])
    tokens_grad = (c_back + m_back + f_back).astype(BF16)
    terms = jnp.concatenate([c_up, c_down, m_up, m_down, f_up, f_down], axis=1)
    parts = exchange(terms.reshape(member_count, row_count, -1), ("x", "z"))

    coarse_local = collect_blocks(coarse_pick, parts[:, :, :low])
    middle_local = collect_blocks(middle_pick, parts[:, :, low:high])
    fine_parts = parts[:, :, high:]
    def cut(array):
        return jnp.concatenate(jnp.split(array, array.shape[2] // fine_width, axis=2), axis=0)

    def join(array, width):
        return jnp.concatenate(jnp.split(array, width // fine_width, axis=0), axis=2)

    local = jnp.concatenate([cut(middle_local), cut(coarse_local)], axis=0).astype(BF16)
    unit = local.shape[1:]

    def with_fine(shares, fine):
        copies = jnp.broadcast_to(fine[None], shares.shape[:1] + fine.shape)
        return jnp.concatenate([shares, copies], axis=1)

    shares = local.reshape((c_count, -1) + unit)
    count = shares.shape[1]
    two = exchange(with_fine(shares, fine_parts), "c")
    half = (two[0, :count].astype(F32) + two[1, :count].astype(F32)).astype(BF16)
    fine_both = two[:, count:].reshape((-1,) + unit)
    shares = half.reshape((y_count, -1) + unit)
    count = shares.shape[1]
    four = exchange(with_fine(shares, fine_both), "y")
    done = jnp.sum(four[:, :count], axis=0, dtype=F32).astype(BF16)
    fine_four = four[:, count:].reshape((-1,) + unit)
    total = gather(gather(done, "y"), "c").reshape(local.shape)
    fine_offsets = fine_all.reshape(-1) - group * fine_owned
    fine_total = collect_blocks(one_hot_rows(fine_offsets, fine_owned), fine_four)
    units = middle_count * (middle_width // fine_width)
    middle_total = join(total[:units], middle_width)
    coarse_total = join(total[units:], coarse_width)
    return (tokens_grad, coarse_total, middle_total, fine_total.astype(BF16))


def solution(mesh):
    fine_mesh = Mesh(mesh.devices.reshape(4, 2, 4, 16), ("y", "c", "x", "z"))
    everyone = ("y", "c", "x", "z")
    members = ("x", "z")
    return jax.shard_map(
        on_device,
        mesh=fine_mesh,
        in_specs=(
            P(everyone, None),
            P(everyone, None),
            P(everyone, None),
            P(None, members, None),
            P(None, members, None),
            P(("y", "c"), members, None),
        ),
        out_specs=(
            P(everyone, None),
            P(None, members, None),
            P(None, members, None),
            P(("y", "c"), members, None),
        ),
        check_vma=False,
    )
```

time: 556 us -> 337 us (0.61)
  waiting for transfers between devices: 247 us -> 65.3 us
  starting transfers between devices: 55.2 us -> 35.2 us
  between operations: 14.5 us -> 1.04 us
    all_to_all x1 -> x5, blocking collectives: 34.8 us -> 203 us  [exchange(): return lax.all_to_all(array, axes, split_axis=0, concat_axis=0, tiled=True)]
    all_to_all x6 -> x4, waiting for transfers between devices: 193 us -> 65.3 us  [exchange(): return lax.all_to_all(array, axes, split_axis=0, concat_axis=0, tiled=True)]
    all_gather x1 -> x0, blocking collectives: 108 us -> none  [on_device(): all_paths = lax.all_gather(path, ('grp', 'mem'), axis=0, tiled=True)]
    psum x1 -> x0, blocking collectives: 61.1 us -> none  [on_device(): coarse_total, middle_total = lax.psum((coarse_local, middle_local), 'grp')]
    all_gather x1 -> x0, waiting for transfers between devices: 53.5 us -> none  [on_device(): every_block = lax.all_gather(coarse_weights, 'mem', axis=1, tiled=True)]
    all_to_all x6 -> x4, starting transfers between devices: 55.1 us -> 35.2 us  [exchange(): return lax.all_to_all(array, axes, split_axis=0, concat_axis=0, tiled=True)]
    dot_general x11 -> x12, matrix products: 11.2 us -> 5.35 us  [the longest x3 1.96 us: collect_blocks(): return jnp.einsum('mk,mrh->krh', picker, pieces, preferred_element_type=F32)]
  transfers between devices with their start and end apart: 7 -> 4, of which waited for: 6 -> 4; matrix products, arithmetic and copies ran while one was open for 5% -> 2% of each run, Pallas kernels for 0% -> 0%
where the time goes in v1:
time: 337 us; the launch traced here: 336 us
  blocking collectives  203 us (60%)
  waiting for transfers between devices  65.3 us (19%)
  starting transfers between devices  35.2 us (10%)
  local copies, waits for them, and re-layouts  15.8 us (5%)
  matrix products  11.2 us (3%)
  other arithmetic  3.77 us (1%)
    all_to_all x5, blocking collectives, exchange(): return lax.all_to_all(array, axes, split_axis=0, concat_axis=0, tiled=True)  203 us
    all_to_all x4, waiting for transfers between devices, exchange(): return lax.all_to_all(array, axes, split_axis=0, concat_axis=0, tiled=True)  65.3 us
    all_to_all x4, starting transfers between devices, exchange(): return lax.all_to_all(array, axes, split_axis=0, concat_axis=0, tiled=True)  35.2 us
  transfers between devices with their start and end apart: 4, of which 4 were waited for; matrix products, arithmetic and copies ran while one was open for 2% of the time, Pallas kernels for 0%

profile of v1, /device:TPU:1, one launch (start us, length us, event | category | flops | bytes accessed | tf_op | source)
XLA Modules:
  0.0 335.6 jit_solution(2650940320134652886)
XLA Ops:
  0.6 1.6 broadcast_in_dim.12
  2.2 24.3 %all-to-all-start = ((s32[512,1,3]{2,1,0:T(1,128)}), s32[512,1,3]{2,1,0:T(1,128)S(1)}, u32[]{:S(2)}, u32[]{:S(2)}) async-start(s32[512,1,3]{2,1,0:T(1,128)} %broadcast_in_dim.12), calls=%async_computation | async-start | bytes 524288 | tf_op jit(solution)/shard_map/all_to_all | solution.py:48
  26.5 23.7 %all-to-all-done = s32[512,1,3]{2,1,0:T(1,128)S(1)} async-done(((s32[512,1,3]{2,1,0:T(1,128)}), s32[512,1,3]{2,1,0:T(1,128)S(1)}, u32[]{:S(2)}, u32[]{:S(2)}) %all-to-all-start) | async-done | bytes 6176 | tf_op jit(solution)/shard_map/all_to_all | solution.py:48
  52.0 1.4 copy.37
  53.3 6.5 %all_to_all.46 = bf16[2,256,16,128]{3,2,1,0:T(8,128)(2,1)S(1)} all-to-all(bf16[2,256,16,128]{3,2,1,0:T(8,128)(2,1)S(1)} %copy.37), channel_id=1, replica_groups=mesh['y'=4,'c'=2,'x'=4,'z'=16] {'c'}, dimensions={0} | all-to-all | bytes 4194304 | tf_op jit(solution)/shard_map/all_to_all | solution.py:48
  60.0 1.3 copy.38
  61.3 3.6 %all-to-all-start.2 = ((bf16[4,64,16,128]{3,1,2,0:T(8,128)(2,1)}), bf16[4,64,16,128]{3,1,2,0:T(8,128)(2,1)S(1)}, u32[]{:S(2)}, u32[]{:S(2)}) async-start(bf16[4,64,16,128]{3,1,2,0:T(8,128)(2,1)} %copy.38), calls=%async_computation.2 | async-start | bytes 2097152 | tf_op jit(solution)/shard_map/all_to_all | solution.py:48
  66.0 13.7 %all-to-all-done.2 = bf16[4,64,16,128]{3,1,2,0:T(8,128)(2,1)S(1)} async-done(((bf16[4,64,16,128]{3,1,2,0:T(8,128)(2,1)}), bf16[4,64,16,128]{3,1,2,0:T(8,128)(2,1)S(1)}, u32[]{:S(2)}, u32[]{:S(2)}) %all-to-all-start.2) | async-done | bytes 1048608 | tf_op jit(solution)/shard_map/all_to_all | solution.py:48
  81.1 84.9 %all_to_all.47 = bf16[64,16,896]{2,1,0:T(8,128)(2,1)S(1)} all-to-all(bf16[64,16,896]{2,1,0:T(8,128)(2,1)S(1)} %copy.39), channel_id=1, replica_groups=mesh['y'=4,'c'=2,'x'=4,'z'=16] {'x','z'}, dimensions={0} | all-to-all | bytes 3670016 | tf_op jit(solution)/shard_map/all_to_all | solution.py:48
  169.5 2.5 copy.40
  172.0 95.2 %all_to_all.48 = bf16[64,16,896]{2,1,0:T(8,128)(2,1)S(1)} all-to-all(bf16[64,16,896]{2,1,0:T(8,128)(2,1)} %bitcast.103), channel_id=1, replica_groups=mesh['y'=4,'c'=2,'x'=4,'z'=16] {'x','z'}, dimensions={0} | all-to-all | bytes 3670016 | tf_op jit(solution)/shard_map/all_to_all | solution.py:48
  268.2 1.2 convolution_convert_fusion.11
  270.0 1.7 concatenate.24
  272.2 10.7 %all_to_all.49 = bf16[2,136,16,128]{3,2,1,0:T(8,128)(2,1)S(1)} all-to-all(bf16[2,136,16,128]{3,2,1,0:T(8,128)(2,1)S(1)} %pad_maximum_fusion.2), channel_id=1, replica_groups=mesh['y'=4,'c'=2,'x'=4,'z'=16] {'c'}, dimensions={0} | all-to-all | bytes 2228224 | tf_op jit(solution)/shard_map/all_to_all | solution.py:48
  283.2 1.7 pad_maximum_fusion
  284.9 3.8 %all-to-all-start.6 = ((bf16[4,146,16,128]{3,2,1,0:T(8,128)(2,1)}), bf16[4,146,16,128]{3,2,1,0:T(8,128)(2,1)S(1)}, u32[]{:S(2)}, u32[]{:S(2)}) async-start(bf16[4,146,16,128]{3,2,1,0:T(8,128)(2,1)} %pad_maximum_fusion), calls=%async_computation.6 | async-start | bytes 4784128 | tf_op jit(solution)/shard_map/all_to_all | solution.py:48
  288.7 1.3 fusion.18
  290.1 1.2 convolution_add_fusion.1
  291.3 1.9 fusion.4
  293.2 24.7 %all-to-all-done.6 = bf16[4,146,16,128]{3,2,1,0:T(8,128)(2,1)S(1)} async-done(((bf16[4,146,16,128]{3,2,1,0:T(8,128)(2,1)}), bf16[4,146,16,128]{3,2,1,0:T(8,128)(2,1)S(1)}, u32[]{:S(2)}, u32[]{:S(2)}) %all-to-all-start.6) | async-done | bytes 2392096 | tf_op jit(solution)/shard_map/all_to_all | solution.py:48
  318.7 3.5 %all-to-all-start.7 = ((bf16[4,18,16,128]{3,2,1,0:T(8,128)(2,1)}), bf16[4,18,16,128]{3,2,1,0:T(8,128)(2,1)S(1)}, u32[]{:S(2)}, u32[]{:S(2)}) async-start(bf16[4,18,16,128]{3,2,1,0:T(8,128)(2,1)} %broadcast_in_dim.16), calls=%async_computation.7 | async-start | bytes 589824 | tf_op jit(solution)/shard_map/all_to_all | solution.py:48
  323.5 1.1 copy.47
  324.6 3.2 all-to-all-done.7
  327.9 6.2 %all_to_all.50 = bf16[2,4,18,16,128]{4,3,2,1,0:T(8,128)(2,1)S(1)} all-to-all(bf16[2,4,18,16,128]{4,3,2,1,0:T(8,128)(2,1)S(1)} %broadcast_in_dim.17), channel_id=1, replica_groups=mesh['y'=4,'c'=2,'x'=4,'z'=16] {'c'}, dimensions={0} | all-to-all | bytes 1179648 | tf_op jit(solution)/shard_map/all_to_all | solution.py:48
  (74 shorter events, 13.9 us)
Async XLA Ops:
  0.6 50.6 %copy-start = (bf16[128,16,128]{2,1,0:T(8,128)(2,1)S(1)}, bf16[128,16,128]{2,1,0:T(8,128)(2,1)}, u32[]{:S(2)}) copy-start(bf16[128,16,128]{2,1,0:T(8,128)(2,1)} %param.11) | copy-start | bytes 1572868
  2.2 48.0 %all-to-all-start = ((s32[512,1,3]{2,1,0:T(1,128)}), s32[512,1,3]{2,1,0:T(1,128)S(1)}, u32[]{:S(2)}, u32[]{:S(2)}) async-start(s32[512,1,3]{2,1,0:T(1,128)} %broadcast_in_dim.12), calls=%async_computation | async-start | bytes 524288 | tf_op jit(solution)/shard_map/all_to_all | solution.py:48
  50.5 0.6 copy-start.8
  60.0 5.0 %copy-start.4 = (bf16[64,16,256]{2,1,0:T(8,128)(2,1)S(1)}, bf16[64,16,256]{2,1,0:T(8,128)(2,1)}, u32[]{:S(2)}) copy-start(bf16[64,16,256]{2,1,0:T(8,128)(2,1)} %param.10) | copy-start | bytes 1572868
  61.3 4.3 %copy-start.7 = (bf16[4,16,512]{2,1,0:T(8,128)(2,1)S(1)}, bf16[4,16,512]{2,1,0:T(8,128)(2,1)}, u32[]{:S(2)}) copy-start(bf16[4,16,512]{2,1,0:T(8,128)(2,1)} %param.9) | copy-start | bytes 196612
  61.3 18.5 %all-to-all-start.2 = ((bf16[4,64,16,128]{3,1,2,0:T(8,128)(2,1)}), bf16[4,64,16,128]{3,1,2,0:T(8,128)(2,1)S(1)}, u32[]{:S(2)}, u32[]{:S(2)}) async-start(bf16[4,64,16,128]{3,1,2,0:T(8,128)(2,1)} %copy.38), calls=%async_computation.2 | async-start | bytes 2097152 | tf_op jit(solution)/shard_map/all_to_all | solution.py:48
  65.0 0.5 copy-start.10
  81.1 84.9 %copy-start.1 = (bf16[128,1024]{1,0:T(8,128)(2,1)S(1)}, bf16[128,1024]{1,0:T(8,128)(2,1)}, u32[]{:S(2)}) copy-start(bf16[128,1024]{1,0:T(8,128)(2,1)} %param.6) | copy-start | bytes 786436
  165.9 1.8 copy-start.2
  166.0 1.1 copy-start.3
  167.7 1.6 copy-start.5
  267.5 0.7 copy-start.11
  284.9 3.8 %copy-start.9 = (s32[8,64,1]{1,0,2:T(8,128)S(1)}, s32[8,64,1]{1,0,2:T(8,128)}, u32[]{:S(2)}) copy-start(s32[8,64,1]{1,0,2:T(8,128)} %copy-done.8) | copy-start | bytes 6148
  284.9 5.2 %copy-start.6 = (bf16[128,128]{0,1:T(8,128)(2,1)S(1)}, bf16[128,128]{0,1:T(8,128)(2,1)}, u32[]{:S(2)}) copy-start(bf16[128,128]{0,1:T(8,128)(2,1)} %copy-done.5) | copy-start | bytes 98308
  284.9 33.0 %all-to-all-start.6 = ((bf16[4,146,16,128]{3,2,1,0:T(8,128)(2,1)}), bf16[4,146,16,128]{3,2,1,0:T(8,128)(2,1)S(1)}, u32[]{:S(2)}, u32[]{:S(2)}) async-start(bf16[4,146,16,128]{3,2,1,0:T(8,128)(2,1)} %pad_maximum_fusion), calls=%async_computation.6 | async-start | bytes 4784128 | tf_op jit(solution)/shard_map/all_to_all | solution.py:48
  318.7 9.2 %all-to-all-start.7 = ((bf16[4,18,16,128]{3,2,1,0:T(8,128)(2,1)}), bf16[4,18,16,128]{3,2,1,0:T(8,128)(2,1)S(1)}, u32[]{:S(2)}, u32[]{:S(2)}) async-start(bf16[4,18,16,128]{3,2,1,0:T(8,128)(2,1)} %broadcast_in_dim.16), calls=%async_computation.7 | async-start | bytes 589824 | tf_op jit(solution)/shard_map/all_to_all | solution.py:48

commit v2 on v1

v2 whole, which is shorter than its diff:
```python
from functools import partial

import jax
import jax.numpy as jnp
from jax import lax
from jax.experimental import pallas as pl
from jax.experimental.pallas import tpu as pltpu
from jax.sharding import Mesh, PartitionSpec as P

F32 = jnp.float32
BF16 = jnp.bfloat16
I32 = jnp.int32
Y, C, X, Z = 4, 2, 4, 16
MEMBERS = X * Z
ROWS = 16
EVERYONE = ("y", "c", "x", "z")


def contract_rows(left, right):
    return lax.dot_general(
        left, right, (((0,), (0,)), ((), ())), preferred_element_type=F32
    )


def level_terms(inputs, upstream, weights):
    hidden_width = weights.shape[1] // 2
    up_half = weights[:, :hidden_width]
    down_half = weights[:, hidden_width:]
    before = jnp.dot(inputs, up_half, preferred_element_type=F32)
    hidden, pullback = jax.vjp(partial(jax.nn.gelu, approximate=True), before)
    hidden_low = hidden.astype(BF16)
    hidden_grad = jnp.dot(upstream, down_half, preferred_element_type=F32)
    before_grad = pullback(hidden_grad)[0].astype(BF16)
    up_grad = contract_rows(inputs, before_grad)
    down_grad = contract_rows(upstream, hidden_low)
    input_part = lax.dot_general(
        before_grad, up_half, (((1,), (1,)), ((), ())), preferred_element_type=F32
    )
    return (up_grad, down_grad, input_part)


def one_hot_rows(identity, count):
    return (identity[:, None] == jnp.arange(count, dtype=I32)[None, :]).astype(BF16)


def collect_blocks(picker, pieces):
    return jnp.einsum("mk,mrh->krh", picker, pieces, preferred_element_type=F32)


def exchange(array, axes):
    return lax.all_to_all(array, axes, split_axis=0, concat_axis=0, tiled=True)


def gather(array, axes):
    count = lax.axis_size(axes)
    return exchange(jnp.broadcast_to(array[None], (count,) + array.shape), axes)


def shift(array, axis, step):
    count = lax.axis_size(axis)
    return lax.ppermute(array, axis, [(i, (i + step) % count) for i in range(count)])


def pick_kernel(ids_ref, middle_ref, own_ref, other_ref, out_ref):
    def step(m, carry):
        middle_id, slot, same = ids_ref[0, m], ids_ref[1, m], ids_ref[2, m]
        out_ref[m, :, : middle_ref.shape[2]] = middle_ref[middle_id]
        out_ref[m, :, middle_ref.shape[2] :] = jnp.where(
            same == 1, own_ref[slot], other_ref[slot]
        )
        return carry

    lax.fori_loop(0, MEMBERS, step, 0, unroll=8)


def pick(ids, middle, own, other):
    vmem = pl.BlockSpec(memory_space=pltpu.VMEM)
    return pl.pallas_call(
        pick_kernel,
        out_shape=jax.ShapeDtypeStruct(
            (MEMBERS, ROWS, middle.shape[2] + own.shape[2]), BF16
        ),
        in_specs=[pl.BlockSpec(memory_space=pltpu.SMEM), vmem, vmem, vmem],
        out_specs=vmem,
        compiler_params=pltpu.CompilerParams(vmem_limit_bytes=24 * 1024 * 1024),
    )(ids, middle, own, other)


def on_device(tokens, cotangent, path, coarse_weights, middle_weights, fine_weights):
    y_index, c_index = lax.axis_index("y"), lax.axis_index("c")
    x_index = lax.axis_index("x")
    group = y_index * C + c_index
    fine_owned, _, fine_width = fine_weights.shape
    coarse_count, _, coarse_width = coarse_weights.shape
    middle_count, _, middle_width = middle_weights.shape
    quarter = coarse_width // 4

    fine_own = jnp.concatenate(
        [fine_weights] + [shift(fine_weights, "y", s) for s in range(1, Y)], axis=0
    )
    fine_other = shift(fine_own, "c", 1)
    other_tokens = shift(tokens, "c", 1)
    other_cotangent = shift(cotangent, "c", 1)
    other_path = shift(path, "c", 1)

    mine_coarse = lax.dynamic_index_in_dim(coarse_weights, y_index, 0, keepdims=False)
    mine_coarse = jnp.concatenate(
        [
            lax.dynamic_slice_in_dim(mine_coarse, c_index * quarter, quarter, 1),
            lax.dynamic_slice_in_dim(mine_coarse, (c_index + 2) * quarter, quarter, 1),
        ],
        axis=1,
    )
    digits = jnp.stack([path[0, 1], path[0, 2] // 32, path[0, 2] % 32, path[0, 0]])
    line = gather(digits, "x").reshape(-1)
    line = jnp.zeros((8, 2 * quarter), I32).at[0, : line.shape[0]].set(line)
    packet = jnp.concatenate([mine_coarse, line.astype(BF16)], axis=0)
    packets = gather(packet, "z").reshape(Z, ROWS + 8, 2 * quarter)
    coarse_column = packets[:, :ROWS].reshape(Z * ROWS, 2 * quarter)
    numbers = packets[:, ROWS, : 4 * X].astype(I32).reshape(Z, X, 4)
    numbers = jnp.transpose(numbers, (2, 1, 0)).reshape(4, MEMBERS)
    middle_ids = numbers[0]
    fine_ids = numbers[1] * 32 + numbers[2]
    owner = fine_ids // fine_owned
    slots = ((y_index - owner // C) % Y) * fine_owned + fine_ids % fine_owned
    same = (owner % C == c_index).astype(I32)
    send = pick(jnp.stack([middle_ids, slots, same]), middle_weights, fine_own, fine_other)
    mine = exchange(send, ("x", "z")).reshape(MEMBERS * ROWS, -1)

    columns = jnp.stack([coarse_column] + [shift(coarse_column, "x", s) for s in range(1, X)])
    columns = jnp.stack([columns[(x_index - i) % X] for i in range(X)])
    half_block = columns.reshape(MEMBERS * ROWS, 2 * quarter)
    halves = jnp.stack([half_block] + [shift(half_block, "y", s) for s in range(1, Y)])
    own_id, other_id = path[0, 0], other_path[0, 0]
    own_half = halves[(y_index - own_id) % Y]
    other_half = halves[(y_index - other_id) % Y]
    a_up, a_down, a_back = level_terms(tokens, cotangent, own_half)
    b_up, b_down, b_back = level_terms(other_tokens, other_cotangent, other_half)
    own_term = jnp.concatenate([a_up, a_down], axis=1)
    other_term = jnp.concatenate([b_up, b_down], axis=1)

    def slot_of(block):
        both = jnp.where(own_id == block, own_term, 0.0) + jnp.where(
            other_id == block, other_term, 0.0
        )
        return both.astype(BF16)

    coarse_sum = slot_of(y_index).astype(F32)
    for s in range(1, Y):
        coarse_sum = coarse_sum + shift(slot_of((y_index + s) % Y), "y", s).astype(F32)
    coarse_sum = coarse_sum.astype(BF16)
    coarse_back = a_back + shift(b_back, "c", 1)

    m_up, m_down, m_back = level_terms(tokens, cotangent, mine[:, :middle_width])
    f_up, f_down, f_back = level_terms(tokens, cotangent, mine[:, middle_width:])
    tokens_grad = (coarse_back + m_back + f_back).astype(BF16)
    terms = [t.astype(BF16) for t in (m_up, m_down, f_up, f_down)]
    terms = jnp.concatenate(terms + [coarse_sum], axis=1)
    parts = exchange(terms.reshape(MEMBERS, ROWS, -1), ("x", "z"))

    def cut(array):
        return jnp.concatenate(jnp.split(array, array.shape[-1] // fine_width, axis=-1), axis=0)

    def join(array, width):
        return jnp.concatenate(jnp.split(array, width // fine_width, axis=0), axis=-1)

    coarse_done = jnp.sum(parts[:, :, middle_width + fine_width :], axis=0, dtype=F32)
    coarse_done = cut(coarse_done.astype(BF16)[None])
    middle_local = collect_blocks(
        one_hot_rows(middle_ids, middle_count), parts[:, :, :middle_width]
    )
    fine_parts = parts[:, :, middle_width : middle_width + fine_width]

    local = cut(middle_local).astype(BF16)
    unit = local.shape[1:]
    shares = local.reshape((C, -1) + unit)
    count = shares.shape[1]
    copies = jnp.broadcast_to(fine_parts[None], (C,) + fine_parts.shape)
    two = exchange(jnp.concatenate([shares, copies], axis=1), "c")
    half = (two[0, :count].astype(F32) + two[1, :count].astype(F32)).astype(BF16)
    fine_both = two[:, count:].reshape((-1,) + unit)
    all_ids = gather(fine_ids, "c").reshape(-1)
    fine_four = jnp.concatenate([fine_both] + [shift(fine_both, "y", s) for s in range(1, Y)])
    id_four = jnp.concatenate([all_ids] + [shift(all_ids, "y", s) for s in range(1, Y)])
    four = exchange(half.reshape((Y, -1) + unit), "y")
    done = jnp.sum(four, axis=0, dtype=F32).astype(BF16)
    done = jnp.concatenate([done, coarse_done], axis=0)
    total = gather(gather(done, "y"), "c").reshape((C, Y, done.shape[0]) + unit)
    fine_offsets = id_four - group * fine_owned
    fine_total = collect_blocks(one_hot_rows(fine_offsets, fine_owned), fine_four)
    middle_total = total[:, :, :-2].reshape(local.shape)
    middle_total = join(middle_total, middle_width)
    coarse_total = jnp.transpose(total[:, :, -2:], (1, 3, 2, 0, 4)).reshape(coarse_weights.shape)
    return (tokens_grad, coarse_total, middle_total, fine_total.astype(BF16))


def solution(mesh):
    fine_mesh = Mesh(mesh.devices.reshape(Y, C, X, Z), EVERYONE)
    members = ("x", "z")
    return jax.shard_map(
        on_device,
        mesh=fine_mesh,
        in_specs=(
            P(EVERYONE, None),
            P(EVERYONE, None),
            P(EVERYONE, None),
            P(None, members, None),
            P(None, members, None),
            P(("y", "c"), members, None),
        ),
        out_specs=(
            P(EVERYONE, None),
            P(None, members, None),
            P(None, members, None),
            P(("y", "c"), members, None),
        ),
        check_vma=False,
    )
```

time: 337 us -> 308 us (0.914)
  blocking collectives: 203 us -> 16.4 us
  starting transfers between devices: 35.2 us -> 129 us
  waiting for transfers between devices: 65.3 us -> 113 us
  other arithmetic: 3.77 us -> 10.4 us
  between operations: 1.04 us -> 7.53 us
    all_to_all x5 -> x2, blocking collectives: 203 us -> 16.4 us  [exchange(): return lax.all_to_all(array, axes, split_axis=0, concat_axis=0, tiled=True)]
    ppermute x0 -> x23, starting transfers between devices: none -> 73.2 us  [shift(): lax.ppermute(array, axis, [(i, (i + step) % count) for i in range(count)])]
    ppermute x0 -> x23, waiting for transfers between devices: none -> 51 us  [shift(): lax.ppermute(array, axis, [(i, (i + step) % count) for i in range(count)])]
    all_to_all x4 -> x7, starting transfers between devices: 35.2 us -> 55.8 us  [exchange(): return lax.all_to_all(array, axes, split_axis=0, concat_axis=0, tiled=True)]
    dot_general x6 -> x8, matrix products: 1.37 us -> 5.34 us  [contract_rows(): lax.dot_general(left, right, (((0,), (0,)), ((), ())), preferred_element_...]
    another operation x0 -> x6, other arithmetic: none -> 3.75 us  [the longest x1 1.37 us: on_device(): jnp.stack([path[0, 1], path[0, 2] // 32, path[0, 2] % 32, path[0, 0]])]
    all_to_all x4 -> x7, waiting for transfers between devices: 65.3 us -> 61.8 us  [exchange(): return lax.all_to_all(array, axes, split_axis=0, concat_axis=0, tiled=True)]
  transfers between devices with their start and end apart: 4 -> 30, of which waited for: 4 -> 11; matrix products, arithmetic and copies ran while one was open for 2% -> 11% of each run, Pallas kernels for 0% -> 0%
where the time goes in v2:
time: 308 us; the launch traced here: 306 us
  starting transfers between devices  129 us (42%)
  waiting for transfers between devices  113 us (37%)
  blocking collectives  16.4 us (5%)
  local copies, waits for them, and re-layouts  14 us (5%)
  matrix products  12.8 us (4%)
  other arithmetic  10.4 us (3%)
  between operations  7.53 us (2%)
    ppermute x23, starting transfers between devices, shift(): lax.ppermute(array, axis, [(i, (i + step) % count) for i in range(count)])  73.2 us
    all_to_all x7, waiting for transfers between devices, exchange(): return lax.all_to_all(array, axes, split_axis=0, concat_axis=0, tiled=True)  61.8 us
    all_to_all x7, starting transfers between devices, exchange(): return lax.all_to_all(array, axes, split_axis=0, concat_axis=0, tiled=True)  55.8 us
    ppermute x23, waiting for transfers between devices, shift(): lax.ppermute(array, axis, [(i, (i + step) % count) for i in range(count)])  51 us
    all_to_all x2, blocking collectives, exchange(): return lax.all_to_all(array, axes, split_axis=0, concat_axis=0, tiled=True)  16.4 us
  transfers between devices with their start and end apart: 30, of which 11 were waited for; matrix products, arithmetic and copies ran while one was open for 11% of the time, Pallas kernels for 0%

profile of v2, /device:TPU:1, one launch (start us, length us, event | category | flops | bytes accessed | tf_op | source)
XLA Modules:
  0.0 305.7 jit_solution(14117200559081445655)
XLA Ops:
  0.6 4.0 %collective-permute-start.10 = (bf16[128,16,128]{2,1,0:T(8,128)(2,1)}, bf16[128,16,128]{2,1,0:T(8,128)(2,1)S(1)}, u32[]{:S(2)}, u32[]{:S(2)}) collective-permute-start(bf16[128,16,128]{2,1,0:T(8,128)(2,1)} %param.13), channel_id=1, source_target_pairs={{0,128},{128,256},{256,384},{384,0},{1,129},{129,257},{257,385},{3... | collective-permute-start | bytes 1572872 | tf_op jit(solution)/shard_map/ppermute | solution.py:61
  4.7 4.5 %collective-permute-start.11 = (bf16[128,16,128]{2,1,0:T(8,128)(2,1)}, bf16[128,16,128]{2,1,0:T(8,128)(2,1)}, u32[]{:S(2)}, u32[]{:S(2)}) collective-permute-start(bf16[128,16,128]{2,1,0:T(8,128)(2,1)} %param.13), channel_id=1, source_target_pairs={{0,256},{128,384},{256,0},{384,128},{1,257},{129,385},{257,1},{385... | collective-permute-start | bytes 1572872 | tf_op jit(solution)/shard_map/ppermute | solution.py:61
  18.1 4.0 %all-to-all-start = ((s32[4,1,4]{2,1,0:T(1,128)}), s32[4,1,4]{2,1,0:T(1,128)S(1)}, u32[]{:S(2)}, u32[]{:S(2)}) async-start(s32[4,1,4]{2,1,0:T(1,128)} %broadcast_in_dim.25), calls=%async_computation | async-start | bytes 4096 | tf_op jit(solution)/shard_map/all_to_all | solution.py:51
  24.1 6.1 %collective-permute-done.11 = bf16[128,16,128]{2,1,0:T(8,128)(2,1)} collective-permute-done((bf16[128,16,128]{2,1,0:T(8,128)(2,1)}, bf16[128,16,128]{2,1,0:T(8,128)(2,1)}, u32[]{:S(2)}, u32[]{:S(2)}) %collective-permute-start.11) | collective-permute-done | bytes 524320 | tf_op jit(solution)/shard_map/ppermute | solution.py:61
  31.4 3.6 %collective-permute-start.13 = (bf16[512,16,128]{2,1,0:T(8,128)(2,1)S(1)}, bf16[512,16,128]{2,1,0:T(8,128)(2,1)}, u32[]{:S(2)}, u32[]{:S(2)}) collective-permute-start(bf16[512,16,128]{2,1,0:T(8,128)(2,1)S(1)} %constant_dynamic-update-slice_fusion.own_ref), channel_id=1, source_target_pairs={{0,64},{64,0},{1,65},{65,1},{2,66},{66,2},{3,67},{67,3},{4,68},{68... | collective-permute-start | bytes 6291464 | tf_op jit(solution)/shard_map/ppermute | solution.py:61
  35.8 14.9 %all-to-all-start.1 = ((bf16[16,24,256]{2,1,0:T(8,128)(2,1)}), bf16[16,24,256]{2,1,0:T(8,128)(2,1)S(1)}, u32[]{:S(2)}, u32[]{:S(2)}) async-start(bf16[16,24,256]{2,1,0:T(8,128)(2,1)} %broadcast_in_dim.26), calls=%async_computation.1 | async-start | bytes 393216 | tf_op jit(solution)/shard_map/all_to_all | solution.py:51
  50.8 13.2 %all-to-all-done.1 = bf16[16,24,256]{2,1,0:T(8,128)(2,1)S(1)} async-done(((bf16[16,24,256]{2,1,0:T(8,128)(2,1)}), bf16[16,24,256]{2,1,0:T(8,128)(2,1)S(1)}, u32[]{:S(2)}, u32[]{:S(2)}) %all-to-all-start.1) | async-done | bytes 196640 | tf_op jit(solution)/shard_map/all_to_all | solution.py:51
  64.0 4.4 %collective-permute-start.2 = (bf16[256,256]{1,0:T(8,128)(2,1)S(1)}, bf16[256,256]{1,0:T(8,128)(2,1)S(1)}, u32[]{:S(2)}, u32[]{:S(2)}) collective-permute-start(bf16[256,256]{1,0:T(8,128)(2,1)S(1)} %bitcast.138), channel_id=1, source_target_pairs={{0,48},{16,0},{32,16},{48,32},{1,49},{17,1},{33,17},{49,33},{2,50}... | collective-permute-start | bytes 393224 | tf_op jit(solution)/shard_map/ppermute | solution.py:61
  81.7 10.9 %all-to-all-start.2 = ((bf16[64,16,384]{2,1,0:T(8,128)(2,1)}), bf16[64,16,384]{2,1,0:T(8,128)(2,1)S(1)}, u32[]{:S(2)}, u32[]{:S(2)}) async-start(bf16[64,16,384]{2,1,0:T(8,128)(2,1)} %shard_map.93), calls=%async_computation.2 | async-start | bytes 1572864 | tf_op jit(solution)/shard_map/all_to_all | solution.py:51
  92.7 4.3 %collective-permute-start.5 = (bf16[1024,256]{1,0:T(8,128)(2,1)S(1)}, bf16[1024,256]{1,0:T(8,128)(2,1)S(1)}, u32[]{:S(2)}, u32[]{:S(2)}) collective-permute-start(bf16[1024,256]{1,0:T(8,128)(2,1)S(1)} %bitcast.127), channel_id=1, source_target_pairs={{0,384},{128,0},{256,128},{384,256},{1,385},{129,1},{257,129},{385... | collective-permute-start | bytes 1572872 | tf_op jit(solution)/shard_map/ppermute | solution.py:61
  102.5 4.3 %collective-permute-start.6 = (s32[1,3]{1,0:T(1,128)S(1)}, s32[1,3]{1,0:T(1,128)S(1)}, u32[]{:S(2)}, u32[]{:S(2)}) collective-permute-start(s32[1,3]{1,0:T(1,128)S(1)} %copy-done.8), channel_id=1, source_target_pairs={{0,64},{64,0},{1,65},{65,1},{2,66},{66,2},{3,67},{67,3},{4,68},{68... | collective-permute-start | bytes 44 | tf_op jit(solution)/shard_map/ppermute | solution.py:61
  114.8 10.8 %collective-permute-done.3 = bf16[1024,256]{1,0:T(8,128)(2,1)} collective-permute-done((bf16[1024,256]{1,0:T(8,128)(2,1)S(1)}, bf16[1024,256]{1,0:T(8,128)(2,1)}, u32[]{:S(2)}, u32[]{:S(2)}) %collective-permute-start.3) | collective-permute-done | bytes 524320 | tf_op jit(solution)/shard_map/ppermute | solution.py:61
  133.4 3.5 %collective-permute-start.15 = (bf16[1024,256]{0,1:T(8,128)(2,1)}, bf16[1024,256]{0,1:T(8,128)(2,1)}, u32[]{:S(2)}, u32[]{:S(2)}) collective-permute-start(bf16[1024,256]{0,1:T(8,128)(2,1)} %get-tuple-element.49), channel_id=1, source_target_pairs={{0,256},{128,384},{256,0},{384,128},{1,257},{129,385},{257,1},{385... | collective-permute-start | bytes 1572872 | tf_op jit(solution)/shard_map/ppermute | solution.py:61
  140.3 4.5 %all-to-all-start.8 = ((s32[2,1,64]{2,1,0:T(1,128)}), s32[2,1,64]{2,1,0:T(1,128)S(1)}, u32[]{:S(2)}, u32[]{:S(2)}) async-start(s32[2,1,64]{2,1,0:T(1,128)} %broadcast_in_dim.61), calls=%async_computation.8 | async-start | bytes 2048 | tf_op jit(solution)/shard_map/all_to_all | solution.py:51
  149.5 12.7 %collective-permute-done.14 = bf16[1024,256]{0,1:T(8,128)(2,1)} collective-permute-done((bf16[1024,256]{0,1:T(8,128)(2,1)}, bf16[1024,256]{0,1:T(8,128)(2,1)}, u32[]{:S(2)}, u32[]{:S(2)}) %collective-permute-start.14) | collective-permute-done | bytes 524320 | tf_op jit(solution)/shard_map/ppermute | solution.py:61
  167.3 14.6 %all-to-all-start.3 = ((bf16[64,16,640]{2,1,0:T(8,128)(2,1)}), bf16[64,16,640]{2,1,0:T(8,128)(2,1)S(1)}, u32[]{:S(2)}, u32[]{:S(2)}) async-start(bf16[64,16,640]{2,1,0:T(8,128)(2,1)} %bitcast.42), calls=%async_computation.3 | async-start | bytes 2621440 | tf_op jit(solution)/shard_map/all_to_all | solution.py:51
  184.5 3.5 %collective-permute-start.18 = (s32[128]{0:T(128)S(1)}, s32[128]{0:T(128)S(1)}, u32[]{:S(2)}, u32[]{:S(2)}) collective-permute-start(s32[128]{0:T(128)S(1)} %concatenate.55), channel_id=1, source_target_pairs={{0,256},{128,384},{256,0},{384,128},{1,257},{129,385},{257,1},{385... | collective-permute-start | bytes 1544 | tf_op jit(solution)/shard_map/ppermute | solution.py:61
  194.9 4.4 %collective-permute-start.9 = (f32[128,1024]{1,0:T(8,128)}, f32[128,1024]{1,0:T(8,128)}, u32[]{:S(2)}, u32[]{:S(2)}) collective-permute-start(f32[128,1024]{1,0:T(8,128)} %fusion.36), channel_id=1, source_target_pairs={{0,64},{64,0},{1,65},{65,1},{2,66},{66,2},{3,67},{67,3},{4,68},{68... | collective-permute-start | bytes 1572872 | tf_op jit(solution)/shard_map/ppermute | solution.py:61
  199.8 42.5 %all-to-all-done.3 = bf16[64,16,640]{2,1,0:T(8,128)(2,1)S(1)} async-done(((bf16[64,16,640]{2,1,0:T(8,128)(2,1)}), bf16[64,16,640]{2,1,0:T(8,128)(2,1)S(1)}, u32[]{:S(2)}, u32[]{:S(2)}) %all-to-all-start.3) | async-done | bytes 1310752 | tf_op jit(solution)/shard_map/all_to_all | solution.py:51
  243.3 10.0 %all_to_all.47 = bf16[2,128,16,128]{3,1,2,0:T(8,128)(2,1)S(1)} all-to-all(bf16[2,128,16,128]{3,1,2,0:T(8,128)(2,1)S(1)} %pad_maximum_fusion.3), channel_id=1, replica_groups=mesh['y'=4,'c'=2,'x'=4,'z'=16] {'c'}, dimensions={0} | all-to-all | bytes 2097152 | tf_op jit(solution)/shard_map/all_to_all | solution.py:51
  257.5 6.0 %all-to-all-done.5 = bf16[4,16,16,128]{3,1,2,0:T(8,128)(2,1)S(1)} async-done(((bf16[4,16,16,128]{3,1,2,0:T(8,128)(2,1)}), bf16[4,16,16,128]{3,1,2,0:T(8,128)(2,1)S(1)}, u32[]{:S(2)}, u32[]{:S(2)}) %all-to-all-start.5) | async-done | bytes 262176 | tf_op jit(solution)/shard_map/all_to_all | solution.py:51
  270.0 4.5 %collective-permute-start.22 = (bf16[128,16,128]{2,0,1:T(8,128)(2,1)S(1)}, bf16[128,16,128]{2,0,1:T(8,128)(2,1)S(1)}, u32[]{:S(2)}, u32[]{:S(2)}) collective-permute-start(bf16[128,16,128]{2,0,1:T(8,128)(2,1)S(1)} %bitcast.134), channel_id=1, source_target_pairs={{0,384},{128,0},{256,128},{384,256},{1,385},{129,1},{257,129},{385... | collective-permute-start | bytes 1572872 | tf_op jit(solution)/shard_map/ppermute | solution.py:61
  279.6 6.5 %all_to_all.48 = bf16[2,4,18,16,128]{4,3,2,1,0:T(8,128)(2,1)S(1)} all-to-all(bf16[2,4,18,16,128]{4,3,2,1,0:T(8,128)(2,1)S(1)} %broadcast_in_dim.60), channel_id=1, replica_groups=mesh['y'=4,'c'=2,'x'=4,'z'=16] {'c'}, dimensions={0} | all-to-all | bytes 1179648 | tf_op jit(solution)/shard_map/all_to_all | solution.py:51
  289.3 13.8 %collective-permute-done.20 = bf16[128,16,128]{2,0,1:T(8,128)(2,1)} collective-permute-done((bf16[128,16,128]{2,0,1:T(8,128)(2,1)S(1)}, bf16[128,16,128]{2,0,1:T(8,128)(2,1)}, u32[]{:S(2)}, u32[]{:S(2)}) %collective-permute-start.20) | collective-permute-done | bytes 524320 | tf_op jit(solution)/shard_map/ppermute | solution.py:61
  (141 shorter events, 86.6 us)
Async XLA Ops:
  0.6 23.4 %collective-permute-start.10 = (bf16[128,16,128]{2,1,0:T(8,128)(2,1)}, bf16[128,16,128]{2,1,0:T(8,128)(2,1)S(1)}, u32[]{:S(2)}, u32[]{:S(2)}) collective-permute-start(bf16[128,16,128]{2,1,0:T(8,128)(2,1)} %param.13), channel_id=1, source_target_pairs={{0,128},{128,256},{256,384},{384,0},{1,129},{129,257},{257,385},{3... | collective-permute-start | bytes 1572872 | tf_op jit(solution)/shard_map/ppermute | solution.py:61
  4.7 25.5 %collective-permute-start.11 = (bf16[128,16,128]{2,1,0:T(8,128)(2,1)}, bf16[128,16,128]{2,1,0:T(8,128)(2,1)}, u32[]{:S(2)}, u32[]{:S(2)}) collective-permute-start(bf16[128,16,128]{2,1,0:T(8,128)(2,1)} %param.13), channel_id=1, source_target_pairs={{0,256},{128,384},{256,0},{384,128},{1,257},{129,385},{257,1},{385... | collective-permute-start | bytes 1572872 | tf_op jit(solution)/shard_map/ppermute | solution.py:61
  9.2 22.1 %collective-permute-start.12 = (bf16[128,16,128]{2,1,0:T(8,128)(2,1)}, bf16[128,16,128]{2,1,0:T(8,128)(2,1)S(1)}, u32[]{:S(2)}, u32[]{:S(2)}) collective-permute-start(bf16[128,16,128]{2,1,0:T(8,128)(2,1)} %param.13), channel_id=1, source_target_pairs={{0,384},{128,0},{256,128},{384,256},{1,385},{129,1},{257,129},{385... | collective-permute-start | bytes 1572872 | tf_op jit(solution)/shard_map/ppermute | solution.py:61
  18.1 16.9 %all-to-all-start = ((s32[4,1,4]{2,1,0:T(1,128)}), s32[4,1,4]{2,1,0:T(1,128)S(1)}, u32[]{:S(2)}, u32[]{:S(2)}) async-start(s32[4,1,4]{2,1,0:T(1,128)} %broadcast_in_dim.25), calls=%async_computation | async-start | bytes 4096 | tf_op jit(solution)/shard_map/all_to_all | solution.py:51
  31.4 47.5 %collective-permute-start.13 = (bf16[512,16,128]{2,1,0:T(8,128)(2,1)S(1)}, bf16[512,16,128]{2,1,0:T(8,128)(2,1)}, u32[]{:S(2)}, u32[]{:S(2)}) collective-permute-start(bf16[512,16,128]{2,1,0:T(8,128)(2,1)S(1)} %constant_dynamic-update-slice_fusion.own_ref), channel_id=1, source_target_pairs={{0,64},{64,0},{1,65},{65,1},{2,66},{66,2},{3,67},{67,3},{4,68},{68... | collective-permute-start | bytes 6291464 | tf_op jit(solution)/shard_map/ppermute | solution.py:61
  35.8 28.2 %all-to-all-start.1 = ((bf16[16,24,256]{2,1,0:T(8,128)(2,1)}), bf16[16,24,256]{2,1,0:T(8,128)(2,1)S(1)}, u32[]{:S(2)}, u32[]{:S(2)}) async-start(bf16[16,24,256]{2,1,0:T(8,128)(2,1)} %broadcast_in_dim.26), calls=%async_computation.1 | async-start | bytes 393216 | tf_op jit(solution)/shard_map/all_to_all | solution.py:51
  64.0 10.9 %collective-permute-start.2 = (bf16[256,256]{1,0:T(8,128)(2,1)S(1)}, bf16[256,256]{1,0:T(8,128)(2,1)S(1)}, u32[]{:S(2)}, u32[]{:S(2)}) collective-permute-start(bf16[256,256]{1,0:T(8,128)(2,1)S(1)} %bitcast.138), channel_id=1, source_target_pairs={{0,48},{16,0},{32,16},{48,32},{1,49},{17,1},{33,17},{49,33},{2,50}... | collective-permute-start | bytes 393224 | tf_op jit(solution)/shard_map/ppermute | solution.py:61
  81.7 58.1 %all-to-all-start.2 = ((bf16[64,16,384]{2,1,0:T(8,128)(2,1)}), bf16[64,16,384]{2,1,0:T(8,128)(2,1)S(1)}, u32[]{:S(2)}, u32[]{:S(2)}) async-start(bf16[64,16,384]{2,1,0:T(8,128)(2,1)} %shard_map.93), calls=%async_computation.2 | async-start | bytes 1572864 | tf_op jit(solution)/shard_map/all_to_all | solution.py:51
  92.7 22.0 %collective-permute-start.5 = (bf16[1024,256]{1,0:T(8,128)(2,1)S(1)}, bf16[1024,256]{1,0:T(8,128)(2,1)S(1)}, u32[]{:S(2)}, u32[]{:S(2)}) collective-permute-start(bf16[1024,256]{1,0:T(8,128)(2,1)S(1)} %bitcast.127), channel_id=1, source_target_pairs={{0,384},{128,0},{256,128},{384,256},{1,385},{129,1},{257,129},{385... | collective-permute-start | bytes 1572872 | tf_op jit(solution)/shard_map/ppermute | solution.py:61
  97.0 17.7 %collective-permute-start.4 = (bf16[1024,256]{1,0:T(8,128)(2,1)S(1)}, bf16[1024,256]{1,0:T(8,128)(2,1)S(1)}, u32[]{:S(2)}, u32[]{:S(2)}) collective-permute-start(bf16[1024,256]{1,0:T(8,128)(2,1)S(1)} %bitcast.128), channel_id=1, source_target_pairs={{0,256},{128,384},{256,0},{384,128},{1,257},{129,385},{257,1},{385... | collective-permute-start | bytes 1572872 | tf_op jit(solution)/shard_map/ppermute | solution.py:61
  100.6 25.0 %collective-permute-start.3 = (bf16[1024,256]{1,0:T(8,128)(2,1)S(1)}, bf16[1024,256]{1,0:T(8,128)(2,1)}, u32[]{:S(2)}, u32[]{:S(2)}) collective-permute-start(bf16[1024,256]{1,0:T(8,128)(2,1)S(1)} %bitcast.129), channel_id=1, source_target_pairs={{0,128},{128,256},{256,384},{384,0},{1,129},{129,257},{257,385},{3... | collective-permute-start | bytes 1572872 | tf_op jit(solution)/shard_map/ppermute | solution.py:61
  102.5 9.5 %collective-permute-start.6 = (s32[1,3]{1,0:T(1,128)S(1)}, s32[1,3]{1,0:T(1,128)S(1)}, u32[]{:S(2)}, u32[]{:S(2)}) collective-permute-start(s32[1,3]{1,0:T(1,128)S(1)} %copy-done.8), channel_id=1, source_target_pairs={{0,64},{64,0},{1,65},{65,1},{2,66},{66,2},{3,67},{67,3},{4,68},{68... | collective-permute-start | bytes 44 | tf_op jit(solution)/shard_map/ppermute | solution.py:61
  106.8 20.5 %collective-permute-start.8 = (bf16[128,1024]{1,0:T(8,128)(2,1)S(1)}, bf16[128,1024]{1,0:T(8,128)(2,1)S(1)}, u32[]{:S(2)}, u32[]{:S(2)}) collective-permute-start(bf16[128,1024]{1,0:T(8,128)(2,1)S(1)} %copy-done.1), channel_id=1, source_target_pairs={{0,64},{64,0},{1,65},{65,1},{2,66},{66,2},{3,67},{67,3},{4,68},{68... | collective-permute-start | bytes 786440 | tf_op jit(solution)/shard_map/ppermute | solution.py:61
  112.0 15.8 %collective-permute-start.7 = (bf16[128,1024]{1,0:T(8,128)(2,1)S(1)}, bf16[128,1024]{1,0:T(8,128)(2,1)S(1)}, u32[]{:S(2)}, u32[]{:S(2)}) collective-permute-start(bf16[128,1024]{1,0:T(8,128)(2,1)S(1)} %copy-done.2), channel_id=1, source_target_pairs={{0,64},{64,0},{1,65},{65,1},{2,66},{66,2},{3,67},{67,3},{4,68},{68... | collective-permute-start | bytes 786440 | tf_op jit(solution)/shard_map/ppermute | solution.py:61
  131.5 18.0 %collective-permute-start.16 = (bf16[1024,256]{0,1:T(8,128)(2,1)}, bf16[1024,256]{0,1:T(8,128)(2,1)}, u32[]{:S(2)}, u32[]{:S(2)}) collective-permute-start(bf16[1024,256]{0,1:T(8,128)(2,1)} %get-tuple-element.50), channel_id=1, source_target_pairs={{0,384},{128,0},{256,128},{384,256},{1,385},{129,1},{257,129},{385... | collective-permute-start | bytes 1572872 | tf_op jit(solution)/shard_map/ppermute | solution.py:61
  133.4 16.1 %collective-permute-start.15 = (bf16[1024,256]{0,1:T(8,128)(2,1)}, bf16[1024,256]{0,1:T(8,128)(2,1)}, u32[]{:S(2)}, u32[]{:S(2)}) collective-permute-start(bf16[1024,256]{0,1:T(8,128)(2,1)} %get-tuple-element.49), channel_id=1, source_target_pairs={{0,256},{128,384},{256,0},{384,128},{1,257},{129,385},{257,1},{385... | collective-permute-start | bytes 1572872 | tf_op jit(solution)/shard_map/ppermute | solution.py:61
  137.0 25.2 %collective-permute-start.14 = (bf16[1024,256]{0,1:T(8,128)(2,1)}, bf16[1024,256]{0,1:T(8,128)(2,1)}, u32[]{:S(2)}, u32[]{:S(2)}) collective-permute-start(bf16[1024,256]{0,1:T(8,128)(2,1)} %get-tuple-element.48), channel_id=1, source_target_pairs={{0,128},{128,256},{256,384},{384,0},{1,129},{129,257},{257,385},{3... | collective-permute-start | bytes 1572872 | tf_op jit(solution)/shard_map/ppermute | solution.py:61
  140.3 26.9 %all-to-all-start.8 = ((s32[2,1,64]{2,1,0:T(1,128)}), s32[2,1,64]{2,1,0:T(1,128)S(1)}, u32[]{:S(2)}, u32[]{:S(2)}) async-start(s32[2,1,64]{2,1,0:T(1,128)} %broadcast_in_dim.61), calls=%async_computation.8 | async-start | bytes 2048 | tf_op jit(solution)/shard_map/all_to_all | solution.py:51
  167.3 75.0 %all-to-all-start.3 = ((bf16[64,16,640]{2,1,0:T(8,128)(2,1)}), bf16[64,16,640]{2,1,0:T(8,128)(2,1)S(1)}, u32[]{:S(2)}, u32[]{:S(2)}) async-start(bf16[64,16,640]{2,1,0:T(8,128)(2,1)} %bitcast.42), calls=%async_computation.3 | async-start | bytes 2621440 | tf_op jit(solution)/shard_map/all_to_all | solution.py:51
  194.9 73.0 %collective-permute-start.9 = (f32[128,1024]{1,0:T(8,128)}, f32[128,1024]{1,0:T(8,128)}, u32[]{:S(2)}, u32[]{:S(2)}) collective-permute-start(f32[128,1024]{1,0:T(8,128)} %fusion.36), channel_id=1, source_target_pairs={{0,64},{64,0},{1,65},{65,1},{2,66},{66,2},{3,67},{67,3},{4,68},{68... | collective-permute-start | bytes 1572872 | tf_op jit(solution)/shard_map/ppermute | solution.py:61
  264.4 15.1 %all-to-all-start.6 = ((bf16[4,18,16,128]{3,2,1,0:T(8,128)(2,1)}), bf16[4,18,16,128]{3,2,1,0:T(8,128)(2,1)S(1)}, u32[]{:S(2)}, u32[]{:S(2)}) async-start(bf16[4,18,16,128]{3,2,1,0:T(8,128)(2,1)} %broadcast_in_dim.30), calls=%async_computation.6 | async-start | bytes 589824 | tf_op jit(solution)/shard_map/all_to_all | solution.py:51
  270.0 17.7 %collective-permute-start.22 = (bf16[128,16,128]{2,0,1:T(8,128)(2,1)S(1)}, bf16[128,16,128]{2,0,1:T(8,128)(2,1)S(1)}, u32[]{:S(2)}, u32[]{:S(2)}) collective-permute-start(bf16[128,16,128]{2,0,1:T(8,128)(2,1)S(1)} %bitcast.134), channel_id=1, source_target_pairs={{0,384},{128,0},{256,128},{384,256},{1,385},{129,1},{257,129},{385... | collective-permute-start | bytes 1572872 | tf_op jit(solution)/shard_map/ppermute | solution.py:61
  274.5 14.8 %collective-permute-start.21 = (bf16[128,16,128]{2,0,1:T(8,128)(2,1)S(1)}, bf16[128,16,128]{2,0,1:T(8,128)(2,1)S(1)}, u32[]{:S(2)}, u32[]{:S(2)}) collective-permute-start(bf16[128,16,128]{2,0,1:T(8,128)(2,1)S(1)} %bitcast.135), channel_id=1, source_target_pairs={{0,256},{128,384},{256,0},{384,128},{1,257},{129,385},{257,1},{385... | collective-permute-start | bytes 1572872 | tf_op jit(solution)/shard_map/ppermute | solution.py:61
  277.0 26.1 %collective-permute-start.20 = (bf16[128,16,128]{2,0,1:T(8,128)(2,1)S(1)}, bf16[128,16,128]{2,0,1:T(8,128)(2,1)}, u32[]{:S(2)}, u32[]{:S(2)}) collective-permute-start(bf16[128,16,128]{2,0,1:T(8,128)(2,1)S(1)} %bitcast.136), channel_id=1, source_target_pairs={{0,128},{128,256},{256,384},{384,0},{1,129},{129,257},{257,385},{3... | collective-permute-start | bytes 1572872 | tf_op jit(solution)/shard_map/ppermute | solution.py:61
  (15 other events, 222.2 us)

commit v3 on v1

v3 whole, which is shorter than its diff:
```python
import jax
import jax.numpy as jnp
from jax import lax
from jax.experimental import pallas as pl
from jax.experimental.pallas import tpu as pltpu
from jax.sharding import Mesh, PartitionSpec as P

F32 = jnp.float32
BF16 = jnp.bfloat16
I32 = jnp.int32
Y, C, X, Z = 4, 2, 4, 16
MEMBERS = X * Z
ROWS = 16
EVERYONE = ("y", "c", "x", "z")
VMEM = pl.BlockSpec(memory_space=pltpu.VMEM)
SMEM = pl.BlockSpec(memory_space=pltpu.SMEM)


def exchange(array, axes):
    return lax.all_to_all(array, axes, split_axis=0, concat_axis=0, tiled=True)


def gather(array, axes):
    count = lax.axis_size(axes)
    return exchange(jnp.broadcast_to(array[None], (count,) + array.shape), axes)


def shift(array, axis, step):
    count = lax.axis_size(axis)
    return lax.ppermute(array, axis, [(i, (i + step) % count) for i in range(count)])


def after(array, *others):
    return lax.optimization_barrier((array,) + others)[0]


def kernel_call(body, in_specs, out_shape, scratch=(), cost=1_000_000, limit=16):
    return pl.pallas_call(
        body,
        out_shape=out_shape,
        in_specs=in_specs,
        out_specs=jax.tree.map(lambda _: VMEM, out_shape),
        scratch_shapes=list(scratch),
        compiler_params=pltpu.CompilerParams(vmem_limit_bytes=limit * 1024 * 1024),
        cost_estimate=pl.CostEstimate(flops=cost, bytes_accessed=cost, transcendentals=0),
    )


def bf16(*shape):
    return jax.ShapeDtypeStruct(shape, BF16)


def f32(*shape):
    return jax.ShapeDtypeStruct(shape, F32)


def dot(left, right, left_dim, right_dim):
    return lax.dot_general(
        left, right, (((left_dim,), (right_dim,)), ((), ())), preferred_element_type=F32
    )


def gelu_pair(v, upstream):
    scale = 0.7978845608028654
    square = v * v
    t = jnp.tanh(scale * (v + 0.044715 * (square * v)))
    half = 0.5 * (1.0 + t)
    slope = half + 0.5 * v * (1.0 - t * t) * (scale * (1.0 + 0.134145 * square))
    return (v * half).astype(BF16), (upstream * slope).astype(BF16)


def packet_kernel(where_ref, line_ref, coarse_ref, out_ref):
    y_index, c_index = where_ref[0], where_ref[1]
    width = coarse_ref.shape[2] // 4
    up = coarse_ref[y_index, :, pl.ds(pl.multiple_of(c_index * width, width), width)]
    down = coarse_ref[
        y_index, :, pl.ds(pl.multiple_of((c_index + 2) * width, width), width)
    ]
    lanes = lax.broadcasted_iota(I32, (ROWS, 128), 1)
    numbers = jnp.zeros((ROWS, 128), F32)
    for x in range(C * X):
        fine = line_ref[x, 0, 2]
        values = (line_ref[x, 0, 1], fine // 32, fine % 32)
        for i, value in enumerate(values):
            numbers = jnp.where(lanes == 4 * x + i, value.astype(F32), numbers)
    numbers = numbers.astype(BF16)
    for z in range(Z):
        out_ref[z, :, :width] = up
        out_ref[z, :, width : 2 * width] = down
        out_ref[z, :, 2 * width :] = numbers


def pick_kernel(where_ref, ids_ref, middle_ref, f0, f1, f2, f3, out_ref, other_ref):
    y_index, c_index = where_ref[0], where_ref[1]
    pieces = (f0, f1, f2, f3)
    owned = f0.shape[0]
    middle_width = middle_ref.shape[2]
    zeros = jnp.zeros(f0.shape[1:], BF16)

    def step(z, carry):
        for core in range(C):
            for x in range(X):
                place = 4 * (((core + c_index) % C) * X + x)
                fine_id = ids_ref[z, place + 1] * 32 + ids_ref[z, place + 2]
                owner = fine_id // owned
                choice = (y_index - owner // C + Y) % Y
                slot = fine_id % owned
                here = owner % C == c_index
                rows = zeros
                for s, piece in enumerate(pieces):
                    rows = jnp.where(jnp.logical_and(here, choice == s), piece[slot], rows)
                m = x * Z + z
                if core == 0:
                    out_ref[m, :, :middle_width] = middle_ref[ids_ref[z, place]]
                    out_ref[m, :, middle_width:] = rows
                else:
                    other_ref[m] = rows
        return carry

    lax.fori_loop(0, Z, step, 0, unroll=2)


def merge_kernel(send_ref, extra_ref, out_ref):
    middle_width = send_ref.shape[2] - extra_ref.shape[2]
    out_ref[:, :, :middle_width] = send_ref[:, :, :middle_width]
    out_ref[:, :, middle_width:] = send_ref[:, :, middle_width:] + extra_ref[...]


def coarse_kernel(
    where_ref, ids_ref, x_ref, g_ref, ox_ref, og_ref, h0, h1, h2, h3,
    s0, s1, s2, s3, back_ref, other_back_ref, half_ref, own_term, other_term,
):
    y_index = where_ref[0]
    c_index, x_index, z_index = where_ref[1], where_ref[2], where_ref[3]
    own_id = ids_ref[z_index, 4 * (c_index * X + x_index)] // 16
    other_id = ids_ref[z_index, 4 * ((1 - c_index) * X + x_index)] // 16
    width = h0.shape[1] // 2

    def level(identity, inputs, upstream, term_ref, into_ref):
        choice = (y_index - identity + Y) % Y
        for s, ref in enumerate((h0, h1, h2, h3)):

            @pl.when(choice == s)
            def _(ref=ref):
                half_ref[...] = ref[...]

        tokens, cotangent = inputs[...], upstream[...]
        before = dot(tokens, half_ref[:, :width], 1, 0)
        hidden_grad = dot(cotangent, half_ref[:, width:], 1, 0)
        hidden, before_grad = gelu_pair(before, hidden_grad)
        term_ref[:, :width] = dot(tokens, before_grad, 0, 0)
        term_ref[:, width:] = dot(cotangent, hidden, 0, 0)
        into_ref[...] = dot(before_grad, half_ref[:, :width], 1, 1)

    level(own_id, x_ref, g_ref, own_term, back_ref)
    level(other_id, ox_ref, og_ref, other_term, other_back_ref)
    for s, ref in enumerate((s0, s1, s2, s3)):
        block = (y_index + s) % Y
        own, other = own_id == block, other_id == block

        @pl.when(jnp.logical_and(own, other))
        def _(ref=ref):
            ref[...] = (own_term[...] + other_term[...]).astype(BF16)

        @pl.when(jnp.logical_and(own, jnp.logical_not(other)))
        def _(ref=ref):
            ref[...] = own_term[...].astype(BF16)

        @pl.when(jnp.logical_and(other, jnp.logical_not(own)))
        def _(ref=ref):
            ref[...] = other_term[...].astype(BF16)

        @pl.when(jnp.logical_not(jnp.logical_or(own, other)))
        def _(ref=ref):
            ref[...] = jnp.zeros(ref.shape, BF16)


def levels_kernel(x_ref, g_ref, w_ref, term_ref, back_ref):
    tokens, cotangent = x_ref[...], g_ref[...]
    middle = 256
    half = middle // 2
    before = dot(tokens, w_ref[:, :half], 1, 0)
    hidden_grad = dot(cotangent, w_ref[:, half:middle], 1, 0)
    hidden, before_grad = gelu_pair(before, hidden_grad)
    fine = w_ref[:, middle:]
    width = fine.shape[1]
    fine_before = dot(tokens, fine, 1, 0)
    fine_hidden_grad = pltpu.roll(dot(cotangent, fine, 1, 0), width // 2, 1)
    first = lax.broadcasted_iota(I32, fine_before.shape, 1) < width // 2
    fine_before = jnp.where(first, fine_before, 0.0)
    fine_hidden_grad = jnp.where(first, fine_hidden_grad, 0.0)
    fine_hidden, fine_before_grad = gelu_pair(fine_before, fine_hidden_grad)
    fine_hidden = pltpu.roll(fine_hidden.astype(F32), width // 2, 1).astype(BF16)
    term_ref[:, :half] = dot(tokens, before_grad, 0, 0).astype(BF16)
    term_ref[:, half:middle] = dot(cotangent, hidden, 0, 0).astype(BF16)
    term_ref[:, middle:] = (
        dot(tokens, fine_before_grad, 0, 0) + dot(cotangent, fine_hidden, 0, 0)
    ).astype(BF16)
    back_ref[...] = dot(before_grad, w_ref[:, :half], 1, 1) + dot(fine_before_grad, fine, 1, 1)


def collect_kernel(where_ref, ids_ref, parts_ref, keep_ref, send_ref, fine_ref, sums_ref):
    c_index = where_ref[1]
    middle = keep_ref.shape[2]
    half = keep_ref.shape[0]
    share = half // Y
    sums_ref[...] = jnp.zeros(sums_ref.shape, F32)

    def step(z, carry):
        for x in range(X):
            block = ids_ref[z, 4 * (c_index * X + x)]
            owner = block // share
            side = (owner + c_index) % C
            place = side * half + (owner // C) * share + block % share
            m = x * Z + z
            sums_ref[place] = sums_ref[place] + parts_ref[m, :, :middle].astype(F32)
            pair = (x % (X // 2)) * Z + z
            low = (x // (X // 2)) * 128
            fine_ref[pair, :, low : low + 128] = parts_ref[m, :, middle:]
        return carry

    lax.fori_loop(0, Z, step, 0, unroll=2)
    keep_ref[...] = sums_ref[:half].astype(BF16)
    send_ref[...] = sums_ref[half:].astype(BF16)


def fine_kernel(where_ref, ids_ref, *refs):
    pieces, out_ref, sums_ref = refs[:-2], refs[-2], refs[-1]
    group = where_ref[0] * C + where_ref[1]
    owned = out_ref.shape[0]
    sums_ref[...] = jnp.zeros(sums_ref.shape, F32)
    c_index = where_ref[1]
    for p, piece in enumerate(pieces):
        for core in range(C):

            def step(z, carry, p=p, core=core, piece=piece):
                for x in range(X):
                    place = 4 * (((core + c_index) % C) * X + x)
                    fine_id = ids_ref[p, z, place + 1] * 32 + ids_ref[p, z, place + 2]

                    @pl.when(fine_id // owned == group)
                    def _():
                        slot = fine_id % owned
                        pair = core * (MEMBERS // 2) + (x % (X // 2)) * Z + z
                        low = (x // (X // 2)) * 128
                        part = piece[pair, :, low : low + 128]
                        sums_ref[slot] = sums_ref[slot] + part.astype(F32)

                return carry

            lax.fori_loop(0, Z, step, 0, unroll=2)
    out_ref[...] = sums_ref[...].astype(BF16)


def on_device(tokens, cotangent, path, coarse_weights, middle_weights, fine_weights):
    y_index, c_index = lax.axis_index("y"), lax.axis_index("c")
    x_index = lax.axis_index("x")
    where = jnp.stack([y_index, c_index, x_index, lax.axis_index("z")]).astype(I32)
    fine_owned, _, fine_width = fine_weights.shape
    coarse_width = coarse_weights.shape[2]
    middle_width = middle_weights.shape[2]
    half = coarse_width // 2
    depth = MEMBERS * ROWS

    line = gather(path, ("c", "x"))
    packet = kernel_call(packet_kernel, [SMEM, SMEM, VMEM], bf16(Z, ROWS, half + 128))(
        where, line, coarse_weights
    )
    packets = exchange(packet, "z")

    fine_start = after(fine_weights, line)
    fine_rows = [fine_weights] + [shift(fine_start, "y", s) for s in range(1, Y)]
    both = jnp.concatenate([after(tokens, line), cotangent], axis=0)
    other_both = shift(both, "c", 1)
    *fine_rows, other_both = lax.optimization_barrier(fine_rows + [other_both])

    ids = packets[:, 0, half : half + 4 * C * X].astype(I32)
    send, extra = kernel_call(
        pick_kernel,
        [SMEM, SMEM, VMEM] + [VMEM] * Y,
        (bf16(MEMBERS, ROWS, middle_width + fine_width), bf16(MEMBERS, ROWS, fine_width)),
    )(where, ids, middle_weights, *fine_rows)
    send = kernel_call(merge_kernel, [VMEM] * 2, bf16(*send.shape))(send, shift(extra, "c", 1))
    mine = exchange(send, ("x", "z")).reshape(depth, -1)

    column = after(packets[:, :, :half].reshape(1, Z * ROWS, half), send)
    block = jnp.zeros((X, Z * ROWS, half), BF16)
    block = lax.dynamic_update_slice_in_dim(block, column, x_index, 0)
    for s in range(1, X):
        block = lax.dynamic_update_slice_in_dim(
            block, shift(column, "x", s), (x_index - s) % X, 0
        )
    block = block.reshape(depth, half)
    halves = [block] + [shift(block, "y", s) for s in range(1, Y)]
    length = tokens.shape[0]
    mine, *halves = lax.optimization_barrier([mine] + halves)
    slots = kernel_call(
        coarse_kernel,
        [SMEM, SMEM] + [VMEM] * 8,
        tuple([bf16(depth, half)] * Y + [f32(length, depth)] * 2),
        [
            pltpu.VMEM((depth, half), BF16),
            pltpu.VMEM((depth, half), F32),
            pltpu.VMEM((depth, half), F32),
        ],
        cost=20_000_000,
        limit=24,
    )(
        where, ids, tokens, cotangent, other_both[:length], other_both[length:], *halves
    )
    slots, coarse_back, other_back = slots[:Y], slots[Y], slots[Y + 1]

    terms, back = kernel_call(
        levels_kernel,
        [VMEM] * 3,
        (bf16(depth, middle_width + fine_width), f32(length, depth)),
        cost=10_000_000,
    )(tokens, cotangent, mine)
    parts = exchange(terms.reshape(MEMBERS, ROWS, -1), ("x", "z"))
    summed = slots[0].astype(F32)
    for s in range(1, Y):
        summed = summed + shift(after(slots[s], terms), "y", s).astype(F32)
    summed = summed.astype(BF16).reshape(X, Z * ROWS, half)
    column_sum = lax.dynamic_index_in_dim(summed, x_index, 0, keepdims=False).astype(F32)
    for s in range(1, X):
        leaving = lax.dynamic_index_in_dim(summed, (x_index + s) % X, 0, keepdims=False)
        column_sum = column_sum + shift(leaving, "x", s).astype(F32)
    column_sum = column_sum.astype(BF16).reshape(Z, ROWS, half)
    coarse_four = exchange(column_sum, "z")

    middle_count = middle_weights.shape[0]
    keep, leave, fine_pairs = kernel_call(
        collect_kernel,
        [SMEM, SMEM, VMEM],
        (
            bf16(middle_count // C, ROWS, middle_width),
            bf16(middle_count // C, ROWS, middle_width),
            bf16(MEMBERS // 2, ROWS, 2 * fine_width),
        ),
        [pltpu.VMEM((middle_count, ROWS, middle_width), F32)],
    )(where, ids, parts)
    numbers = jnp.pad(packets[None, :, 0, half:], ((0, 0), (0, ROWS - Z), (0, fine_width)))
    middle_half = keep.astype(F32) + shift(leave, "c", 1).astype(F32)
    middle_half = middle_half.astype(BF16).reshape(Y, -1, ROWS, middle_width)
    fine_both = jnp.concatenate([fine_pairs, shift(fine_pairs, "c", 1), numbers])
    middle_done = lax.dynamic_index_in_dim(middle_half, y_index, 0, keepdims=False).astype(F32)
    for s in range(1, Y):
        leaving = lax.dynamic_index_in_dim(middle_half, (y_index + s) % Y, 0, keepdims=False)
        middle_done = middle_done + shift(leaving, "y", s).astype(F32)
    fine_four = [fine_both] + [shift(fine_both, "y", s) for s in range(1, Y)]
    other_back = shift(after(other_back, middle_half), "c", 1)
    tokens_grad = (coarse_back + other_back + back).astype(BF16)
    coarse_four, middle_done = lax.optimization_barrier((coarse_four, middle_done))
    coarse_done = jnp.sum(coarse_four, axis=0, dtype=F32).astype(BF16)
    done = jnp.concatenate([middle_done.astype(BF16), coarse_done[None]], axis=0)
    total = gather(done, ("y", "c")).reshape((Y, C) + done.shape)
    middle_total = total[:, :, :-1].reshape(middle_weights.shape)
    coarse_total = total[:, :, -1].reshape(Y, C, ROWS, 2, half // 2)
    coarse_total = jnp.transpose(coarse_total, (0, 2, 3, 1, 4)).reshape(coarse_weights.shape)
    fine_ids = jnp.concatenate([f[MEMBERS:, :Z, : 4 * C * X] for f in fine_four]).astype(I32)
    fine_total = kernel_call(
        fine_kernel,
        [SMEM, SMEM] + [VMEM] * Y,
        bf16(fine_owned, ROWS, fine_width),
        [pltpu.VMEM((fine_owned, ROWS, fine_width), F32)],
    )(where, fine_ids, *fine_four)
    return (tokens_grad, coarse_total, middle_total, fine_total)


def solution(mesh):
    fine_mesh = Mesh(mesh.devices.reshape(Y, C, X, Z), EVERYONE)
    members = ("x", "z")
    return jax.shard_map(
        on_device,
        mesh=fine_mesh,
        in_specs=(
            P(EVERYONE, None),
            P(EVERYONE, None),
            P(EVERYONE, None),
            P(None, members, None),
            P(None, members, None),
            P(("y", "c"), members, None),
        ),
        out_specs=(
            P(EVERYONE, None),
            P(None, members, None),
            P(None, members, None),
            P(("y", "c"), members, None),
        ),
        check_vma=False,
    )
```

time: 337 us -> 282 us (0.84)
  blocking collectives: 203 us -> 0 us
  starting transfers between devices: 35.2 us -> 142 us
  Pallas kernels: 0 us -> 26.5 us
  waiting for transfers between devices: 65.3 us -> 91 us
  matrix products: 11.2 us -> 0 us
    all_to_all x5 -> x0, blocking collectives: 203 us -> none  [exchange(): return lax.all_to_all(array, axes, split_axis=0, concat_axis=0, tiled=True)]
    ppermute x0 -> x26, waiting for transfers between devices: none -> 86.6 us  [shift(): lax.ppermute(array, axis, [(i, (i + step) % count) for i in range(count)])]
    ppermute x0 -> x26, starting transfers between devices: none -> 78 us  [shift(): lax.ppermute(array, axis, [(i, (i + step) % count) for i in range(count)])]
    all_to_all x4 -> x6, waiting for transfers between devices: 65.3 us -> 4.41 us  [exchange(): return lax.all_to_all(array, axes, split_axis=0, concat_axis=0, tiled=True)]
    all_to_all x4 -> x6, starting transfers between devices: 35.2 us -> 64.2 us  [exchange(): return lax.all_to_all(array, axes, split_axis=0, concat_axis=0, tiled=True)]
    pallas_call x0 -> x7, Pallas kernels: none -> 26.5 us  [the longest x1 12.9 us: on_device(): kernel_call(fine_kernel, [SMEM, SMEM] + [VMEM] * Y, bf16(fine_owned, ROWS...]
    dot_general x21 -> x0, matrix products: 11.2 us -> none  [the longest x3 4.44 us: level_terms(): lax.dot_general(before_grad, up_half, (((1,), (1,)), ((), ())), preferred...]
    convert_element_type x1 -> x6, other arithmetic: 0.08 us -> 5.37 us  [the longest x1 1.88 us: on_device(): tokens_grad = (coarse_back + other_back + back).astype(BF16)]
  transfers between devices with their start and end apart: 4 -> 32, of which waited for: 4 -> 12; matrix products, arithmetic and copies ran while one was open for 2% -> 3% of each run, Pallas kernels for 0% -> 7%
where the time goes in v3:
time: 282 us; the launch traced here: 280 us
  starting transfers between devices  142 us (50%)
  waiting for transfers between devices  91 us (32%)
  Pallas kernels  26.5 us (9%)
  local copies, waits for them, and re-layouts  12.8 us (5%)
  other arithmetic  6.5 us (2%)
    ppermute x26, waiting for transfers between devices, shift(): lax.ppermute(array, axis, [(i, (i + step) % count) for i in range(count)])  86.6 us
    ppermute x26, starting transfers between devices, shift(): lax.ppermute(array, axis, [(i, (i + step) % count) for i in range(count)])  78 us
    all_to_all x6, starting transfers between devices, exchange(): return lax.all_to_all(array, axes, split_axis=0, concat_axis=0, tiled=True)  64.2 us
    pallas_call x1, Pallas kernels, on_device(): kernel_call(fine_kernel, [SMEM, SMEM] + [VMEM] * Y, bf16(fine_owned, ROWS...  12.9 us
    unnamed x29, local copies, waits for them, and re-layouts  6.24 us
  transfers between devices with their start and end apart: 32, of which 12 were waited for; matrix products, arithmetic and copies ran while one was open for 3% of the time, Pallas kernels for 7%

profile of v3, /device:TPU:1, one launch (start us, length us, event | category | flops | bytes accessed | tf_op | source)
XLA Modules:
  0.0 280.3 jit_solution(5061285334927057184)
XLA Ops:
  2.0 10.1 %all-to-all-start = ((s32[8,1,3]{2,1,0:T(1,128)}), s32[8,1,3]{2,1,0:T(1,128)S(1)}, u32[]{:S(2)}, u32[]{:S(2)}) async-start(s32[8,1,3]{2,1,0:T(1,128)} %broadcast_in_dim.21), calls=%async_computation | async-start | bytes 8192 | tf_op jit(solution)/shard_map/all_to_all | solution.py:20
  12.1 4.4 %all-to-all-done.line_ref = s32[8,1,3]{2,1,0:T(1,128)S(1)} async-done(((s32[8,1,3]{2,1,0:T(1,128)}), s32[8,1,3]{2,1,0:T(1,128)S(1)}, u32[]{:S(2)}, u32[]{:S(2)}) %all-to-all-start) | async-done | bytes 128 | tf_op jit(solution)/shard_map/all_to_all | solution.py:20
  18.7 10.8 %all-to-all-start.1 = ((bf16[16,16,384]{2,1,0:T(8,128)(2,1)}), bf16[16,16,384]{2,1,0:T(8,128)(2,1)S(1)}, u32[]{:S(2)}, u32[]{:S(2)}) async-start(bf16[16,16,384]{2,1,0:T(8,128)(2,1)} %shard_map.93), calls=%async_computation.1 | async-start | bytes 393216 | tf_op jit(solution)/shard_map/all_to_all | solution.py:20
  32.4 4.6 %collective-permute-start.2 = (bf16[128,16,128]{2,1,0:T(8,128)(2,1)S(1)}, bf16[128,16,128]{2,1,0:T(8,128)(2,1)S(1)}, u32[]{:S(2)}, u32[]{:S(2)}) collective-permute-start(bf16[128,16,128]{2,1,0:T(8,128)(2,1)S(1)} %copy-done.4), channel_id=1, source_target_pairs={{0,384},{128,0},{256,128},{384,256},{1,385},{129,1},{257,129},{385... | collective-permute-start | bytes 1572872 | tf_op jit(solution)/shard_map/ppermute | solution.py:30
  42.0 17.5 %collective-permute-done.2.f3 = bf16[128,16,128]{2,1,0:T(8,128)(2,1)S(1)} collective-permute-done((bf16[128,16,128]{2,1,0:T(8,128)(2,1)S(1)}, bf16[128,16,128]{2,1,0:T(8,128)(2,1)S(1)}, u32[]{:S(2)}, u32[]{:S(2)}) %collective-permute-start.2) | collective-permute-done | bytes 524320 | tf_op jit(solution)/shard_map/ppermute | solution.py:30
  59.5 6.1 %collective-permute-done.f1 = bf16[128,16,128]{2,1,0:T(8,128)(2,1)S(1)} collective-permute-done((bf16[128,16,128]{2,1,0:T(8,128)(2,1)S(1)}, bf16[128,16,128]{2,1,0:T(8,128)(2,1)S(1)}, u32[]{:S(2)}, u32[]{:S(2)}) %collective-permute-start) | collective-permute-done | bytes 524320 | tf_op jit(solution)/shard_map/ppermute | solution.py:30
  65.6 4.0 %shard_map.94 = (bf16[64,16,384]{2,1,0:T(8,128)(2,1)S(1)}, bf16[64,16,128]{2,1,0:T(8,128)(2,1)S(1)}) custom-call(s32[4]{0:T(128)S(1)} %pad_add_fusion.where_ref, s32[16,32]{1,0:T(8,128)S(1)} %fusion.7.ids_ref, bf16[64,16,256]{2,1,0:T(8,128)(2,1)S(1)} %copy-done.3, bf16[128,16,128]{2,1,0:T(8,128)(2,1)S(1)} %copy-done.4, ...), custom_call_target="tpu_custom_call" | custom-call | flops 1000000 | bytes 1000000 | tf_op jit(solution)/shard_map/pallas_call | solution.py:278
  74.2 13.3 %all-to-all-start.2 = ((bf16[64,16,384]{2,1,0:T(8,128)(2,1)}), bf16[64,16,384]{2,1,0:T(8,128)(2,1)S(1)}, u32[]{:S(2)}, u32[]{:S(2)}) async-start(bf16[64,16,384]{2,1,0:T(8,128)(2,1)} %shard_map.95), calls=%async_computation.2 | async-start | bytes 1572864 | tf_op jit(solution)/shard_map/all_to_all | solution.py:20
  90.5 3.6 %collective-permute-start.7 = (bf16[1,256,256]{2,1,0:T(8,128)(2,1)S(1)}, bf16[1,256,256]{2,1,0:T(8,128)(2,1)S(1)}, u32[]{:S(2)}, u32[]{:S(2)}) collective-permute-start(bf16[1,256,256]{2,1,0:T(8,128)(2,1)S(1)} %bitcast.58), channel_id=1, source_target_pairs={{0,48},{16,0},{32,16},{48,32},{1,49},{17,1},{33,17},{49,33},{2,50}... | collective-permute-start | bytes 393224 | tf_op jit(solution)/shard_map/ppermute | solution.py:30
  97.4 4.2 %collective-permute-done.6 = bf16[1,256,256]{2,1,0:T(8,128)(2,1)S(1)} collective-permute-done((bf16[1,256,256]{2,1,0:T(8,128)(2,1)S(1)}, bf16[1,256,256]{2,1,0:T(8,128)(2,1)S(1)}, u32[]{:S(2)}, u32[]{:S(2)}) %collective-permute-start.6) | collective-permute-done | bytes 131104 | tf_op jit(solution)/shard_map/ppermute | solution.py:30
  109.0 5.1 %collective-permute-done.10.h3 = bf16[1024,256]{1,0:T(8,128)(2,1)S(1)} collective-permute-done((bf16[1024,256]{1,0:T(8,128)(2,1)S(1)}, bf16[1024,256]{1,0:T(8,128)(2,1)S(1)}, u32[]{:S(2)}, u32[]{:S(2)}) %collective-permute-start.10) | collective-permute-done | bytes 524320 | tf_op jit(solution)/shard_map/ppermute | solution.py:30
  118.4 14.1 %collective-permute-done.8.h1 = bf16[1024,256]{1,0:T(8,128)(2,1)S(1)} collective-permute-done((bf16[1024,256]{1,0:T(8,128)(2,1)S(1)}, bf16[1024,256]{1,0:T(8,128)(2,1)S(1)}, u32[]{:S(2)}, u32[]{:S(2)}) %collective-permute-start.8) | collective-permute-done | bytes 524320 | tf_op jit(solution)/shard_map/ppermute | solution.py:30
  135.0 13.7 %all-to-all-start.3 = ((bf16[64,16,384]{2,1,0:T(8,128)(2,1)}), bf16[64,16,384]{2,1,0:T(8,128)(2,1)S(1)}, u32[]{:S(2)}, u32[]{:S(2)}) async-start(bf16[64,16,384]{2,1,0:T(8,128)(2,1)} %bitcast.10), calls=%async_computation.3 | async-start | bytes 1572864 | tf_op jit(solution)/shard_map/all_to_all | solution.py:20
  151.0 3.6 %shard_map.96 = (bf16[1024,256]{1,0:T(8,128)(2,1)S(1)}, bf16[1024,256]{1,0:T(8,128)(2,1)}, bf16[1024,256]{1,0:T(8,128)(2,1)}, bf16[1024,256]{1,0:T(8,128)(2,1)},...) custom-call(s32[4]{0:T(128)S(1)} %pad_add_fusion.where_ref, s32[16,32]{1,0:T(8,128)S(1)} %fusion.7.ids_ref, ...), custom_call_target="tpu_custom_call" | custom-call | flops 20000000 | bytes 20000000 | tf_op jit(solution)/shard_map/pallas_call | solution.py:297
  159.7 4.2 %collective-permute-start.15 = (bf16[1024,256]{1,0:T(8,128)(2,1)}, bf16[1024,256]{1,0:T(8,128)(2,1)}, u32[]{:S(2)}, u32[]{:S(2)}) collective-permute-start(bf16[1024,256]{1,0:T(8,128)(2,1)} %get-tuple-element.64), channel_id=1, source_target_pairs={{0,384},{128,0},{256,128},{384,256},{1,385},{129,1},{257,129},{385... | collective-permute-start | bytes 1572872 | tf_op jit(solution)/shard_map/ppermute | solution.py:30
  163.9 18.7 %collective-permute-done.13 = bf16[1024,256]{1,0:T(8,128)(2,1)S(1)} collective-permute-done((bf16[1024,256]{1,0:T(8,128)(2,1)}, bf16[1024,256]{1,0:T(8,128)(2,1)S(1)}, u32[]{:S(2)}, u32[]{:S(2)}) %collective-permute-start.13) | collective-permute-done | bytes 524320 | tf_op jit(solution)/shard_map/ppermute | solution.py:30
  190.7 3.6 %collective-permute-start.18 = (bf16[256,256]{1,0:T(8,128)(2,1)}, bf16[256,256]{1,0:T(8,128)(2,1)}, u32[]{:S(2)}, u32[]{:S(2)}) collective-permute-start(bf16[256,256]{1,0:T(8,128)(2,1)} %get-tuple-element.69), channel_id=1, source_target_pairs={{0,48},{16,0},{32,16},{48,32},{1,49},{17,1},{33,17},{49,33},{2,50}... | collective-permute-start | bytes 393224 | tf_op jit(solution)/shard_map/ppermute | solution.py:30
  199.4 4.3 %collective-permute-start.11 = (bf16[32,16,256]{2,1,0:T(8,128)(2,1)S(1)}, bf16[32,16,256]{2,1,0:T(8,128)(2,1)S(1)}, u32[]{:S(2)}, u32[]{:S(2)}) collective-permute-start(bf16[32,16,256]{2,1,0:T(8,128)(2,1)S(1)} %get-tuple-element.55), channel_id=1, source_target_pairs={{0,64},{64,0},{1,65},{65,1},{2,66},{66,2},{3,67},{67,3},{4,68},{68... | collective-permute-start | bytes 786440 | tf_op jit(solution)/shard_map/ppermute | solution.py:30
  205.6 11.4 %all-to-all-start.4 = ((bf16[16,16,256]{2,1,0:T(8,128)(2,1)}), bf16[16,16,256]{2,1,0:T(8,128)(2,1)}, u32[]{:S(2)}, u32[]{:S(2)}) async-start(bf16[16,16,256]{2,1,0:T(8,128)(2,1)} %bitcast.17), calls=%async_computation.4 | async-start | bytes 262144 | tf_op jit(solution)/shard_map/all_to_all | solution.py:20
  222.0 4.6 %collective-permute-start.21 = (bf16[8,16,256]{2,1,0:T(8,128)(2,1)S(1)}, bf16[8,16,256]{2,1,0:T(8,128)(2,1)S(1)}, u32[]{:S(2)}, u32[]{:S(2)}) collective-permute-start(bf16[8,16,256]{2,1,0:T(8,128)(2,1)S(1)} %get-tuple-element.74), channel_id=1, source_target_pairs={{0,384},{128,0},{256,128},{384,256},{1,385},{129,1},{257,129},{385... | collective-permute-start | bytes 196616 | tf_op jit(solution)/shard_map/ppermute | solution.py:30
  234.4 4.3 %collective-permute-start.24 = (bf16[65,16,256]{2,1,0:T(8,128)(2,1)S(1)}, bf16[65,16,256]{2,1,0:T(8,128)(2,1)S(1)}, u32[]{:S(2)}, u32[]{:S(2)}) collective-permute-start(bf16[65,16,256]{2,1,0:T(8,128)(2,1)S(1)} %fusion.1.refs_0_), channel_id=1, source_target_pairs={{0,256},{128,384},{256,0},{384,128},{1,257},{129,385},{257,1},{385... | collective-permute-start | bytes 1597448 | tf_op jit(solution)/shard_map/ppermute | solution.py:30
  242.8 4.9 %all-to-all-start.5 = ((bf16[8,9,16,256]{3,2,1,0:T(8,128)(2,1)}), bf16[8,9,16,256]{3,2,1,0:T(8,128)(2,1)}, u32[]{:S(2)}, u32[]{:S(2)}) async-start(bf16[8,9,16,256]{3,2,1,0:T(8,128)(2,1)} %broadcast_in_dim.24), calls=%async_computation.5 | async-start | bytes 1179648 | tf_op jit(solution)/shard_map/all_to_all | solution.py:20
  251.3 12.7 %collective-permute-done.23.refs_1_ = bf16[65,16,256]{2,1,0:T(8,128)(2,1)S(1)} collective-permute-done((bf16[65,16,256]{2,1,0:T(8,128)(2,1)S(1)}, bf16[65,16,256]{2,1,0:T(8,128)(2,1)S(1)}, u32[]{:S(2)}, u32[]{:S(2)}) %collective-permute-start.23) | collective-permute-done | bytes 532512 | tf_op jit(solution)/shard_map/ppermute | solution.py:30
  263.9 12.9 %shard_map.99 = bf16[128,16,128]{2,1,0:T(8,128)(2,1)} custom-call(s32[4]{0:T(128)S(1)} %pad_add_fusion.where_ref, s32[4,16,32]{2,1,0:T(8,128)S(1)} %maximum_convert_fusion.ids_ref, bf16[65,16,256]{2,1,0:T(8,128)(2,1)S(1)} %fusion.1.refs_0_, bf16[65,16,256]{2,1,0:T(8,128)(2,1)S(1)} %collective-permute-done.23.refs_1_, ...), custom_call_target="tpu_custom_call" | custom-call | flops 1000000 | bytes 1000000 | tf_op jit(solution)/shard_map/pallas_call | solution.py:361
  (109 shorter events, 82.3 us)
Async XLA Ops:
  2.0 14.6 %all-to-all-start = ((s32[8,1,3]{2,1,0:T(1,128)}), s32[8,1,3]{2,1,0:T(1,128)S(1)}, u32[]{:S(2)}, u32[]{:S(2)}) async-start(s32[8,1,3]{2,1,0:T(1,128)} %broadcast_in_dim.21), calls=%async_computation | async-start | bytes 8192 | tf_op jit(solution)/shard_map/all_to_all | solution.py:20
  18.7 46.8 %all-to-all-start.1 = ((bf16[16,16,384]{2,1,0:T(8,128)(2,1)}), bf16[16,16,384]{2,1,0:T(8,128)(2,1)S(1)}, u32[]{:S(2)}, u32[]{:S(2)}) async-start(bf16[16,16,384]{2,1,0:T(8,128)(2,1)} %shard_map.93), calls=%async_computation.1 | async-start | bytes 393216 | tf_op jit(solution)/shard_map/all_to_all | solution.py:20
  32.4 27.1 %collective-permute-start.2 = (bf16[128,16,128]{2,1,0:T(8,128)(2,1)S(1)}, bf16[128,16,128]{2,1,0:T(8,128)(2,1)S(1)}, u32[]{:S(2)}, u32[]{:S(2)}) collective-permute-start(bf16[128,16,128]{2,1,0:T(8,128)(2,1)S(1)} %copy-done.4), channel_id=1, source_target_pairs={{0,384},{128,0},{256,128},{384,256},{1,385},{129,1},{257,129},{385... | collective-permute-start | bytes 1572872 | tf_op jit(solution)/shard_map/ppermute | solution.py:30
  37.1 22.4 %collective-permute-start.1 = (bf16[128,16,128]{2,1,0:T(8,128)(2,1)S(1)}, bf16[128,16,128]{2,1,0:T(8,128)(2,1)S(1)}, u32[]{:S(2)}, u32[]{:S(2)}) collective-permute-start(bf16[128,16,128]{2,1,0:T(8,128)(2,1)S(1)} %copy-done.4), channel_id=1, source_target_pairs={{0,256},{128,384},{256,0},{384,128},{1,257},{129,385},{257,1},{385... | collective-permute-start | bytes 1572872 | tf_op jit(solution)/shard_map/ppermute | solution.py:30
  39.4 26.2 %collective-permute-start = (bf16[128,16,128]{2,1,0:T(8,128)(2,1)S(1)}, bf16[128,16,128]{2,1,0:T(8,128)(2,1)S(1)}, u32[]{:S(2)}, u32[]{:S(2)}) collective-permute-start(bf16[128,16,128]{2,1,0:T(8,128)(2,1)S(1)} %copy-done.4), channel_id=1, source_target_pairs={{0,128},{128,256},{256,384},{384,0},{1,129},{129,257},{257,385},{3... | collective-permute-start | bytes 1572872 | tf_op jit(solution)/shard_map/ppermute | solution.py:30
  74.2 59.1 %all-to-all-start.2 = ((bf16[64,16,384]{2,1,0:T(8,128)(2,1)}), bf16[64,16,384]{2,1,0:T(8,128)(2,1)S(1)}, u32[]{:S(2)}, u32[]{:S(2)}) async-start(bf16[64,16,384]{2,1,0:T(8,128)(2,1)} %shard_map.95), calls=%async_computation.2 | async-start | bytes 1572864 | tf_op jit(solution)/shard_map/all_to_all | solution.py:20
  104.0 13.6 %collective-permute-start.9 = (bf16[1024,256]{1,0:T(8,128)(2,1)S(1)}, bf16[1024,256]{1,0:T(8,128)(2,1)S(1)}, u32[]{:S(2)}, u32[]{:S(2)}) collective-permute-start(bf16[1024,256]{1,0:T(8,128)(2,1)S(1)} %bitcast.49), channel_id=1, source_target_pairs={{0,256},{128,384},{256,0},{384,128},{1,257},{129,385},{257,1},{385... | collective-permute-start | bytes 1572872 | tf_op jit(solution)/shard_map/ppermute | solution.py:30
  106.2 26.2 %collective-permute-start.8 = (bf16[1024,256]{1,0:T(8,128)(2,1)S(1)}, bf16[1024,256]{1,0:T(8,128)(2,1)S(1)}, u32[]{:S(2)}, u32[]{:S(2)}) collective-permute-start(bf16[1024,256]{1,0:T(8,128)(2,1)S(1)} %bitcast.50), channel_id=1, source_target_pairs={{0,128},{128,256},{256,384},{384,0},{1,129},{129,257},{257,385},{3... | collective-permute-start | bytes 1572872 | tf_op jit(solution)/shard_map/ppermute | solution.py:30
  135.0 62.6 %all-to-all-start.3 = ((bf16[64,16,384]{2,1,0:T(8,128)(2,1)}), bf16[64,16,384]{2,1,0:T(8,128)(2,1)S(1)}, u32[]{:S(2)}, u32[]{:S(2)}) async-start(bf16[64,16,384]{2,1,0:T(8,128)(2,1)} %bitcast.10), calls=%async_computation.3 | async-start | bytes 1572864 | tf_op jit(solution)/shard_map/all_to_all | solution.py:20
  155.4 27.2 %collective-permute-start.13 = (bf16[1024,256]{1,0:T(8,128)(2,1)}, bf16[1024,256]{1,0:T(8,128)(2,1)S(1)}, u32[]{:S(2)}, u32[]{:S(2)}) collective-permute-start(bf16[1024,256]{1,0:T(8,128)(2,1)} %get-tuple-element.60), channel_id=1, source_target_pairs={{0,128},{128,256},{256,384},{384,0},{1,129},{129,257},{257,385},{3... | collective-permute-start | bytes 1572872 | tf_op jit(solution)/shard_map/ppermute | solution.py:30
  157.4 25.3 %collective-permute-start.14 = (bf16[1024,256]{1,0:T(8,128)(2,1)}, bf16[1024,256]{1,0:T(8,128)(2,1)}, u32[]{:S(2)}, u32[]{:S(2)}) collective-permute-start(bf16[1024,256]{1,0:T(8,128)(2,1)} %get-tuple-element.62), channel_id=1, source_target_pairs={{0,256},{128,384},{256,0},{384,128},{1,257},{129,385},{257,1},{385... | collective-permute-start | bytes 1572872 | tf_op jit(solution)/shard_map/ppermute | solution.py:30
  159.7 25.7 %collective-permute-start.15 = (bf16[1024,256]{1,0:T(8,128)(2,1)}, bf16[1024,256]{1,0:T(8,128)(2,1)}, u32[]{:S(2)}, u32[]{:S(2)}) collective-permute-start(bf16[1024,256]{1,0:T(8,128)(2,1)} %get-tuple-element.64), channel_id=1, source_target_pairs={{0,384},{128,0},{256,128},{384,256},{1,385},{129,1},{257,129},{385... | collective-permute-start | bytes 1572872 | tf_op jit(solution)/shard_map/ppermute | solution.py:30
  187.8 16.0 %collective-permute-start.16 = (bf16[256,256]{1,0:T(8,128)(2,1)}, bf16[256,256]{1,0:T(8,128)(2,1)}, u32[]{:S(2)}, u32[]{:S(2)}) collective-permute-start(bf16[256,256]{1,0:T(8,128)(2,1)} %get-tuple-element.68), channel_id=1, source_target_pairs={{0,16},{16,32},{32,48},{48,0},{1,17},{17,33},{33,49},{49,1},{2,18}... | collective-permute-start | bytes 393224 | tf_op jit(solution)/shard_map/ppermute | solution.py:30
  199.4 20.5 %collective-permute-start.11 = (bf16[32,16,256]{2,1,0:T(8,128)(2,1)S(1)}, bf16[32,16,256]{2,1,0:T(8,128)(2,1)S(1)}, u32[]{:S(2)}, u32[]{:S(2)}) collective-permute-start(bf16[32,16,256]{2,1,0:T(8,128)(2,1)S(1)} %get-tuple-element.55), channel_id=1, source_target_pairs={{0,64},{64,0},{1,65},{65,1},{2,66},{66,2},{3,67},{67,3},{4,68},{68... | collective-permute-start | bytes 786440 | tf_op jit(solution)/shard_map/ppermute | solution.py:30
  205.6 35.4 %all-to-all-start.4 = ((bf16[16,16,256]{2,1,0:T(8,128)(2,1)}), bf16[16,16,256]{2,1,0:T(8,128)(2,1)}, u32[]{:S(2)}, u32[]{:S(2)}) async-start(bf16[16,16,256]{2,1,0:T(8,128)(2,1)} %bitcast.17), calls=%async_computation.4 | async-start | bytes 262144 | tf_op jit(solution)/shard_map/all_to_all | solution.py:20
  217.0 14.9 %collective-permute-start.22 = (bf16[32,16,256]{2,1,0:T(8,128)(2,1)S(1)}, bf16[32,16,256]{2,1,0:T(8,128)(2,1)S(1)}, u32[]{:S(2)}, u32[]{:S(2)}) collective-permute-start(bf16[32,16,256]{2,1,0:T(8,128)(2,1)S(1)} %get-tuple-element.67), channel_id=1, source_target_pairs={{0,64},{64,0},{1,65},{65,1},{2,66},{66,2},{3,67},{67,3},{4,68},{68... | collective-permute-start | bytes 786440 | tf_op jit(solution)/shard_map/ppermute | solution.py:30
  220.1 14.3 %collective-permute-start.19 = (bf16[8,16,256]{2,1,0:T(8,128)(2,1)S(1)}, bf16[8,16,256]{2,1,0:T(8,128)(2,1)S(1)}, u32[]{:S(2)}, u32[]{:S(2)}) collective-permute-start(bf16[8,16,256]{2,1,0:T(8,128)(2,1)S(1)} %get-tuple-element.73), channel_id=1, source_target_pairs={{0,128},{128,256},{256,384},{384,0},{1,129},{129,257},{257,385},{3... | collective-permute-start | bytes 196616 | tf_op jit(solution)/shard_map/ppermute | solution.py:30
  222.0 16.7 %collective-permute-start.21 = (bf16[8,16,256]{2,1,0:T(8,128)(2,1)S(1)}, bf16[8,16,256]{2,1,0:T(8,128)(2,1)S(1)}, u32[]{:S(2)}, u32[]{:S(2)}) collective-permute-start(bf16[8,16,256]{2,1,0:T(8,128)(2,1)S(1)} %get-tuple-element.74), channel_id=1, source_target_pairs={{0,384},{128,0},{256,128},{384,256},{1,385},{129,1},{257,129},{385... | collective-permute-start | bytes 196616 | tf_op jit(solution)/shard_map/ppermute | solution.py:30
  226.6 14.3 %collective-permute-start.20 = (bf16[8,16,256]{2,1,0:T(8,128)(2,1)S(1)}, bf16[8,16,256]{2,1,0:T(8,128)(2,1)S(1)}, u32[]{:S(2)}, u32[]{:S(2)}) collective-permute-start(bf16[8,16,256]{2,1,0:T(8,128)(2,1)S(1)} %get-tuple-element.75), channel_id=1, source_target_pairs={{0,256},{128,384},{256,0},{384,128},{1,257},{129,385},{257,1},{385... | collective-permute-start | bytes 196616 | tf_op jit(solution)/shard_map/ppermute | solution.py:30
  229.4 18.4 %collective-permute-start.12 = (f32[128,1024]{1,0:T(8,128)}, f32[128,1024]{1,0:T(8,128)}, u32[]{:S(2)}, u32[]{:S(2)}) collective-permute-start(f32[128,1024]{1,0:T(8,128)} %get-tuple-element.56), channel_id=1, source_target_pairs={{0,64},{64,0},{1,65},{65,1},{2,66},{66,2},{3,67},{67,3},{4,68},{68... | collective-permute-start | bytes 1572872 | tf_op jit(solution)/shard_map/ppermute | solution.py:30
  231.9 17.7 %collective-permute-start.25 = (bf16[65,16,256]{2,1,0:T(8,128)(2,1)S(1)}, bf16[65,16,256]{2,1,0:T(8,128)(2,1)S(1)}, u32[]{:S(2)}, u32[]{:S(2)}) collective-permute-start(bf16[65,16,256]{2,1,0:T(8,128)(2,1)S(1)} %fusion.1.refs_0_), channel_id=1, source_target_pairs={{0,384},{128,0},{256,128},{384,256},{1,385},{129,1},{257,129},{385... | collective-permute-start | bytes 1597448 | tf_op jit(solution)/shard_map/ppermute | solution.py:30
  234.4 16.8 %collective-permute-start.24 = (bf16[65,16,256]{2,1,0:T(8,128)(2,1)S(1)}, bf16[65,16,256]{2,1,0:T(8,128)(2,1)S(1)}, u32[]{:S(2)}, u32[]{:S(2)}) collective-permute-start(bf16[65,16,256]{2,1,0:T(8,128)(2,1)S(1)} %fusion.1.refs_0_), channel_id=1, source_target_pairs={{0,256},{128,384},{256,0},{384,128},{1,257},{129,385},{257,1},{385... | collective-permute-start | bytes 1597448 | tf_op jit(solution)/shard_map/ppermute | solution.py:30
  238.7 25.2 %collective-permute-start.23 = (bf16[65,16,256]{2,1,0:T(8,128)(2,1)S(1)}, bf16[65,16,256]{2,1,0:T(8,128)(2,1)S(1)}, u32[]{:S(2)}, u32[]{:S(2)}) collective-permute-start(bf16[65,16,256]{2,1,0:T(8,128)(2,1)S(1)} %fusion.1.refs_0_), channel_id=1, source_target_pairs={{0,128},{128,256},{256,384},{384,0},{1,129},{129,257},{257,385},{3... | collective-permute-start | bytes 1597448 | tf_op jit(solution)/shard_map/ppermute | solution.py:30
  242.8 34.0 %all-to-all-start.5 = ((bf16[8,9,16,256]{3,2,1,0:T(8,128)(2,1)}), bf16[8,9,16,256]{3,2,1,0:T(8,128)(2,1)}, u32[]{:S(2)}, u32[]{:S(2)}) async-start(bf16[8,9,16,256]{3,2,1,0:T(8,128)(2,1)} %broadcast_in_dim.24), calls=%async_computation.5 | async-start | bytes 1179648 | tf_op jit(solution)/shard_map/all_to_all | solution.py:20
  (22 other events, 236.8 us)

commit v4 on v3

v4 whole, which is shorter than its diff:
```python
import jax
import jax.numpy as jnp
from jax import lax
from jax.experimental import pallas as pl
from jax.experimental.pallas import tpu as pltpu
from jax.sharding import Mesh, PartitionSpec as P

F32 = jnp.float32
BF16 = jnp.bfloat16
I32 = jnp.int32
Y, C, X, Z = 4, 2, 4, 16
MEMBERS = X * Z
ROWS = 16
EVERYONE = ("y", "c", "x", "z")
VMEM = pl.BlockSpec(memory_space=pltpu.VMEM)
SMEM = pl.BlockSpec(memory_space=pltpu.SMEM)


def exchange(array, axes):
    return lax.all_to_all(array, axes, split_axis=0, concat_axis=0, tiled=True)


def gather(array, axes):
    count = lax.axis_size(axes)
    return exchange(jnp.broadcast_to(array[None], (count,) + array.shape), axes)


def shift(array, axis, step):
    count = lax.axis_size(axis)
    return lax.ppermute(array, axis, [(i, (i + step) % count) for i in range(count)])


def after(array, *others):
    return lax.optimization_barrier((array,) + others)[0]


def kernel_call(body, in_specs, out_shape, scratch=(), cost=1_000_000, limit=16):
    return pl.pallas_call(
        body,
        out_shape=out_shape,
        in_specs=in_specs,
        out_specs=jax.tree.map(lambda _: VMEM, out_shape),
        scratch_shapes=list(scratch),
        compiler_params=pltpu.CompilerParams(vmem_limit_bytes=limit * 1024 * 1024),
        cost_estimate=pl.CostEstimate(flops=cost, bytes_accessed=cost, transcendentals=0),
    )


def bf16(*shape):
    return jax.ShapeDtypeStruct(shape, BF16)


def f32(*shape):
    return jax.ShapeDtypeStruct(shape, F32)


def dot(left, right, left_dim, right_dim):
    return lax.dot_general(
        left, right, (((left_dim,), (right_dim,)), ((), ())), preferred_element_type=F32
    )


def gelu_pair(v, upstream):
    scale = 0.7978845608028654
    square = v * v
    t = jnp.tanh(scale * (v + 0.044715 * (square * v)))
    half = 0.5 * (1.0 + t)
    slope = half + 0.5 * v * (1.0 - t * t) * (scale * (1.0 + 0.134145 * square))
    return (v * half).astype(BF16), (upstream * slope).astype(BF16)


def packet_kernel(where_ref, own_ref, other_ref, coarse_ref, out_ref):
    y_index, c_index = where_ref[0], where_ref[1]
    width = coarse_ref.shape[2] // 4
    up = coarse_ref[y_index, :, pl.ds(pl.multiple_of(c_index * width, width), width)]
    down = coarse_ref[
        y_index, :, pl.ds(pl.multiple_of((c_index + 2) * width, width), width)
    ]
    lanes = lax.broadcasted_iota(I32, (ROWS, 128), 1)
    numbers = jnp.zeros((ROWS, 128), F32)
    for core, ref in ((c_index, own_ref), (1 - c_index, other_ref)):
        values = (ref[0, 1], ref[0, 2] // 32, ref[0, 2] % 32)
        for i, value in enumerate(values):
            numbers = jnp.where(lanes == 4 * core + i, value.astype(F32), numbers)
    numbers = numbers.astype(BF16)
    for z in range(Z):
        out_ref[z, :, :width] = up
        out_ref[z, :, width : 2 * width] = down
        out_ref[z, :, 2 * width :] = numbers


def numbers_kernel(grid_ref, out_ref):
    width = grid_ref.shape[3] - 128
    rows = lax.broadcasted_iota(I32, (ROWS, 128), 0)
    total = jnp.zeros((ROWS, 128), F32)
    for x in range(X):
        line = jnp.zeros((ROWS, 128), F32)
        for z in range(Z):
            line = jnp.where(rows == z, grid_ref[x, z, :, width:].astype(F32), line)
        total = total + (pltpu.roll(line, 8 * x, 1) if x else line)
    out_ref[0, :, :128] = total.astype(BF16)
    out_ref[0, :, 128:] = jnp.zeros((ROWS, 128), BF16)


def pick_kernel(
    where_ref, ids_ref, middle_ref, f0, f1, f2a, f2b, f3, out_ref, other_ref
):
    y_index, c_index = where_ref[0], where_ref[1]
    owned = f0.shape[0]
    split = f2a.shape[0]
    middle_width = middle_ref.shape[2]
    zeros = jnp.zeros(f0.shape[1:], BF16)

    def step(z, carry):
        for core in range(C):
            for x in range(X):
                place = 4 * ((core + c_index) % C)
                fine_id = ids_ref[x, z, place + 1] * 32 + ids_ref[x, z, place + 2]
                owner = fine_id // owned
                choice = (y_index - owner // C + Y) % Y
                slot = fine_id % owned
                choice = jnp.where(owner % C == c_index, choice, Y + 1)
                choice = jnp.where(jnp.logical_and(choice == 2, slot >= split), Y, choice)
                rows = zeros
                for s, piece in enumerate((f0, f1, f2a, f3, f2b)):
                    here = choice == s
                    local = slot % split if s in (2, 4) else slot
                    rows = jnp.where(here, piece[local], rows)
                m = x * Z + z
                if core == 0:
                    out_ref[m, :, :middle_width] = middle_ref[ids_ref[x, z, place]]
                    out_ref[m, :, middle_width:] = rows
                else:
                    other_ref[m] = rows
        return carry

    lax.fori_loop(0, Z, step, 0, unroll=2)


def merge_kernel(send_ref, extra_ref, out_ref):
    middle_width = send_ref.shape[2] - extra_ref.shape[2]
    out_ref[:, :, :middle_width] = send_ref[:, :, :middle_width]
    out_ref[:, :, middle_width:] = send_ref[:, :, middle_width:] + extra_ref[...]


def coarse_kernel(
    where_ref, ids_ref, x_ref, g_ref, ox_ref, og_ref, h0, h1, h2a, h2b, h3,
    s0, s1, s2, s3, back_ref, other_back_ref, half_ref, own_term, other_term,
):
    y_index = where_ref[0]
    c_index, x_index, z_index = where_ref[1], where_ref[2], where_ref[3]
    own_id = ids_ref[x_index, z_index, 4 * c_index] // 16
    other_id = ids_ref[x_index, z_index, 4 * (1 - c_index)] // 16
    width = h0.shape[1] // 2

    def level(identity, inputs, upstream, term_ref, into_ref):
        choice = (y_index - identity + Y) % Y
        for s, ref in ((0, h0), (1, h1), (3, h3)):

            @pl.when(choice == s)
            def _(ref=ref):
                half_ref[...] = ref[...]

        @pl.when(choice == 2)
        def _():
            half_ref[: h2a.shape[0]] = h2a[...]
            half_ref[h2a.shape[0] :] = h2b[...]

        tokens, cotangent = inputs[...], upstream[...]
        before = dot(tokens, half_ref[:, :width], 1, 0)
        hidden_grad = dot(cotangent, half_ref[:, width:], 1, 0)
        hidden, before_grad = gelu_pair(before, hidden_grad)
        term_ref[:, :width] = dot(tokens, before_grad, 0, 0)
        term_ref[:, width:] = dot(cotangent, hidden, 0, 0)
        into_ref[...] = dot(before_grad, half_ref[:, :width], 1, 1)

    level(own_id, x_ref, g_ref, own_term, back_ref)
    level(other_id, ox_ref, og_ref, other_term, other_back_ref)
    for s, ref in enumerate((s0, s1, s2, s3)):
        block = (y_index + s) % Y
        own, other = own_id == block, other_id == block

        @pl.when(jnp.logical_and(own, other))
        def _(ref=ref):
            ref[...] = (own_term[...] + other_term[...]).astype(BF16)

        @pl.when(jnp.logical_and(own, jnp.logical_not(other)))
        def _(ref=ref):
            ref[...] = own_term[...].astype(BF16)

        @pl.when(jnp.logical_and(other, jnp.logical_not(own)))
        def _(ref=ref):
            ref[...] = other_term[...].astype(BF16)

        @pl.when(jnp.logical_not(jnp.logical_or(own, other)))
        def _(ref=ref):
            ref[...] = jnp.zeros(ref.shape, BF16)


def levels_kernel(x_ref, g_ref, w_ref, term_ref, back_ref):
    tokens, cotangent = x_ref[...], g_ref[...]
    middle = 256
    half = middle // 2
    before = dot(tokens, w_ref[:, :half], 1, 0)
    hidden_grad = dot(cotangent, w_ref[:, half:middle], 1, 0)
    hidden, before_grad = gelu_pair(before, hidden_grad)
    fine = w_ref[:, middle:]
    width = fine.shape[1]
    fine_before = dot(tokens, fine, 1, 0)
    fine_hidden_grad = pltpu.roll(dot(cotangent, fine, 1, 0), width // 2, 1)
    first = lax.broadcasted_iota(I32, fine_before.shape, 1) < width // 2
    fine_before = jnp.where(first, fine_before, 0.0)
    fine_hidden_grad = jnp.where(first, fine_hidden_grad, 0.0)
    fine_hidden, fine_before_grad = gelu_pair(fine_before, fine_hidden_grad)
    fine_hidden = pltpu.roll(fine_hidden.astype(F32), width // 2, 1).astype(BF16)
    term_ref[:, :half] = dot(tokens, before_grad, 0, 0).astype(BF16)
    term_ref[:, half:middle] = dot(cotangent, hidden, 0, 0).astype(BF16)
    term_ref[:, middle:] = (
        dot(tokens, fine_before_grad, 0, 0) + dot(cotangent, fine_hidden, 0, 0)
    ).astype(BF16)
    back_ref[...] = dot(before_grad, w_ref[:, :half], 1, 1) + dot(fine_before_grad, fine, 1, 1)


def collect_kernel(where_ref, ids_ref, parts_ref, keep_ref, leave_ref, sums_ref):
    c_index = where_ref[1]
    middle = keep_ref.shape[2]
    half = keep_ref.shape[0]
    share = half // Y
    sums_ref[...] = jnp.zeros(sums_ref.shape, F32)

    def step(z, carry):
        for x in range(X):
            block = ids_ref[x, z, 4 * c_index]
            owner = block // share
            side = (owner + c_index) % C
            place = side * half + (owner // C) * share + block % share
            m = x * Z + z
            sums_ref[place] = sums_ref[place] + parts_ref[m, :, :middle].astype(F32)
            pair = half + (x % (X // 2)) * Z + z
            low = (x // (X // 2)) * 128
            leave_ref[pair, :, low : low + 128] = parts_ref[m, :, middle:]
        return carry

    lax.fori_loop(0, Z, step, 0, unroll=2)
    keep_ref[...] = sums_ref[:half]
    leave_ref[:half] = sums_ref[half:].astype(BF16)


def combine_kernel(
    where_ref, keep_ref, leave_ref, arrived_ref, numbers_ref, packet_ref, s0, s1, s3
):
    y_index = where_ref[0]
    half = keep_ref.shape[0]
    share = half // Y
    pairs = MEMBERS // 2
    packet_ref[:pairs] = leave_ref[half:]
    packet_ref[pairs : 2 * pairs] = arrived_ref[half:]
    packet_ref[2 * pairs] = numbers_ref[0]
    for s, ref in ((0, s0), (1, s1), (3, s3)):
        at = pl.ds(((y_index + s) % Y) * share, share)
        ref[...] = keep_ref[at] + arrived_ref[at].astype(F32)
    at = pl.ds(((y_index + 2) % Y) * share, share)
    packet_ref[2 * pairs + 1 :] = (keep_ref[at] + arrived_ref[at].astype(F32)).astype(BF16)


def relay_kernel(r1, r3, s1, s3, up_ref, down_ref):
    pairs = MEMBERS // 2
    share = s1.shape[0]
    middle = 2 * pairs + 1
    split = share // 2
    up_ref[:pairs] = r1[:pairs]
    up_ref[pairs] = r1[2 * pairs]
    up_ref[pairs + 1 : pairs + 1 + split] = (
        s1[:split] + r1[middle : middle + split].astype(F32)
    ).astype(BF16)
    up_ref[pairs + 1 + split :] = s1[split:].astype(BF16)
    down_ref[:pairs] = r3[pairs : 2 * pairs]
    down_ref[pairs : pairs + split] = s3[:split].astype(BF16)
    down_ref[pairs + split :] = (s3[split:] + r3[middle + split :].astype(F32)).astype(BF16)


def add_fine(group, c_index, owned, ids_ref, p, core, piece, base, sums_ref):
    def step(z, carry):
        for x in range(X):
            place = x * 8 + 4 * ((core + c_index) % C)
            fine_id = ids_ref[p, z, place + 1] * 32 + ids_ref[p, z, place + 2]
            slot = jnp.where(fine_id // owned == group, fine_id % owned, owned)
            pair = base + (x % (X // 2)) * Z + z
            low = (x // (X // 2)) * 128
            part = piece[pair, :, low : low + 128]
            sums_ref[slot] = sums_ref[slot] + part.astype(F32)
        return carry

    lax.fori_loop(0, Z, step, 0, unroll=4)


def first_fine_kernel(where_ref, ids_ref, p0, p1, p3, sums_ref):
    group = where_ref[0] * C + where_ref[1]
    owned = sums_ref.shape[0] - 8
    sums_ref[...] = jnp.zeros(sums_ref.shape, F32)
    for p, piece in enumerate((p0, p1, p3)):
        for core in range(C):
            base = core * (MEMBERS // 2)
            add_fine(group, where_ref[1], owned, ids_ref, p, core, piece, base, sums_ref)


def last_fine_kernel(where_ref, ids_ref, before_ref, q1, q3, out_ref, sums_ref):
    group = where_ref[0] * C + where_ref[1]
    owned = sums_ref.shape[0] - 8
    sums_ref[...] = before_ref[...]
    for core, piece in enumerate((q1, q3)):
        add_fine(group, where_ref[1], owned, ids_ref, 0, core, piece, 0, sums_ref)
    out_ref[...] = sums_ref[:owned].astype(BF16)


def spread_kernel(total_ref, coarse_ref, middle_ref):
    share = total_ref.shape[1] - 1
    width = total_ref.shape[3] // 2
    for y in range(Y):
        for core in range(C):
            g = y * C + core
            middle_ref[g * share : (g + 1) * share] = total_ref[g, :share]
            low = core * width
            coarse_ref[y, :, low : low + width] = total_ref[g, share, :, :width]
            low = (C + core) * width
            coarse_ref[y, :, low : low + width] = total_ref[g, share, :, width:]


def on_device(tokens, cotangent, path, coarse_weights, middle_weights, fine_weights):
    y_index, c_index = lax.axis_index("y"), lax.axis_index("c")
    x_index = lax.axis_index("x")
    where = jnp.stack([y_index, c_index, x_index, lax.axis_index("z")]).astype(I32)
    fine_owned, _, fine_width = fine_weights.shape
    coarse_width = coarse_weights.shape[2]
    middle_width = middle_weights.shape[2]
    half = coarse_width // 2
    depth = MEMBERS * ROWS

    other_path = shift(path, "c", 1)
    packet = kernel_call(packet_kernel, [SMEM, SMEM, SMEM, VMEM], bf16(Z, ROWS, half + 128))(
        where, path, other_path, coarse_weights
    )
    packets = gather(exchange(packet, "z"), "x").reshape(X, Z, ROWS, half + 128)

    fine_one = shift(after(fine_weights, packet), "y", 1)
    fine_three = shift(after(fine_weights, packet), "y", 3)
    split = fine_owned // 2
    fine_rows = [
        fine_weights,
        fine_one,
        shift(fine_one[:split], "y", 1),
        shift(fine_three[split:], "y", 3),
        fine_three,
    ]
    both = jnp.concatenate([after(tokens, packet), cotangent], axis=0)
    other_both = shift(both, "c", 1)
    *fine_rows, other_both = lax.optimization_barrier(fine_rows + [other_both])

    ids = packets[:, :, 0, half : half + 4 * C].astype(I32)
    send, extra = kernel_call(
        pick_kernel,
        [SMEM, SMEM, VMEM] + [VMEM] * 5,
        (bf16(MEMBERS, ROWS, middle_width + fine_width), bf16(MEMBERS, ROWS, fine_width)),
    )(where, ids, middle_weights, *fine_rows)
    send = kernel_call(merge_kernel, [VMEM] * 2, bf16(*send.shape))(send, shift(extra, "c", 1))
    mine = exchange(send, ("x", "z")).reshape(depth, -1)

    numbers = kernel_call(numbers_kernel, [VMEM], bf16(1, ROWS, 2 * fine_width))(
        after(packets, send)
    )
    block = after(packets, send)[:, :, :, :half].reshape(depth, half)
    one, three = shift(block, "y", 1), shift(block, "y", 3)
    middle_row = depth // 2
    halves = [
        block,
        one,
        shift(one[:middle_row], "y", 1),
        shift(three[middle_row:], "y", 3),
        three,
    ]
    length = tokens.shape[0]
    slots = kernel_call(
        coarse_kernel,
        [SMEM, SMEM] + [VMEM] * 9,
        tuple([bf16(depth, half)] * Y + [f32(length, depth)] * 2),
        [
            pltpu.VMEM((depth, half), BF16),
            pltpu.VMEM((depth, half), F32),
            pltpu.VMEM((depth, half), F32),
        ],
        cost=10_000_000,
    )(
        where, ids, tokens, cotangent, other_both[:length], other_both[length:], *halves
    )
    mine, numbers, *slots = lax.optimization_barrier([mine, numbers] + list(slots))
    slots, coarse_back, other_back = slots[:Y], slots[Y], slots[Y + 1]

    terms, back = kernel_call(
        levels_kernel,
        [VMEM] * 3,
        (bf16(depth, middle_width + fine_width), f32(length, depth)),
        cost=10_000_000,
    )(tokens, cotangent, mine)
    parts = exchange(terms.reshape(MEMBERS, ROWS, -1), ("x", "z"))

    up = shift(slots[2][:middle_row], "y", 1).astype(F32)
    down = shift(slots[2][middle_row:], "y", 3).astype(F32)
    up = (slots[1][:middle_row].astype(F32) + up).astype(BF16)
    down = (slots[3][middle_row:].astype(F32) + down).astype(BF16)
    up = shift(jnp.concatenate([up, slots[1][middle_row:]]), "y", 1).astype(F32)
    down = shift(jnp.concatenate([slots[3][:middle_row], down]), "y", 3).astype(F32)
    summed = (slots[0].astype(F32) + up + down).astype(BF16).reshape(X, Z * ROWS, half)
    column_sum = lax.dynamic_index_in_dim(summed, x_index, 0, keepdims=False).astype(F32)
    for s in range(1, X):
        leaving = lax.dynamic_index_in_dim(summed, (x_index + s) % X, 0, keepdims=False)
        column_sum = column_sum + shift(leaving, "x", s).astype(F32)
    column_sum = column_sum.astype(BF16).reshape(Z, ROWS, half)
    parts, column_sum = lax.optimization_barrier((parts, column_sum))
    coarse_four = exchange(column_sum, "z")

    middle_count = middle_weights.shape[0]
    pairs = MEMBERS // 2
    side = middle_count // C
    share = side // Y
    keep, leave = kernel_call(
        collect_kernel,
        [SMEM, SMEM, VMEM],
        (f32(side, ROWS, middle_width), bf16(side + pairs, ROWS, middle_width)),
        [pltpu.VMEM((middle_count, ROWS, middle_width), F32)],
    )(where, ids, parts)
    arrived = shift(leave, "c", 1)
    first, s0, s1, s3 = kernel_call(
        combine_kernel,
        [SMEM] + [VMEM] * 4,
        tuple([bf16(2 * pairs + 1 + share, ROWS, middle_width)] + [f32(share, ROWS, middle_width)] * 3),
    )(where, keep, leave, arrived, numbers)
    r1, r3 = shift(first, "y", 1), shift(first, "y", 3)
    second = kernel_call(
        relay_kernel,
        [VMEM] * 4,
        (
            bf16(pairs + 1 + share, ROWS, middle_width),
            bf16(pairs + share, ROWS, middle_width),
        ),
    )(r1, r3, s1, s3)
    q1, q3 = shift(second[0], "y", 1), shift(second[1], "y", 3)
    fine_ids = [f[2 * pairs, :Z, : 4 * C * X].astype(I32) for f in (first, r1, r3)]
    fine_sums = kernel_call(
        first_fine_kernel,
        [SMEM, SMEM] + [VMEM] * 3,
        f32(fine_owned + 8, ROWS, fine_width),
    )(where, jnp.stack(fine_ids), first, r1, r3)
    fine_sums, q1, q3 = lax.optimization_barrier((fine_sums, q1, q3))
    other_back = shift(after(other_back, second[0]), "c", 1)
    tokens_grad = (coarse_back + other_back + back).astype(BF16)
    middle_done = s0 + q1[pairs + 1 :].astype(F32) + q3[pairs:].astype(F32)
    coarse_four, middle_done = lax.optimization_barrier((coarse_four, middle_done))
    coarse_done = jnp.sum(coarse_four, axis=0, dtype=F32).astype(BF16)
    done = jnp.concatenate([middle_done.astype(BF16), coarse_done[None]], axis=0)
    total = gather(done, ("y", "c")).reshape((Y * C,) + done.shape)
    coarse_total, middle_total = kernel_call(
        spread_kernel, [VMEM], (bf16(*coarse_weights.shape), bf16(*middle_weights.shape))
    )(total)
    fine_total = kernel_call(
        last_fine_kernel,
        [SMEM, SMEM] + [VMEM] * 3,
        bf16(fine_owned, ROWS, fine_width),
        [pltpu.VMEM((fine_owned + 8, ROWS, fine_width), F32)],
    )(where, q1[pairs, :Z, : 4 * C * X].astype(I32)[None], fine_sums, q1, q3)
    return (tokens_grad, coarse_total, middle_total, fine_total)


def solution(mesh):
    fine_mesh = Mesh(mesh.devices.reshape(Y, C, X, Z), EVERYONE)
    members = ("x", "z")
    return jax.shard_map(
        on_device,
        mesh=fine_mesh,
        in_specs=(
            P(EVERYONE, None),
            P(EVERYONE, None),
            P(EVERYONE, None),
            P(None, members, None),
            P(None, members, None),
            P(("y", "c"), members, None),
        ),
        out_specs=(
            P(EVERYONE, None),
            P(None, members, None),
            P(None, members, None),
            P(("y", "c"), members, None),
        ),
        check_vma=False,
    )
```

time: 282 us -> 258 us (0.915)
  waiting for transfers between devices: 91 us -> 73.2 us
  local copies, waits for them, and re-layouts: 12.8 us -> 6.57 us
    ppermute x26 -> x24, waiting for transfers between devices: 86.6 us -> 53.3 us  [shift(): lax.ppermute(array, axis, [(i, (i + step) % count) for i in range(count)])]
    all_to_all x6, waiting for transfers between devices: 4.41 us -> 20 us  [exchange(): return lax.all_to_all(array, axes, split_axis=0, concat_axis=0, tiled=True)]
    ppermute x26 -> x24, starting transfers between devices: 78 us -> 90.9 us  [shift(): lax.ppermute(array, axis, [(i, (i + step) % count) for i in range(count)])]
    all_to_all x6, starting transfers between devices: 64.2 us -> 51.4 us  [exchange(): return lax.all_to_all(array, axes, split_axis=0, concat_axis=0, tiled=True)]
    unnamed x29 -> x32, local copies, waits for them, and re-layouts: 6.24 us -> 3.16 us
    pallas_call x5 -> x10, Pallas kernels: 23.7 us -> 22.7 us  [the longest x1 5.2 us: on_device(): kernel_call(first_fine_kernel, [SMEM, SMEM] + [VMEM] * 3, f32(fine_owned...]
  transfers between devices with their start and end apart: 32 -> 30, of which waited for: 12 -> 19; matrix products, arithmetic and copies ran while one was open for 3% -> 4% of each run, Pallas kernels for 7% -> 5%
where the time goes in v4:
time: 258 us; the launch traced here: 256 us
  starting transfers between devices  142 us (55%)
  waiting for transfers between devices  73.2 us (28%)
  Pallas kernels  25.5 us (10%)
  other arithmetic  7.11 us (3%)
  local copies, waits for them, and re-layouts  6.57 us (3%)
    ppermute x24, starting transfers between devices, shift(): lax.ppermute(array, axis, [(i, (i + step) % count) for i in range(count)])  90.9 us
    ppermute x24, waiting for transfers between devices, shift(): lax.ppermute(array, axis, [(i, (i + step) % count) for i in range(count)])  53.3 us
    all_to_all x6, starting transfers between devices, exchange(): return lax.all_to_all(array, axes, split_axis=0, concat_axis=0, tiled=True)  51.4 us
    all_to_all x6, waiting for transfers between devices, exchange(): return lax.all_to_all(array, axes, split_axis=0, concat_axis=0, tiled=True)  20 us
    pallas_call x1, Pallas kernels, on_device(): kernel_call(first_fine_kernel, [SMEM, SMEM] + [VMEM] * 3, f32(fine_owned...  5.2 us
  transfers between devices with their start and end apart: 30, of which 19 were waited for; matrix products, arithmetic and copies ran while one was open for 4% of the time, Pallas kernels for 5%

profile of v4, /device:TPU:1, one launch (start us, length us, event | category | flops | bytes accessed | tf_op | source)
XLA Modules:
  0.0 256.0 jit_solution(17384104956827497457)
XLA Ops:
  0.6 8.8 %collective-permute-start = (s32[1,3]{1,0:T(1,128)}, s32[1,3]{1,0:T(1,128)S(1)}, u32[]{:S(2)}, u32[]{:S(2)}) collective-permute-start(s32[1,3]{1,0:T(1,128)} %own_ref.1), channel_id=1, source_target_pairs={{0,64},{64,0},{1,65},{65,1},{2,66},{66,2},{3,67},{67,3},{4,68},{68... | collective-permute-start | bytes 44 | tf_op jit(solution)/shard_map/ppermute | solution.py:30
  13.1 9.5 %all-to-all-start = ((bf16[16,16,384]{2,1,0:T(8,128)(2,1)}), bf16[16,16,384]{2,1,0:T(8,128)(2,1)S(1)}, u32[]{:S(2)}, u32[]{:S(2)}) async-start(bf16[16,16,384]{2,1,0:T(8,128)(2,1)} %shard_map.93), calls=%async_computation | async-start | bytes 393216 | tf_op jit(solution)/shard_map/all_to_all | solution.py:20
  29.3 6.4 %all-to-all-done = bf16[16,16,384]{2,1,0:T(8,128)(2,1)S(1)} async-done(((bf16[16,16,384]{2,1,0:T(8,128)(2,1)}), bf16[16,16,384]{2,1,0:T(8,128)(2,1)S(1)}, u32[]{:S(2)}, u32[]{:S(2)}) %all-to-all-start) | async-done | bytes 196640 | tf_op jit(solution)/shard_map/all_to_all | solution.py:20
  36.7 4.2 %all-to-all-start.1 = ((bf16[4,16,16,384]{3,1,2,0:T(8,128)(2,1)}), bf16[4,16,16,384]{3,1,2,0:T(8,128)(2,1)}, u32[]{:S(2)}, u32[]{:S(2)}) async-start(bf16[4,16,16,384]{3,1,2,0:T(8,128)(2,1)} %broadcast_in_dim.6), calls=%async_computation.1 | async-start | bytes 1572864 | tf_op jit(solution)/shard_map/all_to_all | solution.py:20
  41.0 5.3 %collective-permute-start.5 = (bf16[256,1024]{1,0:T(8,128)(2,1)S(1)}, bf16[256,1024]{1,0:T(8,128)(2,1)S(1)}, u32[]{:S(2)}, u32[]{:S(2)}) collective-permute-start(bf16[256,1024]{1,0:T(8,128)(2,1)S(1)} %pad_maximum_fusion), channel_id=1, source_target_pairs={{0,64},{64,0},{1,65},{65,1},{2,66},{66,2},{3,67},{67,3},{4,68},{68... | collective-permute-start | bytes 1572872 | tf_op jit(solution)/shard_map/ppermute | solution.py:30
  53.0 4.5 %collective-permute-done.2.f2a = bf16[64,16,128]{2,1,0:T(8,128)(2,1)S(1)} collective-permute-done((bf16[64,16,128]{2,1,0:T(8,128)(2,1)S(1)}, bf16[64,16,128]{2,1,0:T(8,128)(2,1)S(1)}, u32[]{:S(2)}, u32[]{:S(2)}) %collective-permute-start.2) | collective-permute-done | bytes 262176 | tf_op jit(solution)/shard_map/ppermute | solution.py:30
  59.8 4.7 %shard_map.94 = (bf16[64,16,384]{2,1,0:T(8,128)(2,1)S(1)}, bf16[64,16,128]{2,1,0:T(8,128)(2,1)S(1)}) custom-call(s32[4]{0:T(128)S(1)} %pad_add_fusion.where_ref, s32[4,16,8]{2,1,0:T(8,128)S(1)} %fusion.3.ids_ref, bf16[64,16,256]{2,1,0:T(8,128)(2,1)S(1)} %copy-done.6, bf16[128,16,128]{2,1,0:T(8,128)(2,1)S(1)} %copy-done.7, ...), custom_call_target="tpu_custom_call" | custom-call | flops 1000000 | bytes 1000000 | tf_op jit(solution)/shard_map/pallas_call | solution.py:360
  69.7 9.7 %all-to-all-start.2 = ((bf16[64,16,384]{2,1,0:T(8,128)(2,1)}), bf16[64,16,384]{2,1,0:T(8,128)(2,1)S(1)}, u32[]{:S(2)}, u32[]{:S(2)}) async-start(bf16[64,16,384]{2,1,0:T(8,128)(2,1)} %shard_map.95), calls=%async_computation.2 | async-start | bytes 1572864 | tf_op jit(solution)/shard_map/all_to_all | solution.py:20
  87.4 9.4 %collective-permute-done.7.h1 = bf16[1024,256]{1,0:T(8,128)(2,1)S(1)} collective-permute-done((bf16[1024,256]{1,0:T(8,128)(2,1)S(1)}, bf16[1024,256]{1,0:T(8,128)(2,1)S(1)}, u32[]{:S(2)}, u32[]{:S(2)}) %collective-permute-start.7) | collective-permute-done | bytes 524320 | tf_op jit(solution)/shard_map/ppermute | solution.py:30
  98.9 4.5 %collective-permute-start.10 = (bf16[512,256]{1,0:T(8,128)(2,1)S(1)}, bf16[512,256]{1,0:T(8,128)(2,1)S(1)}, u32[]{:S(2)}, u32[]{:S(2)}) collective-permute-start(bf16[512,256]{1,0:T(8,128)(2,1)S(1)} %slice.85), channel_id=1, source_target_pairs={{0,384},{128,0},{256,128},{384,256},{1,385},{129,1},{257,129},{385... | collective-permute-start | bytes 786440 | tf_op jit(solution)/shard_map/ppermute | solution.py:30
  112.2 7.4 %all-to-all-done.2 = bf16[64,16,384]{2,1,0:T(8,128)(2,1)S(1)} async-done(((bf16[64,16,384]{2,1,0:T(8,128)(2,1)}), bf16[64,16,384]{2,1,0:T(8,128)(2,1)S(1)}, u32[]{:S(2)}, u32[]{:S(2)}) %all-to-all-start.2) | async-done | bytes 786464 | tf_op jit(solution)/shard_map/all_to_all | solution.py:20
  121.4 9.1 %all-to-all-start.3 = ((bf16[64,16,384]{2,1,0:T(8,128)(2,1)}), bf16[64,16,384]{2,1,0:T(8,128)(2,1)S(1)}, u32[]{:S(2)}, u32[]{:S(2)}) async-start(bf16[64,16,384]{2,1,0:T(8,128)(2,1)} %bitcast.8), calls=%async_computation.3 | async-start | bytes 1572864 | tf_op jit(solution)/shard_map/all_to_all | solution.py:20
  130.6 4.6 %collective-permute-start.13 = (bf16[512,256]{1,0:T(8,128)(2,1)S(1)}, bf16[512,256]{1,0:T(8,128)(2,1)S(1)}, u32[]{:S(2)}, u32[]{:S(2)}) collective-permute-start(bf16[512,256]{1,0:T(8,128)(2,1)S(1)} %get-tuple-element.98), channel_id=1, source_target_pairs={{0,384},{128,0},{256,128},{384,256},{1,385},{129,1},{257,129},{385... | collective-permute-start | bytes 786440 | tf_op jit(solution)/shard_map/ppermute | solution.py:30
  140.1 5.4 %collective-permute-start.14 = (bf16[1024,256]{1,0:T(8,128)(2,1)}, bf16[1024,256]{1,0:T(8,128)(2,1)S(1)}, u32[]{:S(2)}, u32[]{:S(2)}) collective-permute-start(bf16[1024,256]{1,0:T(8,128)(2,1)} %pad_maximum_fusion.2), channel_id=1, source_target_pairs={{0,384},{128,0},{256,128},{384,256},{1,385},{129,1},{257,129},{385... | collective-permute-start | bytes 1572872 | tf_op jit(solution)/shard_map/ppermute | solution.py:30
  147.6 6.9 %collective-permute-done.14 = bf16[1024,256]{1,0:T(8,128)(2,1)S(1)} collective-permute-done((bf16[1024,256]{1,0:T(8,128)(2,1)}, bf16[1024,256]{1,0:T(8,128)(2,1)S(1)}, u32[]{:S(2)}, u32[]{:S(2)}) %collective-permute-start.14) | collective-permute-done | bytes 524320 | tf_op jit(solution)/shard_map/ppermute | solution.py:30
  154.5 4.9 %collective-permute-done.12 = bf16[1024,256]{1,0:T(8,128)(2,1)S(1)} collective-permute-done((bf16[1024,256]{1,0:T(8,128)(2,1)S(1)}, bf16[1024,256]{1,0:T(8,128)(2,1)S(1)}, u32[]{:S(2)}, u32[]{:S(2)}) %collective-permute-start.12) | collective-permute-done | bytes 524320 | tf_op jit(solution)/shard_map/ppermute | solution.py:30
  175.9 7.3 %collective-permute-start.18 = (bf16[64,16,256]{2,1,0:T(8,128)(2,1)S(1)}, bf16[64,16,256]{2,1,0:T(8,128)(2,1)S(1)}, u32[]{:S(2)}, u32[]{:S(2)}) collective-permute-start(bf16[64,16,256]{2,1,0:T(8,128)(2,1)S(1)} %get-tuple-element.76.leave_ref), channel_id=1, source_target_pairs={{0,64},{64,0},{1,65},{65,1},{2,66},{66,2},{3,67},{67,3},{4,68},{68... | collective-permute-start | bytes 1572872 | tf_op jit(solution)/shard_map/ppermute | solution.py:30
  187.2 4.6 %collective-permute-start.20 = (bf16[73,16,256]{2,1,0:T(8,128)(2,1)S(1)}, bf16[73,16,256]{2,1,0:T(8,128)(2,1)S(1)}, u32[]{:S(2)}, u32[]{:S(2)}) collective-permute-start(bf16[73,16,256]{2,1,0:T(8,128)(2,1)S(1)} %get-tuple-element.78.p0), channel_id=1, source_target_pairs={{0,384},{128,0},{256,128},{384,256},{1,385},{129,1},{257,129},{385... | collective-permute-start | bytes 1794056 | tf_op jit(solution)/shard_map/ppermute | solution.py:30
  191.8 11.3 %collective-permute-done.19.r1.p1 = bf16[73,16,256]{2,1,0:T(8,128)(2,1)S(1)} collective-permute-done((bf16[73,16,256]{2,1,0:T(8,128)(2,1)S(1)}, bf16[73,16,256]{2,1,0:T(8,128)(2,1)S(1)}, u32[]{:S(2)}, u32[]{:S(2)}) %collective-permute-start.19) | collective-permute-done | bytes 598048 | tf_op jit(solution)/shard_map/ppermute | solution.py:30
  206.8 5.3 %collective-permute-start.23 = (bf16[40,16,256]{2,1,0:T(8,128)(2,1)}, bf16[40,16,256]{2,1,0:T(8,128)(2,1)}, u32[]{:S(2)}, u32[]{:S(2)}) collective-permute-start(bf16[40,16,256]{2,1,0:T(8,128)(2,1)} %get-tuple-element.86), channel_id=1, source_target_pairs={{0,384},{128,0},{256,128},{384,256},{1,385},{129,1},{257,129},{385... | collective-permute-start | bytes 983048 | tf_op jit(solution)/shard_map/ppermute | solution.py:30
  212.1 11.4 %all-to-all-start.4 = ((bf16[16,16,256]{2,1,0:T(8,128)(2,1)}), bf16[16,16,256]{2,1,0:T(8,128)(2,1)}, u32[]{:S(2)}, u32[]{:S(2)}) async-start(bf16[16,16,256]{2,1,0:T(8,128)(2,1)} %bitcast.14), calls=%async_computation.4 | async-start | bytes 262144 | tf_op jit(solution)/shard_map/all_to_all | solution.py:20
  227.6 5.2 %shard_map.102.before_ref = f32[136,16,128]{2,1,0:T(8,128)S(1)} custom-call(s32[4]{0:T(128)S(1)} %pad_add_fusion.where_ref, s32[3,16,32]{2,1,0:T(8,128)S(1)} %maximum_convert_fusion.ids_ref, bf16[73,16,256]{2,1,0:T(8,128)(2,1)S(1)} %get-tuple-element.78.p0, bf16[73,16,256]{2,1,0:T(8,128)(2,1)S(1)} %collective-permute-done.19.r1.p1, ...), custom_call_target="tpu_custom_call" | custom-call | flops 1000000 | bytes 1000000 | tf_op jit(solution)/shard_map/pallas_call | solution.py:448
  237.4 7.5 %all-to-all-start.5 = ((bf16[8,9,16,256]{3,2,1,0:T(8,128)(2,1)}), bf16[8,9,16,256]{3,2,1,0:T(8,128)(2,1)S(1)}, u32[]{:S(2)}, u32[]{:S(2)}) async-start(bf16[8,9,16,256]{3,2,1,0:T(8,128)(2,1)} %broadcast_in_dim.8), calls=%async_computation.5 | async-start | bytes 1179648 | tf_op jit(solution)/shard_map/all_to_all | solution.py:20
  250.8 4.3 %all-to-all-done.5.total_ref = bf16[8,9,16,256]{3,2,1,0:T(8,128)(2,1)S(1)} async-done(((bf16[8,9,16,256]{3,2,1,0:T(8,128)(2,1)}), bf16[8,9,16,256]{3,2,1,0:T(8,128)(2,1)S(1)}, u32[]{:S(2)}, u32[]{:S(2)}) %all-to-all-start.5) | async-done | bytes 589856 | tf_op jit(solution)/shard_map/all_to_all | solution.py:20
  (112 shorter events, 92.4 us)
Async XLA Ops:
  0.6 9.7 %collective-permute-start = (s32[1,3]{1,0:T(1,128)}, s32[1,3]{1,0:T(1,128)S(1)}, u32[]{:S(2)}, u32[]{:S(2)}) collective-permute-start(s32[1,3]{1,0:T(1,128)} %own_ref.1), channel_id=1, source_target_pairs={{0,64},{64,0},{1,65},{65,1},{2,66},{66,2},{3,67},{67,3},{4,68},{68... | collective-permute-start | bytes 44 | tf_op jit(solution)/shard_map/ppermute | solution.py:30
  13.1 22.5 %all-to-all-start = ((bf16[16,16,384]{2,1,0:T(8,128)(2,1)}), bf16[16,16,384]{2,1,0:T(8,128)(2,1)S(1)}, u32[]{:S(2)}, u32[]{:S(2)}) async-start(bf16[16,16,384]{2,1,0:T(8,128)(2,1)} %shard_map.93), calls=%async_computation | async-start | bytes 393216 | tf_op jit(solution)/shard_map/all_to_all | solution.py:20
  22.7 23.7 %collective-permute-start.1 = (bf16[128,16,128]{2,1,0:T(8,128)(2,1)}, bf16[128,16,128]{2,1,0:T(8,128)(2,1)S(1)}, u32[]{:S(2)}, u32[]{:S(2)}) collective-permute-start(bf16[128,16,128]{2,1,0:T(8,128)(2,1)} %f0), channel_id=1, source_target_pairs={{0,128},{128,256},{256,384},{384,0},{1,129},{129,257},{257,385},{3... | collective-permute-start | bytes 1572872 | tf_op jit(solution)/shard_map/ppermute | solution.py:30
  25.9 23.7 %collective-permute-start.3 = (bf16[128,16,128]{2,1,0:T(8,128)(2,1)}, bf16[128,16,128]{2,1,0:T(8,128)(2,1)S(1)}, u32[]{:S(2)}, u32[]{:S(2)}) collective-permute-start(bf16[128,16,128]{2,1,0:T(8,128)(2,1)} %f0), channel_id=1, source_target_pairs={{0,384},{128,0},{256,128},{384,256},{1,385},{129,1},{257,129},{385... | collective-permute-start | bytes 1572872 | tf_op jit(solution)/shard_map/ppermute | solution.py:30
  36.7 22.4 %all-to-all-start.1 = ((bf16[4,16,16,384]{3,1,2,0:T(8,128)(2,1)}), bf16[4,16,16,384]{3,1,2,0:T(8,128)(2,1)}, u32[]{:S(2)}, u32[]{:S(2)}) async-start(bf16[4,16,16,384]{3,1,2,0:T(8,128)(2,1)} %broadcast_in_dim.6), calls=%async_computation.1 | async-start | bytes 1572864 | tf_op jit(solution)/shard_map/all_to_all | solution.py:20
  41.0 12.0 %collective-permute-start.5 = (bf16[256,1024]{1,0:T(8,128)(2,1)S(1)}, bf16[256,1024]{1,0:T(8,128)(2,1)S(1)}, u32[]{:S(2)}, u32[]{:S(2)}) collective-permute-start(bf16[256,1024]{1,0:T(8,128)(2,1)S(1)} %pad_maximum_fusion), channel_id=1, source_target_pairs={{0,64},{64,0},{1,65},{65,1},{2,66},{66,2},{3,67},{67,3},{4,68},{68... | collective-permute-start | bytes 1572872 | tf_op jit(solution)/shard_map/ppermute | solution.py:30
  46.4 11.2 %collective-permute-start.2 = (bf16[64,16,128]{2,1,0:T(8,128)(2,1)S(1)}, bf16[64,16,128]{2,1,0:T(8,128)(2,1)S(1)}, u32[]{:S(2)}, u32[]{:S(2)}) collective-permute-start(bf16[64,16,128]{2,1,0:T(8,128)(2,1)S(1)} %slice.81), channel_id=1, source_target_pairs={{0,128},{128,256},{256,384},{384,0},{1,129},{129,257},{257,385},{3... | collective-permute-start | bytes 786440 | tf_op jit(solution)/shard_map/ppermute | solution.py:30
  49.6 9.5 %collective-permute-start.4 = (bf16[64,16,128]{2,1,0:T(8,128)(2,1)S(1)}, bf16[64,16,128]{2,1,0:T(8,128)(2,1)S(1)}, u32[]{:S(2)}, u32[]{:S(2)}) collective-permute-start(bf16[64,16,128]{2,1,0:T(8,128)(2,1)S(1)} %slice.82), channel_id=1, source_target_pairs={{0,384},{128,0},{256,128},{384,256},{1,385},{129,1},{257,129},{385... | collective-permute-start | bytes 786440 | tf_op jit(solution)/shard_map/ppermute | solution.py:30
  69.7 49.9 %all-to-all-start.2 = ((bf16[64,16,384]{2,1,0:T(8,128)(2,1)}), bf16[64,16,384]{2,1,0:T(8,128)(2,1)S(1)}, u32[]{:S(2)}, u32[]{:S(2)}) async-start(bf16[64,16,384]{2,1,0:T(8,128)(2,1)} %shard_map.95), calls=%async_computation.2 | async-start | bytes 1572864 | tf_op jit(solution)/shard_map/all_to_all | solution.py:20
  80.8 16.1 %collective-permute-start.7 = (bf16[1024,256]{1,0:T(8,128)(2,1)S(1)}, bf16[1024,256]{1,0:T(8,128)(2,1)S(1)}, u32[]{:S(2)}, u32[]{:S(2)}) collective-permute-start(bf16[1024,256]{1,0:T(8,128)(2,1)S(1)} %bitcast.27), channel_id=1, source_target_pairs={{0,128},{128,256},{256,384},{384,0},{1,129},{129,257},{257,385},{3... | collective-permute-start | bytes 1572872 | tf_op jit(solution)/shard_map/ppermute | solution.py:30
  84.1 14.7 %collective-permute-start.9 = (bf16[1024,256]{1,0:T(8,128)(2,1)S(1)}, bf16[1024,256]{1,0:T(8,128)(2,1)S(1)}, u32[]{:S(2)}, u32[]{:S(2)}) collective-permute-start(bf16[1024,256]{1,0:T(8,128)(2,1)S(1)} %bitcast.28), channel_id=1, source_target_pairs={{0,384},{128,0},{256,128},{384,256},{1,385},{129,1},{257,129},{385... | collective-permute-start | bytes 1572872 | tf_op jit(solution)/shard_map/ppermute | solution.py:30
  96.8 9.4 %collective-permute-start.8 = (bf16[512,256]{1,0:T(8,128)(2,1)S(1)}, bf16[512,256]{1,0:T(8,128)(2,1)S(1)}, u32[]{:S(2)}, u32[]{:S(2)}) collective-permute-start(bf16[512,256]{1,0:T(8,128)(2,1)S(1)} %slice.84), channel_id=1, source_target_pairs={{0,128},{128,256},{256,384},{384,0},{1,129},{129,257},{257,385},{3... | collective-permute-start | bytes 786440 | tf_op jit(solution)/shard_map/ppermute | solution.py:30
  121.4 52.2 %all-to-all-start.3 = ((bf16[64,16,384]{2,1,0:T(8,128)(2,1)}), bf16[64,16,384]{2,1,0:T(8,128)(2,1)S(1)}, u32[]{:S(2)}, u32[]{:S(2)}) async-start(bf16[64,16,384]{2,1,0:T(8,128)(2,1)} %bitcast.8), calls=%async_computation.3 | async-start | bytes 1572864 | tf_op jit(solution)/shard_map/all_to_all | solution.py:20
  135.3 10.2 %collective-permute-start.11 = (bf16[512,256]{1,0:T(8,128)(2,1)S(1)}, bf16[512,256]{1,0:T(8,128)(2,1)S(1)}, u32[]{:S(2)}, u32[]{:S(2)}) collective-permute-start(bf16[512,256]{1,0:T(8,128)(2,1)S(1)} %get-tuple-element.97), channel_id=1, source_target_pairs={{0,128},{128,256},{256,384},{384,0},{1,129},{129,257},{257,385},{3... | collective-permute-start | bytes 786440 | tf_op jit(solution)/shard_map/ppermute | solution.py:30
  140.1 14.4 %collective-permute-start.14 = (bf16[1024,256]{1,0:T(8,128)(2,1)}, bf16[1024,256]{1,0:T(8,128)(2,1)S(1)}, u32[]{:S(2)}, u32[]{:S(2)}) collective-permute-start(bf16[1024,256]{1,0:T(8,128)(2,1)} %pad_maximum_fusion.2), channel_id=1, source_target_pairs={{0,384},{128,0},{256,128},{384,256},{1,385},{129,1},{257,129},{385... | collective-permute-start | bytes 1572872 | tf_op jit(solution)/shard_map/ppermute | solution.py:30
  145.6 13.7 %collective-permute-start.12 = (bf16[1024,256]{1,0:T(8,128)(2,1)S(1)}, bf16[1024,256]{1,0:T(8,128)(2,1)S(1)}, u32[]{:S(2)}, u32[]{:S(2)}) collective-permute-start(bf16[1024,256]{1,0:T(8,128)(2,1)S(1)} %pad_maximum_fusion.1), channel_id=1, source_target_pairs={{0,128},{128,256},{256,384},{384,0},{1,129},{129,257},{257,385},{3... | collective-permute-start | bytes 1572872 | tf_op jit(solution)/shard_map/ppermute | solution.py:30
  175.9 8.8 %collective-permute-start.18 = (bf16[64,16,256]{2,1,0:T(8,128)(2,1)S(1)}, bf16[64,16,256]{2,1,0:T(8,128)(2,1)S(1)}, u32[]{:S(2)}, u32[]{:S(2)}) collective-permute-start(bf16[64,16,256]{2,1,0:T(8,128)(2,1)S(1)} %get-tuple-element.76.leave_ref), channel_id=1, source_target_pairs={{0,64},{64,0},{1,65},{65,1},{2,66},{66,2},{3,67},{67,3},{4,68},{68... | collective-permute-start | bytes 1572872 | tf_op jit(solution)/shard_map/ppermute | solution.py:30
  185.3 17.8 %collective-permute-start.19 = (bf16[73,16,256]{2,1,0:T(8,128)(2,1)S(1)}, bf16[73,16,256]{2,1,0:T(8,128)(2,1)S(1)}, u32[]{:S(2)}, u32[]{:S(2)}) collective-permute-start(bf16[73,16,256]{2,1,0:T(8,128)(2,1)S(1)} %get-tuple-element.78.p0), channel_id=1, source_target_pairs={{0,128},{128,256},{256,384},{384,0},{1,129},{129,257},{257,385},{3... | collective-permute-start | bytes 1794056 | tf_op jit(solution)/shard_map/ppermute | solution.py:30
  187.2 16.8 %collective-permute-start.20 = (bf16[73,16,256]{2,1,0:T(8,128)(2,1)S(1)}, bf16[73,16,256]{2,1,0:T(8,128)(2,1)S(1)}, u32[]{:S(2)}, u32[]{:S(2)}) collective-permute-start(bf16[73,16,256]{2,1,0:T(8,128)(2,1)S(1)} %get-tuple-element.78.p0), channel_id=1, source_target_pairs={{0,384},{128,0},{256,128},{384,256},{1,385},{129,1},{257,129},{385... | collective-permute-start | bytes 1794056 | tf_op jit(solution)/shard_map/ppermute | solution.py:30
  204.9 27.9 %collective-permute-start.22 = (bf16[41,16,256]{2,1,0:T(8,128)(2,1)}, bf16[41,16,256]{2,1,0:T(8,128)(2,1)}, u32[]{:S(2)}, u32[]{:S(2)}) collective-permute-start(bf16[41,16,256]{2,1,0:T(8,128)(2,1)} %get-tuple-element.81), channel_id=1, source_target_pairs={{0,128},{128,256},{256,384},{384,0},{1,129},{129,257},{257,385},{3... | collective-permute-start | bytes 1007624 | tf_op jit(solution)/shard_map/ppermute | solution.py:30
  206.8 26.0 %collective-permute-start.23 = (bf16[40,16,256]{2,1,0:T(8,128)(2,1)}, bf16[40,16,256]{2,1,0:T(8,128)(2,1)}, u32[]{:S(2)}, u32[]{:S(2)}) collective-permute-start(bf16[40,16,256]{2,1,0:T(8,128)(2,1)} %get-tuple-element.86), channel_id=1, source_target_pairs={{0,384},{128,0},{256,128},{384,256},{1,385},{129,1},{257,129},{385... | collective-permute-start | bytes 983048 | tf_op jit(solution)/shard_map/ppermute | solution.py:30
  212.1 23.4 %all-to-all-start.4 = ((bf16[16,16,256]{2,1,0:T(8,128)(2,1)}), bf16[16,16,256]{2,1,0:T(8,128)(2,1)}, u32[]{:S(2)}, u32[]{:S(2)}) async-start(bf16[16,16,256]{2,1,0:T(8,128)(2,1)} %bitcast.14), calls=%async_computation.4 | async-start | bytes 262144 | tf_op jit(solution)/shard_map/all_to_all | solution.py:20
  223.5 25.5 %collective-permute-start.21 = (f32[128,1024]{1,0:T(8,128)}, f32[128,1024]{1,0:T(8,128)}, u32[]{:S(2)}, u32[]{:S(2)}) collective-permute-start(f32[128,1024]{1,0:T(8,128)} %get-tuple-element.82), channel_id=1, source_target_pairs={{0,64},{64,0},{1,65},{65,1},{2,66},{66,2},{3,67},{67,3},{4,68},{68... | collective-permute-start | bytes 1572872 | tf_op jit(solution)/shard_map/ppermute | solution.py:30
  237.4 17.7 %all-to-all-start.5 = ((bf16[8,9,16,256]{3,2,1,0:T(8,128)(2,1)}), bf16[8,9,16,256]{3,2,1,0:T(8,128)(2,1)S(1)}, u32[]{:S(2)}, u32[]{:S(2)}) async-start(bf16[8,9,16,256]{3,2,1,0:T(8,128)(2,1)} %broadcast_in_dim.8), calls=%async_computation.5 | async-start | bytes 1179648 | tf_op jit(solution)/shard_map/all_to_all | solution.py:20
  (22 other events, 193.6 us)

commit v5 on v4

--- a/solution.py
+++ b/solution.py
@@ -1,3 +1,5 @@
+from functools import partial
+
 import jax
 import jax.numpy as jnp
 from jax import lax
@@ -11,6 +13,7 @@
 Y, C, X, Z = 4, 2, 4, 16
 MEMBERS = X * Z
 ROWS = 16
+LANES = 8
 EVERYONE = ("y", "c", "x", "z")
 VMEM = pl.BlockSpec(memory_space=pltpu.VMEM)
 SMEM = pl.BlockSpec(memory_space=pltpu.SMEM)
@@ -69,7 +72,7 @@
     return (v * half).astype(BF16), (upstream * slope).astype(BF16)
 
 
-def packet_kernel(where_ref, own_ref, other_ref, coarse_ref, out_ref):
+def packet_kernel(owned, where_ref, own_ref, other_ref, coarse_ref, out_ref):
     y_index, c_index = where_ref[0], where_ref[1]
     width = coarse_ref.shape[2] // 4
     up = coarse_ref[y_index, :, pl.ds(pl.multiple_of(c_index * width, width), width)]
@@ -79,9 +82,15 @@
     lanes = lax.broadcasted_iota(I32, (ROWS, 128), 1)
     numbers = jnp.zeros((ROWS, 128), F32)
     for core, ref in ((c_index, own_ref), (1 - c_index, other_ref)):
-        values = (ref[0, 1], ref[0, 2] // 32, ref[0, 2] % 32)
+        fine_id = ref[0, 2]
+        owner, slot = fine_id // owned, fine_id % owned
+        choice = (y_index - owner // C + Y) % Y
+        choice = jnp.where(jnp.logical_and(choice == 2, slot >= owned // 2), Y, choice)
+        choice = jnp.where(owner % C == c_index, choice, Y + 1)
+        code = choice * owned + slot
+        values = (ref[0, 1], fine_id // 32, fine_id % 32, code // 32, code % 32)
         for i, value in enumerate(values):
-            numbers = jnp.where(lanes == 4 * core + i, value.astype(F32), numbers)
+            numbers = jnp.where(lanes == LANES * core + i, value.astype(F32), numbers)
     numbers = numbers.astype(BF16)
     for z in range(Z):
         out_ref[z, :, :width] = up
@@ -97,44 +106,50 @@
         line = jnp.zeros((ROWS, 128), F32)
         for z in range(Z):
             line = jnp.where(rows == z, grid_ref[x, z, :, width:].astype(F32), line)
-        total = total + (pltpu.roll(line, 8 * x, 1) if x else line)
+        total = total + (pltpu.roll(line, LANES * C * x, 1) if x else line)
     out_ref[0, :, :128] = total.astype(BF16)
     out_ref[0, :, 128:] = jnp.zeros((ROWS, 128), BF16)
 
 
-def pick_kernel(
-    where_ref, ids_ref, middle_ref, f0, f1, f2a, f2b, f3, out_ref, other_ref
-):
-    y_index, c_index = where_ref[0], where_ref[1]
-    owned = f0.shape[0]
-    split = f2a.shape[0]
+def chosen(code, pieces):
+    owned = pieces[0].shape[0]
+    choice, local = code // owned, code % owned
+    rows = jnp.zeros(pieces[0].shape[1:], BF16)
+    for s, piece in enumerate(pieces):
+        at = local if piece.shape[0] == owned else local % piece.shape[0]
+        rows = jnp.where(choice == s, piece[at], rows)
+    return rows
+
+
+def code_of(ids_ref, x, z, core):
+    return ids_ref[x, z, LANES * core + 3] * 32 + ids_ref[x, z, LANES * core + 4]
+
+
+def pick_other_kernel(where_ref, ids_ref, f0, f1, f2a, f3, f2b, out_ref):
+    core = 1 - where_ref[1]
+
+    def step(z, carry):
+        for x in range(X):
+            code = code_of(ids_ref, x, z, core)
+            out_ref[x * Z + z] = chosen(code, (f0, f1, f2a, f3, f2b))
+        return carry
+
+    lax.fori_loop(0, Z, step, 0, unroll=4)
+
+
+def pick_own_kernel(where_ref, ids_ref, middle_ref, f0, f1, f2a, f3, f2b, out_ref):
+    core = where_ref[1]
     middle_width = middle_ref.shape[2]
-    zeros = jnp.zeros(f0.shape[1:], BF16)
 
     def step(z, carry):
-        for core in range(C):
-            for x in range(X):
-                place = 4 * ((core + c_index) % C)
-                fine_id = ids_ref[x, z, place + 1] * 32 + ids_ref[x, z, place + 2]
-                owner = fine_id // owned
-                choice = (y_index - owner // C + Y) % Y
-                slot = fine_id % owned
-                choice = jnp.where(owner % C == c_index, choice, Y + 1)
-                choice = jnp.where(jnp.logical_and(choice == 2, slot >= split), Y, choice)
-                rows = zeros
-                for s, piece in enumerate((f0, f1, f2a, f3, f2b)):
-                    here = choice == s
-                    local = slot % split if s in (2, 4) else slot
-                    rows = jnp.where(here, piece[local], rows)
-                m = x * Z + z
-                if core == 0:
-                    out_ref[m, :, :middle_width] = middle_ref[ids_ref[x, z, place]]
-                    out_ref[m, :, middle_width:] = rows
-                else:
-                    other_ref[m] = rows
+        for x in range(X):
+            m = x * Z + z
+            code = code_of(ids_ref, x, z, core)
+            out_ref[m, :, :middle_width] = middle_ref[ids_ref[x, z, LANES * core]]
+            out_ref[m, :, middle_width:] = chosen(code, (f0, f1, f2a, f3, f2b))
         return carry
 
-    lax.fori_loop(0, Z, step, 0, unroll=2)
+    lax.fori_loop(0, Z, step, 0, unroll=4)
 
 
 def merge_kernel(send_ref, extra_ref, out_ref):
@@ -149,8 +164,8 @@
 ):
     y_index = where_ref[0]
     c_index, x_index, z_index = where_ref[1], where_ref[2], where_ref[3]
-    own_id = ids_ref[x_index, z_index, 4 * c_index] // 16
-    other_id = ids_ref[x_index, z_index, 4 * (1 - c_index)] // 16
+    own_id = ids_ref[x_index, z_index, LANES * c_index] // 16
+    other_id = ids_ref[x_index, z_index, LANES * (1 - c_index)] // 16
     width = h0.shape[1] // 2
 
     def level(identity, inputs, upstream, term_ref, into_ref):
@@ -221,96 +236,113 @@
     back_ref[...] = dot(before_grad, w_ref[:, :half], 1, 1) + dot(fine_before_grad, fine, 1, 1)
 
 
-def collect_kernel(where_ref, ids_ref, parts_ref, keep_ref, leave_ref, sums_ref):
-    c_index = where_ref[1]
-    middle = keep_ref.shape[2]
-    half = keep_ref.shape[0]
-    share = half // Y
+def collect_kernel(
+    where_ref, ids_ref, numbers_ref, parts_ref, packet_ref, s0, s1, s3, sums_ref
+):
+    y_index, c_index = where_ref[0], where_ref[1]
+    middle = parts_ref.shape[2] - 128
+    slot = s0.shape[0]
+    pairs = MEMBERS // 2
     sums_ref[...] = jnp.zeros(sums_ref.shape, F32)
 
-    def step(z, carry):
+    def step(zz, carry):
         for x in range(X):
-            block = ids_ref[x, z, 4 * c_index]
-            owner = block // share
-            side = (owner + c_index) % C
-            place = side * half + (owner // C) * share + block % share
-            m = x * Z + z
-            sums_ref[place] = sums_ref[place] + parts_ref[m, :, :middle].astype(F32)
-            pair = half + (x % (X // 2)) * Z + z
-            low = (x // (X // 2)) * 128
-            leave_ref[pair, :, low : low + 128] = parts_ref[m, :, middle:]
+            for h in range(2):
+                z = 2 * zz + h
+                block = ids_ref[x, z, LANES * c_index]
+                place = ((block // slot - y_index + Y) % Y) * slot + block % slot
+                m = x * Z + z
+                sums_ref[place] = sums_ref[place] + parts_ref[m, :, :middle].astype(F32)
+                pair = x * (Z // 2) + zz
+                packet_ref[pair, :, h * 128 : h * 128 + 128] = parts_ref[m, :, middle:]
         return carry
 
-    lax.fori_loop(0, Z, step, 0, unroll=2)
-    keep_ref[...] = sums_ref[:half]
-    leave_ref[:half] = sums_ref[half:].astype(BF16)
-
-
-def combine_kernel(
-    where_ref, keep_ref, leave_ref, arrived_ref, numbers_ref, packet_ref, s0, s1, s3
-):
-    y_index = where_ref[0]
-    half = keep_ref.shape[0]
-    share = half // Y
-    pairs = MEMBERS // 2
-    packet_ref[:pairs] = leave_ref[half:]
-    packet_ref[pairs : 2 * pairs] = arrived_ref[half:]
-    packet_ref[2 * pairs] = numbers_ref[0]
-    for s, ref in ((0, s0), (1, s1), (3, s3)):
-        at = pl.ds(((y_index + s) % Y) * share, share)
-        ref[...] = keep_ref[at] + arrived_ref[at].astype(F32)
-    at = pl.ds(((y_index + 2) % Y) * share, share)
-    packet_ref[2 * pairs + 1 :] = (keep_ref[at] + arrived_ref[at].astype(F32)).astype(BF16)
+    lax.fori_loop(0, Z // 2, step, 0)
+    packet_ref[pairs] = numbers_ref[0]
+    packet_ref[pairs + 1 :] = sums_ref[2 * slot : 3 * slot].astype(BF16)
+    s0[...] = sums_ref[:slot]
+    s1[...] = sums_ref[slot : 2 * slot]
+    s3[...] = sums_ref[3 * slot :]
 
 
 def relay_kernel(r1, r3, s1, s3, up_ref, down_ref):
     pairs = MEMBERS // 2
-    share = s1.shape[0]
-    middle = 2 * pairs + 1
-    split = share // 2
-    up_ref[:pairs] = r1[:pairs]
-    up_ref[pairs] = r1[2 * pairs]
-    up_ref[pairs + 1 : pairs + 1 + split] = (
+    lower = pairs // 2
+    split = s1.shape[0] // 2
+    middle = pairs + 1
+    up_ref[:lower] = r1[:lower]
+    up_ref[lower] = r1[pairs]
+    up_ref[lower + 1 : lower + 1 + split] = (
         s1[:split] + r1[middle : middle + split].astype(F32)
     ).astype(BF16)
-    up_ref[pairs + 1 + split :] = s1[split:].astype(BF16)
-    down_ref[:pairs] = r3[pairs : 2 * pairs]
-    down_ref[pairs : pairs + split] = s3[:split].astype(BF16)
-    down_ref[pairs + split :] = (s3[split:] + r3[middle + split :].astype(F32)).astype(BF16)
-
-
-def add_fine(group, c_index, owned, ids_ref, p, core, piece, base, sums_ref):
-    def step(z, carry):
-        for x in range(X):
-            place = x * 8 + 4 * ((core + c_index) % C)
-            fine_id = ids_ref[p, z, place + 1] * 32 + ids_ref[p, z, place + 2]
-            slot = jnp.where(fine_id // owned == group, fine_id % owned, owned)
-            pair = base + (x % (X // 2)) * Z + z
-            low = (x // (X // 2)) * 128
-            part = piece[pair, :, low : low + 128]
-            sums_ref[slot] = sums_ref[slot] + part.astype(F32)
+    up_ref[lower + 1 + split :] = s1[split:].astype(BF16)
+    down_ref[:lower] = r3[lower:pairs]
+    down_ref[lower : lower + split] = s3[:split].astype(BF16)
+    down_ref[lower + split :] = (s3[split:] + r3[middle + split :].astype(F32)).astype(BF16)
+
+
+def add_fine(where_ref, owned, ids_ref, p, piece, xs, sums_ref):
+    y_index, c_index = where_ref[0], where_ref[1]
+
+    def step(zz, carry):
+        for x in xs:
+            for h in range(2):
+                place = LANES * (C * x + c_index)
+                z = 2 * zz + h
+                fine_id = ids_ref[p, z, place + 1] * 32 + ids_ref[p, z, place + 2]
+                owner = fine_id // owned
+                slot = ((owner + c_index) % C) * owned + fine_id % owned
+                slot = jnp.where(owner // C == y_index, slot, C * owned)
+                pair = (x - xs[0]) * (Z // 2) + zz
+                part = piece[pair, :, h * 128 : h * 128 + 128]
+                sums_ref[slot] = sums_ref[slot] + part.astype(F32)
         return carry
 
-    lax.fori_loop(0, Z, step, 0, unroll=4)
+    lax.fori_loop(0, Z // 2, step, 0)
 
 
 def first_fine_kernel(where_ref, ids_ref, p0, p1, p3, sums_ref):
-    group = where_ref[0] * C + where_ref[1]
-    owned = sums_ref.shape[0] - 8
+    owned = (sums_ref.shape[0] - 8) // C
     sums_ref[...] = jnp.zeros(sums_ref.shape, F32)
     for p, piece in enumerate((p0, p1, p3)):
-        for core in range(C):
-            base = core * (MEMBERS // 2)
-            add_fine(group, where_ref[1], owned, ids_ref, p, core, piece, base, sums_ref)
-
-
-def last_fine_kernel(where_ref, ids_ref, before_ref, q1, q3, out_ref, sums_ref):
-    group = where_ref[0] * C + where_ref[1]
-    owned = sums_ref.shape[0] - 8
+        add_fine(where_ref, owned, ids_ref, p, piece, range(X), sums_ref)
+
+
+def last_fine_kernel(
+    where_ref, ids_ref, before_ref, s0, q1, q3, leave_ref, middle_ref, fine_ref, sums_ref
+):
+    owned = fine_ref.shape[0]
+    share = middle_ref.shape[0]
+    lower = MEMBERS // 4
     sums_ref[...] = before_ref[...]
-    for core, piece in enumerate((q1, q3)):
-        add_fine(group, where_ref[1], owned, ids_ref, 0, core, piece, 0, sums_ref)
-    out_ref[...] = sums_ref[:owned].astype(BF16)
+    add_fine(where_ref, owned, ids_ref, 0, q1, range(X // 2), sums_ref)
+    add_fine(where_ref, owned, ids_ref, 0, q3, range(X // 2, X), sums_ref)
+    fine_ref[...] = sums_ref[:owned]
+    half = owned // 2
+    leave_ref[share:, :, :128] = sums_ref[owned : owned + half].astype(BF16)
+    leave_ref[share:, :, 128:] = sums_ref[owned + half : 2 * owned].astype(BF16)
+
+    def middle_of(side):
+        low = side * share
+        return (
+            s0[pl.ds(low, share)]
+            + q1[pl.ds(lower + 1 + low, share)].astype(F32)
+            + q3[pl.ds(lower + low, share)].astype(F32)
+        )
+
+    middle_ref[...] = middle_of(where_ref[1])
+    leave_ref[:share] = middle_of(1 - where_ref[1]).astype(BF16)
+
+
+def finish_kernel(fine_ref, arrived_ref, out_ref):
+    half = fine_ref.shape[0] // 2
+    share = arrived_ref.shape[0] - half
+    for h in range(2):
+        low = h * half
+        out_ref[low : low + half] = (
+            fine_ref[low : low + half]
+            + arrived_ref[share:, :, h * 128 : h * 128 + 128].astype(F32)
+        ).astype(BF16)
 
 
 def spread_kernel(total_ref, coarse_ref, middle_ref):
@@ -337,33 +369,40 @@
     depth = MEMBERS * ROWS
 
     other_path = shift(path, "c", 1)
-    packet = kernel_call(packet_kernel, [SMEM, SMEM, SMEM, VMEM], bf16(Z, ROWS, half + 128))(
-        where, path, other_path, coarse_weights
-    )
-    packets = gather(exchange(packet, "z"), "x").reshape(X, Z, ROWS, half + 128)
+    packet = kernel_call(
+        partial(packet_kernel, fine_owned),
+        [SMEM, SMEM, SMEM, VMEM],
+        bf16(Z, ROWS, half + 128),
+    )(where, path, other_path, coarse_weights)
+    packets = exchange(packet, "z")
 
     fine_one = shift(after(fine_weights, packet), "y", 1)
     fine_three = shift(after(fine_weights, packet), "y", 3)
+    packets, fine_one, fine_three = lax.optimization_barrier((packets, fine_one, fine_three))
+    packets = gather(packets, "x").reshape(X, Z, ROWS, half + 128)
     split = fine_owned // 2
     fine_rows = [
         fine_weights,
         fine_one,
         shift(fine_one[:split], "y", 1),
+        fine_three,
         shift(fine_three[split:], "y", 3),
-        fine_three,
     ]
-    both = jnp.concatenate([after(tokens, packet), cotangent], axis=0)
+    ids = packets[:, :, 0, half : half + LANES * C].astype(I32)
+    extra = kernel_call(
+        pick_other_kernel, [SMEM] * 2 + [VMEM] * 5, bf16(MEMBERS, ROWS, fine_width)
+    )(where, ids, *fine_rows)
+    arrived = shift(extra, "c", 1)
+    send = kernel_call(
+        pick_own_kernel,
+        [SMEM] * 2 + [VMEM] * 6,
+        bf16(MEMBERS, ROWS, middle_width + fine_width),
+    )(where, ids, middle_weights, *fine_rows)
+    send = kernel_call(merge_kernel, [VMEM] * 2, bf16(*send.shape))(send, arrived)
+    mine = exchange(send, ("x", "z")).reshape(depth, -1)
+
+    both = jnp.concatenate([after(tokens, send), cotangent], axis=0)
     other_both = shift(both, "c", 1)
-    *fine_rows, other_both = lax.optimization_barrier(fine_rows + [other_both])
-
-    ids = packets[:, :, 0, half : half + 4 * C].astype(I32)
-    send, extra = kernel_call(
-        pick_kernel,
-        [SMEM, SMEM, VMEM] + [VMEM] * 5,
-        (bf16(MEMBERS, ROWS, middle_width + fine_width), bf16(MEMBERS, ROWS, fine_width)),
-    )(where, ids, middle_weights, *fine_rows)
-    send = kernel_call(merge_kernel, [VMEM] * 2, bf16(*send.shape))(send, shift(extra, "c", 1))
-    mine = exchange(send, ("x", "z")).reshape(depth, -1)
 
     numbers = kernel_call(numbers_kernel, [VMEM], bf16(1, ROWS, 2 * fine_width))(
         after(packets, send)
@@ -416,57 +455,64 @@
         column_sum = column_sum + shift(leaving, "x", s).astype(F32)
     column_sum = column_sum.astype(BF16).reshape(Z, ROWS, half)
     parts, column_sum = lax.optimization_barrier((parts, column_sum))
-    coarse_four = exchange(column_sum, "z")
 
     middle_count = middle_weights.shape[0]
     pairs = MEMBERS // 2
-    side = middle_count // C
-    share = side // Y
-    keep, leave = kernel_call(
+    lower = pairs // 2
+    quarter_count = middle_count // Y
+    share = quarter_count // C
+    first, s0, s1, s3 = kernel_call(
         collect_kernel,
-        [SMEM, SMEM, VMEM],
-        (f32(side, ROWS, middle_width), bf16(side + pairs, ROWS, middle_width)),
+        [SMEM, SMEM, VMEM, VMEM],
+        tuple(
+            [bf16(pairs + 1 + quarter_count, ROWS, middle_width)]
+            + [f32(quarter_count, ROWS, middle_width)] * 3
+        ),
         [pltpu.VMEM((middle_count, ROWS, middle_width), F32)],
-    )(where, ids, parts)
-    arrived = shift(leave, "c", 1)
-    first, s0, s1, s3 = kernel_call(
-        combine_kernel,
-        [SMEM] + [VMEM] * 4,
-        tuple([bf16(2 * pairs + 1 + share, ROWS, middle_width)] + [f32(share, ROWS, middle_width)] * 3),
-    )(where, keep, leave, arrived, numbers)
+    )(where, ids, numbers, parts)
     r1, r3 = shift(first, "y", 1), shift(first, "y", 3)
+    coarse_four = exchange(after(column_sum, first), "z")
     second = kernel_call(
         relay_kernel,
         [VMEM] * 4,
         (
-            bf16(pairs + 1 + share, ROWS, middle_width),
-            bf16(pairs + share, ROWS, middle_width),
+            bf16(lower + 1 + quarter_count, ROWS, middle_width),
+            bf16(lower + quarter_count, ROWS, middle_width),
         ),
     )(r1, r3, s1, s3)
     q1, q3 = shift(second[0], "y", 1), shift(second[1], "y", 3)
-    fine_ids = [f[2 * pairs, :Z, : 4 * C * X].astype(I32) for f in (first, r1, r3)]
+    fine_ids = [f[pairs, :Z, : LANES * C * X].astype(I32) for f in (first, r1, r3)]
     fine_sums = kernel_call(
         first_fine_kernel,
         [SMEM, SMEM] + [VMEM] * 3,
-        f32(fine_owned + 8, ROWS, fine_width),
+        f32(C * fine_owned + 8, ROWS, fine_width),
     )(where, jnp.stack(fine_ids), first, r1, r3)
-    fine_sums, q1, q3 = lax.optimization_barrier((fine_sums, q1, q3))
-    other_back = shift(after(other_back, second[0]), "c", 1)
-    tokens_grad = (coarse_back + other_back + back).astype(BF16)
-    middle_done = s0 + q1[pairs + 1 :].astype(F32) + q3[pairs:].astype(F32)
-    coarse_four, middle_done = lax.optimization_barrier((coarse_four, middle_done))
+    fine_sums, q1, q3, coarse_four = lax.optimization_barrier(
+        (fine_sums, q1, q3, coarse_four)
+    )
+    leave, middle_done, fine_kept = kernel_call(
+        last_fine_kernel,
+        [SMEM, SMEM] + [VMEM] * 4,
+        (
+            bf16(share + fine_owned // 2, ROWS, middle_width),
+            f32(share, ROWS, middle_width),
+            f32(fine_owned, ROWS, fine_width),
+        ),
+        [pltpu.VMEM((C * fine_owned + 8, ROWS, fine_width), F32)],
+    )(where, q1[lower, :Z, : LANES * C * X].astype(I32)[None], fine_sums, s0, q1, q3)
+    arrived = shift(leave, "c", 1)
     coarse_done = jnp.sum(coarse_four, axis=0, dtype=F32).astype(BF16)
-    done = jnp.concatenate([middle_done.astype(BF16), coarse_done[None]], axis=0)
+    middle_done = (middle_done + arrived[:share].astype(F32)).astype(BF16)
+    done = jnp.concatenate([middle_done, coarse_done[None]], axis=0)
     total = gather(done, ("y", "c")).reshape((Y * C,) + done.shape)
     coarse_total, middle_total = kernel_call(
         spread_kernel, [VMEM], (bf16(*coarse_weights.shape), bf16(*middle_weights.shape))
     )(total)
     fine_total = kernel_call(
-        last_fine_kernel,
-        [SMEM, SMEM] + [VMEM] * 3,
-        bf16(fine_owned, ROWS, fine_width),
-        [pltpu.VMEM((fine_owned + 8, ROWS, fine_width), F32)],
-    )(where, q1[pairs, :Z, : 4 * C * X].astype(I32)[None], fine_sums, q1, q3)
+        finish_kernel, [VMEM] * 2, bf16(fine_owned, ROWS, fine_width)
+    )(fine_kept, arrived)
+    other_back = shift(after(other_back, second[0]), "c", 1)
+    tokens_grad = (coarse_back + other_back + back).astype(BF16)
     return (tokens_grad, coarse_total, middle_total, fine_total)
 
 

time: 258 us -> 249 us (0.965)
  waiting for transfers between devices: 73.2 us -> 63.7 us
  local copies, waits for them, and re-layouts: 6.57 us -> 10.9 us
    ppermute x24, waiting for transfers between devices: 53.3 us -> 45.2 us  [shift(): lax.ppermute(array, axis, [(i, (i + step) % count) for i in range(count)])]
    unnamed x32, local copies, waits for them, and re-layouts: 3.16 us -> 7.18 us
    ppermute x24, starting transfers between devices: 90.9 us -> 88.3 us  [shift(): lax.ppermute(array, axis, [(i, (i + step) % count) for i in range(count)])]
    pallas_call x8 -> x9, Pallas kernels: 19.3 us -> 18.2 us  [the longest x1 4.6 us: on_device(): kernel_call(first_fine_kernel, [SMEM, SMEM] + [VMEM] * 3, f32(C * fine_ow...]
  transfers between devices with their start and end apart: 30 -> 30, of which waited for: 19 -> 15; matrix products, arithmetic and copies ran while one was open for 4% -> 4% of each run, Pallas kernels for 5% -> 5%
where the time goes in v5:
time: 249 us; the launch traced here: 247 us
  starting transfers between devices  142 us (57%)
  waiting for transfers between devices  63.7 us (26%)
  Pallas kernels  23.6 us (9%)
  local copies, waits for them, and re-layouts  10.9 us (4%)
  other arithmetic  5.98 us (2%)
    ppermute x24, starting transfers between devices, shift(): lax.ppermute(array, axis, [(i, (i + step) % count) for i in range(count)])  88.3 us
    all_to_all x6, starting transfers between devices, exchange(): return lax.all_to_all(array, axes, split_axis=0, concat_axis=0, tiled=True)  53.5 us
    ppermute x24, waiting for transfers between devices, shift(): lax.ppermute(array, axis, [(i, (i + step) % count) for i in range(count)])  45.2 us
    all_to_all x6, waiting for transfers between devices, exchange(): return lax.all_to_all(array, axes, split_axis=0, concat_axis=0, tiled=True)  18.4 us
    unnamed x32, local copies, waits for them, and re-layouts  7.18 us
  transfers between devices with their start and end apart: 30, of which 15 were waited for; matrix products, arithmetic and copies ran while one was open for 4% of the time, Pallas kernels for 5%

profile of v5, /device:TPU:1, one launch (start us, length us, event | category | flops | bytes accessed | tf_op | source)
XLA Modules:
  0.0 247.2 jit_solution(18082009205608770520)
XLA Ops:
  0.6 8.8 %collective-permute-start = (s32[1,3]{1,0:T(1,128)}, s32[1,3]{1,0:T(1,128)S(1)}, u32[]{:S(2)}, u32[]{:S(2)}) collective-permute-start(s32[1,3]{1,0:T(1,128)} %own_ref.1), channel_id=1, source_target_pairs={{0,64},{64,0},{1,65},{65,1},{2,66},{66,2},{3,67},{67,3},{4,68},{68... | collective-permute-start | bytes 44 | tf_op jit(solution)/shard_map/ppermute | solution.py:33
  13.2 9.7 %all-to-all-start = ((bf16[16,16,384]{2,1,0:T(8,128)(2,1)}), bf16[16,16,384]{2,1,0:T(8,128)(2,1)S(1)}, u32[]{:S(2)}, u32[]{:S(2)}) async-start(bf16[16,16,384]{2,1,0:T(8,128)(2,1)} %shard_map.93), calls=%async_computation | async-start | bytes 393216 | tf_op jit(solution)/shard_map/all_to_all | solution.py:23
  26.1 3.4 %collective-permute-start.2 = (bf16[128,16,128]{2,1,0:T(8,128)(2,1)}, bf16[128,16,128]{2,1,0:T(8,128)(2,1)S(1)}, u32[]{:S(2)}, u32[]{:S(2)}) collective-permute-start(bf16[128,16,128]{2,1,0:T(8,128)(2,1)} %f0.3), channel_id=1, source_target_pairs={{0,384},{128,0},{256,128},{384,256},{1,385},{129,1},{257,129},{385... | collective-permute-start | bytes 1572872 | tf_op jit(solution)/shard_map/ppermute | solution.py:33
  29.4 9.8 %collective-permute-done.1.f1 = bf16[128,16,128]{2,1,0:T(8,128)(2,1)S(1)} collective-permute-done((bf16[128,16,128]{2,1,0:T(8,128)(2,1)}, bf16[128,16,128]{2,1,0:T(8,128)(2,1)S(1)}, u32[]{:S(2)}, u32[]{:S(2)}) %collective-permute-start.1) | collective-permute-done | bytes 524320 | tf_op jit(solution)/shard_map/ppermute | solution.py:33
  41.8 4.1 %all-to-all-start.1 = ((bf16[4,16,16,384]{3,1,2,0:T(8,128)(2,1)}), bf16[4,16,16,384]{3,1,2,0:T(8,128)(2,1)S(1)}, u32[]{:S(2)}, u32[]{:S(2)}) async-start(bf16[4,16,16,384]{3,1,2,0:T(8,128)(2,1)} %broadcast_in_dim.6), calls=%async_computation.1 | async-start | bytes 1572864 | tf_op jit(solution)/shard_map/all_to_all | solution.py:23
  60.3 5.1 %collective-permute-start.5 = (bf16[64,16,128]{2,1,0:T(8,128)(2,1)S(1)}, bf16[64,16,128]{2,1,0:T(8,128)(2,1)S(1)}, u32[]{:S(2)}, u32[]{:S(2)}) collective-permute-start(bf16[64,16,128]{2,1,0:T(8,128)(2,1)S(1)} %shard_map.95), channel_id=1, source_target_pairs={{0,64},{64,0},{1,65},{65,1},{2,66},{66,2},{3,67},{67,3},{4,68},{68... | collective-permute-start | bytes 786440 | tf_op jit(solution)/shard_map/ppermute | solution.py:33
  68.7 15.4 %all-to-all-start.2 = ((bf16[64,16,384]{2,1,0:T(8,128)(2,1)}), bf16[64,16,384]{2,1,0:T(8,128)(2,1)S(1)}, u32[]{:S(2)}, u32[]{:S(2)}) async-start(bf16[64,16,384]{2,1,0:T(8,128)(2,1)} %shard_map.96), calls=%async_computation.2 | async-start | bytes 1572864 | tf_op jit(solution)/shard_map/all_to_all | solution.py:23
  87.3 3.6 %collective-permute-start.9 = (bf16[1024,256]{1,0:T(8,128)(2,1)S(1)}, bf16[1024,256]{1,0:T(8,128)(2,1)S(1)}, u32[]{:S(2)}, u32[]{:S(2)}) collective-permute-start(bf16[1024,256]{1,0:T(8,128)(2,1)S(1)} %bitcast.28), channel_id=1, source_target_pairs={{0,384},{128,0},{256,128},{384,256},{1,385},{129,1},{257,129},{385... | collective-permute-start | bytes 1572872 | tf_op jit(solution)/shard_map/ppermute | solution.py:33
  93.7 7.0 %collective-permute-done.7.h1 = bf16[1024,256]{1,0:T(8,128)(2,1)S(1)} collective-permute-done((bf16[1024,256]{1,0:T(8,128)(2,1)S(1)}, bf16[1024,256]{1,0:T(8,128)(2,1)S(1)}, u32[]{:S(2)}, u32[]{:S(2)}) %collective-permute-start.7) | collective-permute-done | bytes 524320 | tf_op jit(solution)/shard_map/ppermute | solution.py:33
  102.7 4.6 %collective-permute-start.10 = (bf16[512,256]{1,0:T(8,128)(2,1)S(1)}, bf16[512,256]{1,0:T(8,128)(2,1)S(1)}, u32[]{:S(2)}, u32[]{:S(2)}) collective-permute-start(bf16[512,256]{1,0:T(8,128)(2,1)S(1)} %slice.81), channel_id=1, source_target_pairs={{0,384},{128,0},{256,128},{384,256},{1,385},{129,1},{257,129},{385... | collective-permute-start | bytes 786440 | tf_op jit(solution)/shard_map/ppermute | solution.py:33
  115.8 9.0 %all-to-all-done.2 = bf16[64,16,384]{2,1,0:T(8,128)(2,1)S(1)} async-done(((bf16[64,16,384]{2,1,0:T(8,128)(2,1)}), bf16[64,16,384]{2,1,0:T(8,128)(2,1)S(1)}, u32[]{:S(2)}, u32[]{:S(2)}) %all-to-all-start.2) | async-done | bytes 786464 | tf_op jit(solution)/shard_map/all_to_all | solution.py:23
  127.3 9.0 %all-to-all-start.3 = ((bf16[64,16,384]{2,1,0:T(8,128)(2,1)}), bf16[64,16,384]{2,1,0:T(8,128)(2,1)S(1)}, u32[]{:S(2)}, u32[]{:S(2)}) async-start(bf16[64,16,384]{2,1,0:T(8,128)(2,1)} %bitcast.8), calls=%async_computation.3 | async-start | bytes 1572864 | tf_op jit(solution)/shard_map/all_to_all | solution.py:23
  136.4 4.5 %collective-permute-start.13 = (bf16[512,256]{1,0:T(8,128)(2,1)S(1)}, bf16[512,256]{1,0:T(8,128)(2,1)S(1)}, u32[]{:S(2)}, u32[]{:S(2)}) collective-permute-start(bf16[512,256]{1,0:T(8,128)(2,1)S(1)} %get-tuple-element.90), channel_id=1, source_target_pairs={{0,384},{128,0},{256,128},{384,256},{1,385},{129,1},{257,129},{385... | collective-permute-start | bytes 786440 | tf_op jit(solution)/shard_map/ppermute | solution.py:33
  145.7 5.3 %collective-permute-start.14 = (bf16[1024,256]{1,0:T(8,128)(2,1)S(1)}, bf16[1024,256]{1,0:T(8,128)(2,1)S(1)}, u32[]{:S(2)}, u32[]{:S(2)}) collective-permute-start(bf16[1024,256]{1,0:T(8,128)(2,1)S(1)} %pad_maximum_fusion.2), channel_id=1, source_target_pairs={{0,384},{128,0},{256,128},{384,256},{1,385},{129,1},{257,129},{385... | collective-permute-start | bytes 1572872 | tf_op jit(solution)/shard_map/ppermute | solution.py:33
  153.2 7.4 %collective-permute-done.14 = bf16[1024,256]{1,0:T(8,128)(2,1)S(1)} collective-permute-done((bf16[1024,256]{1,0:T(8,128)(2,1)S(1)}, bf16[1024,256]{1,0:T(8,128)(2,1)S(1)}, u32[]{:S(2)}, u32[]{:S(2)}) %collective-permute-start.14) | collective-permute-done | bytes 524320 | tf_op jit(solution)/shard_map/ppermute | solution.py:33
  160.5 5.3 %collective-permute-done.12 = bf16[1024,256]{1,0:T(8,128)(2,1)} collective-permute-done((bf16[1024,256]{1,0:T(8,128)(2,1)S(1)}, bf16[1024,256]{1,0:T(8,128)(2,1)}, u32[]{:S(2)}, u32[]{:S(2)}) %collective-permute-start.12) | collective-permute-done | bytes 524320 | tf_op jit(solution)/shard_map/ppermute | solution.py:33
  167.1 3.7 %collective-permute-start.17 = (bf16[256,256]{1,0:T(8,128)(2,1)S(1)}, bf16[256,256]{1,0:T(8,128)(2,1)S(1)}, u32[]{:S(2)}, u32[]{:S(2)}) collective-permute-start(bf16[256,256]{1,0:T(8,128)(2,1)S(1)} %get-tuple-element.87), channel_id=1, source_target_pairs={{0,48},{16,0},{32,16},{48,32},{1,49},{17,1},{33,17},{49,33},{2,50}... | collective-permute-start | bytes 393224 | tf_op jit(solution)/shard_map/ppermute | solution.py:33
  185.3 4.6 %collective-permute-start.19 = (bf16[49,16,256]{2,1,0:T(8,128)(2,1)S(1)}, bf16[49,16,256]{2,1,0:T(8,128)(2,1)S(1)}, u32[]{:S(2)}, u32[]{:S(2)}) collective-permute-start(bf16[49,16,256]{2,1,0:T(8,128)(2,1)S(1)} %get-tuple-element.67.p0), channel_id=1, source_target_pairs={{0,384},{128,0},{256,128},{384,256},{1,385},{129,1},{257,129},{385... | collective-permute-start | bytes 1204232 | tf_op jit(solution)/shard_map/ppermute | solution.py:33
  189.9 11.4 %all-to-all-start.4 = ((bf16[16,16,256]{2,1,0:T(8,128)(2,1)}), bf16[16,16,256]{2,1,0:T(8,128)(2,1)}, u32[]{:S(2)}, u32[]{:S(2)}) async-start(bf16[16,16,256]{2,1,0:T(8,128)(2,1)} %bitcast.14), calls=%async_computation.4 | async-start | bytes 262144 | tf_op jit(solution)/shard_map/all_to_all | solution.py:23
  204.0 4.6 %collective-permute-start.22 = (bf16[32,16,256]{2,1,0:T(8,128)(2,1)}, bf16[32,16,256]{2,1,0:T(8,128)(2,1)}, u32[]{:S(2)}, u32[]{:S(2)}) collective-permute-start(bf16[32,16,256]{2,1,0:T(8,128)(2,1)} %get-tuple-element.73), channel_id=1, source_target_pairs={{0,384},{128,0},{256,128},{384,256},{1,385},{129,1},{257,129},{385... | collective-permute-start | bytes 786440 | tf_op jit(solution)/shard_map/ppermute | solution.py:33
  209.7 4.6 %shard_map.102.before_ref = f32[264,16,128]{2,1,0:T(8,128)S(1)} custom-call(s32[4]{0:T(128)S(1)} %pad_add_fusion.where_ref, s32[3,16,64]{2,1,0:T(8,128)S(1)} %maximum_convert_fusion.ids_ref, bf16[49,16,256]{2,1,0:T(8,128)(2,1)S(1)} %copy-done.9, bf16[49,16,256]{2,1,0:T(8,128)(2,1)S(1)} %collective-permute-done.18.r1.p1, ...), custom_call_target="tpu_custom_call" | custom-call | flops 1000000 | bytes 1000000 | tf_op jit(solution)/shard_map/pallas_call | solution.py:485
  219.2 8.4 %collective-permute-start.23 = (bf16[72,16,256]{2,1,0:T(8,128)(2,1)}, bf16[72,16,256]{2,1,0:T(8,128)(2,1)S(1)}, u32[]{:S(2)}, u32[]{:S(2)}) collective-permute-start(bf16[72,16,256]{2,1,0:T(8,128)(2,1)} %get-tuple-element.81), channel_id=1, source_target_pairs={{0,64},{64,0},{1,65},{65,1},{2,66},{66,2},{3,67},{67,3},{4,68},{68... | collective-permute-start | bytes 1769480 | tf_op jit(solution)/shard_map/ppermute | solution.py:33
  232.2 3.9 %all-to-all-start.5 = ((bf16[8,9,16,256]{3,2,1,0:T(8,128)(2,1)}), bf16[8,9,16,256]{3,2,1,0:T(8,128)(2,1)S(1)}, u32[]{:S(2)}, u32[]{:S(2)}) async-start(bf16[8,9,16,256]{3,2,1,0:T(8,128)(2,1)} %broadcast_in_dim.8), calls=%async_computation.5 | async-start | bytes 1179648 | tf_op jit(solution)/shard_map/all_to_all | solution.py:23
  238.9 7.5 %all-to-all-done.5.total_ref = bf16[8,9,16,256]{3,2,1,0:T(8,128)(2,1)S(1)} async-done(((bf16[8,9,16,256]{3,2,1,0:T(8,128)(2,1)}), bf16[8,9,16,256]{3,2,1,0:T(8,128)(2,1)S(1)}, u32[]{:S(2)}, u32[]{:S(2)}) %all-to-all-start.5) | async-done | bytes 589856 | tf_op jit(solution)/shard_map/all_to_all | solution.py:23
  (113 shorter events, 85.5 us)
Async XLA Ops:
  0.6 9.7 %collective-permute-start = (s32[1,3]{1,0:T(1,128)}, s32[1,3]{1,0:T(1,128)S(1)}, u32[]{:S(2)}, u32[]{:S(2)}) collective-permute-start(s32[1,3]{1,0:T(1,128)} %own_ref.1), channel_id=1, source_target_pairs={{0,64},{64,0},{1,65},{65,1},{2,66},{66,2},{3,67},{67,3},{4,68},{68... | collective-permute-start | bytes 44 | tf_op jit(solution)/shard_map/ppermute | solution.py:33
  13.2 27.6 %all-to-all-start = ((bf16[16,16,384]{2,1,0:T(8,128)(2,1)}), bf16[16,16,384]{2,1,0:T(8,128)(2,1)S(1)}, u32[]{:S(2)}, u32[]{:S(2)}) async-start(bf16[16,16,384]{2,1,0:T(8,128)(2,1)} %shard_map.93), calls=%async_computation | async-start | bytes 393216 | tf_op jit(solution)/shard_map/all_to_all | solution.py:23
  22.8 16.4 %collective-permute-start.1 = (bf16[128,16,128]{2,1,0:T(8,128)(2,1)}, bf16[128,16,128]{2,1,0:T(8,128)(2,1)S(1)}, u32[]{:S(2)}, u32[]{:S(2)}) collective-permute-start(bf16[128,16,128]{2,1,0:T(8,128)(2,1)} %f0.3), channel_id=1, source_target_pairs={{0,128},{128,256},{256,384},{384,0},{1,129},{129,257},{257,385},{3... | collective-permute-start | bytes 1572872 | tf_op jit(solution)/shard_map/ppermute | solution.py:33
  26.1 14.7 %collective-permute-start.2 = (bf16[128,16,128]{2,1,0:T(8,128)(2,1)}, bf16[128,16,128]{2,1,0:T(8,128)(2,1)S(1)}, u32[]{:S(2)}, u32[]{:S(2)}) collective-permute-start(bf16[128,16,128]{2,1,0:T(8,128)(2,1)} %f0.3), channel_id=1, source_target_pairs={{0,384},{128,0},{256,128},{384,256},{1,385},{129,1},{257,129},{385... | collective-permute-start | bytes 1572872 | tf_op jit(solution)/shard_map/ppermute | solution.py:33
  41.8 14.1 %all-to-all-start.1 = ((bf16[4,16,16,384]{3,1,2,0:T(8,128)(2,1)}), bf16[4,16,16,384]{3,1,2,0:T(8,128)(2,1)S(1)}, u32[]{:S(2)}, u32[]{:S(2)}) async-start(bf16[4,16,16,384]{3,1,2,0:T(8,128)(2,1)} %broadcast_in_dim.6), calls=%async_computation.1 | async-start | bytes 1572864 | tf_op jit(solution)/shard_map/all_to_all | solution.py:23
  46.6 9.3 %collective-permute-start.3 = (bf16[64,16,128]{2,1,0:T(8,128)(2,1)}, bf16[64,16,128]{2,1,0:T(8,128)(2,1)S(1)}, u32[]{:S(2)}, u32[]{:S(2)}) collective-permute-start(bf16[64,16,128]{2,1,0:T(8,128)(2,1)} %slice.58), channel_id=1, source_target_pairs={{0,128},{128,256},{256,384},{384,0},{1,129},{129,257},{257,385},{3... | collective-permute-start | bytes 786440 | tf_op jit(solution)/shard_map/ppermute | solution.py:33
  68.7 56.0 %all-to-all-start.2 = ((bf16[64,16,384]{2,1,0:T(8,128)(2,1)}), bf16[64,16,384]{2,1,0:T(8,128)(2,1)S(1)}, u32[]{:S(2)}, u32[]{:S(2)}) async-start(bf16[64,16,384]{2,1,0:T(8,128)(2,1)} %shard_map.96), calls=%async_computation.2 | async-start | bytes 1572864 | tf_op jit(solution)/shard_map/all_to_all | solution.py:23
  84.4 16.3 %collective-permute-start.7 = (bf16[1024,256]{1,0:T(8,128)(2,1)S(1)}, bf16[1024,256]{1,0:T(8,128)(2,1)S(1)}, u32[]{:S(2)}, u32[]{:S(2)}) collective-permute-start(bf16[1024,256]{1,0:T(8,128)(2,1)S(1)} %bitcast.27), channel_id=1, source_target_pairs={{0,128},{128,256},{256,384},{384,0},{1,129},{129,257},{257,385},{3... | collective-permute-start | bytes 1572872 | tf_op jit(solution)/shard_map/ppermute | solution.py:33
  87.3 15.4 %collective-permute-start.9 = (bf16[1024,256]{1,0:T(8,128)(2,1)S(1)}, bf16[1024,256]{1,0:T(8,128)(2,1)S(1)}, u32[]{:S(2)}, u32[]{:S(2)}) collective-permute-start(bf16[1024,256]{1,0:T(8,128)(2,1)S(1)} %bitcast.28), channel_id=1, source_target_pairs={{0,384},{128,0},{256,128},{384,256},{1,385},{129,1},{257,129},{385... | collective-permute-start | bytes 1572872 | tf_op jit(solution)/shard_map/ppermute | solution.py:33
  91.0 16.4 %collective-permute-start.6 = (bf16[256,1024]{1,0:T(8,128)(2,1)S(1)}, bf16[256,1024]{1,0:T(8,128)(2,1)S(1)}, u32[]{:S(2)}, u32[]{:S(2)}) collective-permute-start(bf16[256,1024]{1,0:T(8,128)(2,1)S(1)} %pad_maximum_fusion), channel_id=1, source_target_pairs={{0,64},{64,0},{1,65},{65,1},{2,66},{66,2},{3,67},{67,3},{4,68},{68... | collective-permute-start | bytes 1572872 | tf_op jit(solution)/shard_map/ppermute | solution.py:33
  100.8 9.8 %collective-permute-start.8 = (bf16[512,256]{1,0:T(8,128)(2,1)S(1)}, bf16[512,256]{1,0:T(8,128)(2,1)S(1)}, u32[]{:S(2)}, u32[]{:S(2)}) collective-permute-start(bf16[512,256]{1,0:T(8,128)(2,1)S(1)} %slice.80), channel_id=1, source_target_pairs={{0,128},{128,256},{256,384},{384,0},{1,129},{129,257},{257,385},{3... | collective-permute-start | bytes 786440 | tf_op jit(solution)/shard_map/ppermute | solution.py:33
  102.7 8.8 %collective-permute-start.10 = (bf16[512,256]{1,0:T(8,128)(2,1)S(1)}, bf16[512,256]{1,0:T(8,128)(2,1)S(1)}, u32[]{:S(2)}, u32[]{:S(2)}) collective-permute-start(bf16[512,256]{1,0:T(8,128)(2,1)S(1)} %slice.81), channel_id=1, source_target_pairs={{0,384},{128,0},{256,128},{384,256},{1,385},{129,1},{257,129},{385... | collective-permute-start | bytes 786440 | tf_op jit(solution)/shard_map/ppermute | solution.py:33
  127.3 53.4 %all-to-all-start.3 = ((bf16[64,16,384]{2,1,0:T(8,128)(2,1)}), bf16[64,16,384]{2,1,0:T(8,128)(2,1)S(1)}, u32[]{:S(2)}, u32[]{:S(2)}) async-start(bf16[64,16,384]{2,1,0:T(8,128)(2,1)} %bitcast.8), calls=%async_computation.3 | async-start | bytes 1572864 | tf_op jit(solution)/shard_map/all_to_all | solution.py:23
  136.4 9.3 %collective-permute-start.13 = (bf16[512,256]{1,0:T(8,128)(2,1)S(1)}, bf16[512,256]{1,0:T(8,128)(2,1)S(1)}, u32[]{:S(2)}, u32[]{:S(2)}) collective-permute-start(bf16[512,256]{1,0:T(8,128)(2,1)S(1)} %get-tuple-element.90), channel_id=1, source_target_pairs={{0,384},{128,0},{256,128},{384,256},{1,385},{129,1},{257,129},{385... | collective-permute-start | bytes 786440 | tf_op jit(solution)/shard_map/ppermute | solution.py:33
  140.9 10.2 %collective-permute-start.11 = (bf16[512,256]{1,0:T(8,128)(2,1)S(1)}, bf16[512,256]{1,0:T(8,128)(2,1)S(1)}, u32[]{:S(2)}, u32[]{:S(2)}) collective-permute-start(bf16[512,256]{1,0:T(8,128)(2,1)S(1)} %get-tuple-element.89), channel_id=1, source_target_pairs={{0,128},{128,256},{256,384},{384,0},{1,129},{129,257},{257,385},{3... | collective-permute-start | bytes 786440 | tf_op jit(solution)/shard_map/ppermute | solution.py:33
  145.7 14.8 %collective-permute-start.14 = (bf16[1024,256]{1,0:T(8,128)(2,1)S(1)}, bf16[1024,256]{1,0:T(8,128)(2,1)S(1)}, u32[]{:S(2)}, u32[]{:S(2)}) collective-permute-start(bf16[1024,256]{1,0:T(8,128)(2,1)S(1)} %pad_maximum_fusion.2), channel_id=1, source_target_pairs={{0,384},{128,0},{256,128},{384,256},{1,385},{129,1},{257,129},{385... | collective-permute-start | bytes 1572872 | tf_op jit(solution)/shard_map/ppermute | solution.py:33
  151.2 14.6 %collective-permute-start.12 = (bf16[1024,256]{1,0:T(8,128)(2,1)S(1)}, bf16[1024,256]{1,0:T(8,128)(2,1)}, u32[]{:S(2)}, u32[]{:S(2)}) collective-permute-start(bf16[1024,256]{1,0:T(8,128)(2,1)S(1)} %pad_maximum_fusion.1), channel_id=1, source_target_pairs={{0,128},{128,256},{256,384},{384,0},{1,129},{129,257},{257,385},{3... | collective-permute-start | bytes 1572872 | tf_op jit(solution)/shard_map/ppermute | solution.py:33
  183.4 17.9 %collective-permute-start.18 = (bf16[49,16,256]{2,1,0:T(8,128)(2,1)S(1)}, bf16[49,16,256]{2,1,0:T(8,128)(2,1)S(1)}, u32[]{:S(2)}, u32[]{:S(2)}) collective-permute-start(bf16[49,16,256]{2,1,0:T(8,128)(2,1)S(1)} %get-tuple-element.67.p0), channel_id=1, source_target_pairs={{0,128},{128,256},{256,384},{384,0},{1,129},{129,257},{257,385},{3... | collective-permute-start | bytes 1204232 | tf_op jit(solution)/shard_map/ppermute | solution.py:33
  185.3 16.0 %collective-permute-start.19 = (bf16[49,16,256]{2,1,0:T(8,128)(2,1)S(1)}, bf16[49,16,256]{2,1,0:T(8,128)(2,1)S(1)}, u32[]{:S(2)}, u32[]{:S(2)}) collective-permute-start(bf16[49,16,256]{2,1,0:T(8,128)(2,1)S(1)} %get-tuple-element.67.p0), channel_id=1, source_target_pairs={{0,384},{128,0},{256,128},{384,256},{1,385},{129,1},{257,129},{385... | collective-permute-start | bytes 1204232 | tf_op jit(solution)/shard_map/ppermute | solution.py:33
  189.9 24.4 %all-to-all-start.4 = ((bf16[16,16,256]{2,1,0:T(8,128)(2,1)}), bf16[16,16,256]{2,1,0:T(8,128)(2,1)}, u32[]{:S(2)}, u32[]{:S(2)}) async-start(bf16[16,16,256]{2,1,0:T(8,128)(2,1)} %bitcast.14), calls=%async_computation.4 | async-start | bytes 262144 | tf_op jit(solution)/shard_map/all_to_all | solution.py:23
  202.1 12.2 %collective-permute-start.21 = (bf16[33,16,256]{2,1,0:T(8,128)(2,1)}, bf16[33,16,256]{2,1,0:T(8,128)(2,1)S(1)}, u32[]{:S(2)}, u32[]{:S(2)}) collective-permute-start(bf16[33,16,256]{2,1,0:T(8,128)(2,1)} %get-tuple-element.70), channel_id=1, source_target_pairs={{0,128},{128,256},{256,384},{384,0},{1,129},{129,257},{257,385},{3... | collective-permute-start | bytes 811016 | tf_op jit(solution)/shard_map/ppermute | solution.py:33
  204.0 10.3 %collective-permute-start.22 = (bf16[32,16,256]{2,1,0:T(8,128)(2,1)}, bf16[32,16,256]{2,1,0:T(8,128)(2,1)}, u32[]{:S(2)}, u32[]{:S(2)}) collective-permute-start(bf16[32,16,256]{2,1,0:T(8,128)(2,1)} %get-tuple-element.73), channel_id=1, source_target_pairs={{0,384},{128,0},{256,128},{384,256},{1,385},{129,1},{257,129},{385... | collective-permute-start | bytes 786440 | tf_op jit(solution)/shard_map/ppermute | solution.py:33
  219.2 11.3 %collective-permute-start.23 = (bf16[72,16,256]{2,1,0:T(8,128)(2,1)}, bf16[72,16,256]{2,1,0:T(8,128)(2,1)S(1)}, u32[]{:S(2)}, u32[]{:S(2)}) collective-permute-start(bf16[72,16,256]{2,1,0:T(8,128)(2,1)} %get-tuple-element.81), channel_id=1, source_target_pairs={{0,64},{64,0},{1,65},{65,1},{2,66},{66,2},{3,67},{67,3},{4,68},{68... | collective-permute-start | bytes 1769480 | tf_op jit(solution)/shard_map/ppermute | solution.py:33
  232.2 14.1 %all-to-all-start.5 = ((bf16[8,9,16,256]{3,2,1,0:T(8,128)(2,1)}), bf16[8,9,16,256]{3,2,1,0:T(8,128)(2,1)S(1)}, u32[]{:S(2)}, u32[]{:S(2)}) async-start(bf16[8,9,16,256]{3,2,1,0:T(8,128)(2,1)} %broadcast_in_dim.8), calls=%async_computation.5 | async-start | bytes 1179648 | tf_op jit(solution)/shard_map/all_to_all | solution.py:23
  (22 other events, 226.3 us)

commit v6 on v5

--- a/solution.py
+++ b/solution.py
@@ -98,17 +98,28 @@
         out_ref[z, :, 2 * width :] = numbers
 
 
-def numbers_kernel(grid_ref, out_ref):
-    width = grid_ref.shape[3] - 128
+def repack_kernel(packets_ref, out_ref):
+    width = out_ref.shape[2]
     rows = lax.broadcasted_iota(I32, (ROWS, 128), 0)
+    line = jnp.zeros((ROWS, 128), F32)
+    for z in range(Z):
+        line = jnp.where(rows == z, packets_ref[z, :, width:].astype(F32), line)
+    line = line.astype(BF16)
+    for x in range(X):
+        for z in range(Z):
+            out_ref[x, z * ROWS : (z + 1) * ROWS] = packets_ref[z, :, :width]
+        out_ref[x, Z * ROWS :, :128] = line
+        out_ref[x, Z * ROWS :, 128:] = jnp.zeros((ROWS, width - 128), BF16)
+
+
+def numbers_kernel(*refs):
+    lines, out_ref = refs[:-1], refs[-1]
     total = jnp.zeros((ROWS, 128), F32)
-    for x in range(X):
-        line = jnp.zeros((ROWS, 128), F32)
-        for z in range(Z):
-            line = jnp.where(rows == z, grid_ref[x, z, :, width:].astype(F32), line)
+    for x, ref in enumerate(lines):
+        line = ref[:, :128].astype(F32)
         total = total + (pltpu.roll(line, LANES * C * x, 1) if x else line)
     out_ref[0, :, :128] = total.astype(BF16)
-    out_ref[0, :, 128:] = jnp.zeros((ROWS, 128), BF16)
+    out_ref[0, :, 128:] = jnp.zeros((ROWS, out_ref.shape[2] - 128), BF16)
 
 
 def chosen(code, pieces):
@@ -160,7 +171,7 @@
 
 def coarse_kernel(
     where_ref, ids_ref, x_ref, g_ref, ox_ref, og_ref, h0, h1, h2a, h2b, h3,
-    s0, s1, s2, s3, back_ref, other_back_ref, half_ref, own_term, other_term,
+    s0, s1, s2a, s2b, s3, back_ref, other_back_ref, half_ref, own_term, other_term,
 ):
     y_index = where_ref[0]
     c_index, x_index, z_index = where_ref[1], where_ref[2], where_ref[3]
@@ -191,25 +202,51 @@
 
     level(own_id, x_ref, g_ref, own_term, back_ref)
     level(other_id, ox_ref, og_ref, other_term, other_back_ref)
-    for s, ref in enumerate((s0, s1, s2, s3)):
+    middle_row = s2a.shape[0]
+    everything = slice(0, s0.shape[0])
+    lower, upper = slice(0, middle_row), slice(middle_row, s0.shape[0])
+    for s, rows, ref in (
+        (2, lower, s2a),
+        (2, upper, s2b),
+        (0, everything, s0),
+        (1, everything, s1),
+        (3, everything, s3),
+    ):
         block = (y_index + s) % Y
         own, other = own_id == block, other_id == block
 
         @pl.when(jnp.logical_and(own, other))
-        def _(ref=ref):
-            ref[...] = (own_term[...] + other_term[...]).astype(BF16)
+        def _(ref=ref, rows=rows):
+            ref[...] = (own_term[rows] + other_term[rows]).astype(BF16)
 
         @pl.when(jnp.logical_and(own, jnp.logical_not(other)))
-        def _(ref=ref):
-            ref[...] = own_term[...].astype(BF16)
+        def _(ref=ref, rows=rows):
+            ref[...] = own_term[rows].astype(BF16)
 
         @pl.when(jnp.logical_and(other, jnp.logical_not(own)))
-        def _(ref=ref):
-            ref[...] = other_term[...].astype(BF16)
+        def _(ref=ref, rows=rows):
+            ref[...] = other_term[rows].astype(BF16)
 
         @pl.when(jnp.logical_not(jnp.logical_or(own, other)))
         def _(ref=ref):
             ref[...] = jnp.zeros(ref.shape, BF16)
+
+
+def coarse_relay_kernel(s1, s3, r1, r3, up_ref, down_ref):
+    middle_row = r1.shape[0]
+    up_ref[:middle_row] = (s1[:middle_row].astype(F32) + r1[...].astype(F32)).astype(BF16)
+    up_ref[middle_row:] = s1[middle_row:]
+    down_ref[:middle_row] = s3[:middle_row]
+    down_ref[middle_row:] = (s3[middle_row:].astype(F32) + r3[...].astype(F32)).astype(BF16)
+
+
+def coarse_sum_kernel(where_ref, s0, up_ref, down_ref, own_ref, *leaving):
+    x_index = where_ref[2]
+    rows = own_ref.shape[0]
+    for s, ref in enumerate((own_ref,) + leaving):
+        at = pl.ds(pl.multiple_of(((x_index + s) % X) * rows, rows), rows)
+        total = s0[at].astype(F32) + up_ref[at].astype(F32) + down_ref[at].astype(F32)
+        ref[...] = total.astype(ref.dtype)
 
 
 def levels_kernel(x_ref, g_ref, w_ref, term_ref, back_ref):
@@ -308,19 +345,9 @@
         add_fine(where_ref, owned, ids_ref, p, piece, range(X), sums_ref)
 
 
-def last_fine_kernel(
-    where_ref, ids_ref, before_ref, s0, q1, q3, leave_ref, middle_ref, fine_ref, sums_ref
-):
-    owned = fine_ref.shape[0]
-    share = middle_ref.shape[0]
+def middle_kernel(where_ref, s0, q1, q3, kept_ref, leave_ref):
+    share = kept_ref.shape[0]
     lower = MEMBERS // 4
-    sums_ref[...] = before_ref[...]
-    add_fine(where_ref, owned, ids_ref, 0, q1, range(X // 2), sums_ref)
-    add_fine(where_ref, owned, ids_ref, 0, q3, range(X // 2, X), sums_ref)
-    fine_ref[...] = sums_ref[:owned]
-    half = owned // 2
-    leave_ref[share:, :, :128] = sums_ref[owned : owned + half].astype(BF16)
-    leave_ref[share:, :, 128:] = sums_ref[owned + half : 2 * owned].astype(BF16)
 
     def middle_of(side):
         low = side * share
@@ -330,18 +357,42 @@
             + q3[pl.ds(lower + low, share)].astype(F32)
         )
 
-    middle_ref[...] = middle_of(where_ref[1])
-    leave_ref[:share] = middle_of(1 - where_ref[1]).astype(BF16)
+    kept_ref[...] = middle_of(where_ref[1])
+    leave_ref[...] = middle_of(1 - where_ref[1]).astype(BF16)
+
+
+def last_fine_kernel(
+    where_ref, ids_ref, before_ref, q1, q3, leave_ref, fine_ref, sums_ref
+):
+    owned = fine_ref.shape[0]
+    sums_ref[...] = before_ref[...]
+    add_fine(where_ref, owned, ids_ref, 0, q1, range(X // 2), sums_ref)
+    add_fine(where_ref, owned, ids_ref, 0, q3, range(X // 2, X), sums_ref)
+    fine_ref[...] = sums_ref[:owned]
+    half = owned // 2
+    leave_ref[:, :, :128] = sums_ref[owned : owned + half].astype(BF16)
+    leave_ref[:, :, 128:] = sums_ref[owned + half : 2 * owned].astype(BF16)
+
+
+def done_kernel(kept_ref, arrived_ref, coarse_ref, out_ref):
+    share = kept_ref.shape[0]
+    middle = (kept_ref[...] + arrived_ref[...].astype(F32)).astype(BF16)
+    coarse = coarse_ref[0].astype(F32)
+    for z in range(1, Z):
+        coarse = coarse + coarse_ref[z].astype(F32)
+    coarse = coarse.astype(BF16)
+    for g in range(out_ref.shape[0]):
+        out_ref[g, :share] = middle
+        out_ref[g, share] = coarse
 
 
 def finish_kernel(fine_ref, arrived_ref, out_ref):
     half = fine_ref.shape[0] // 2
-    share = arrived_ref.shape[0] - half
     for h in range(2):
         low = h * half
         out_ref[low : low + half] = (
             fine_ref[low : low + half]
-            + arrived_ref[share:, :, h * 128 : h * 128 + 128].astype(F32)
+            + arrived_ref[:, :, h * 128 : h * 128 + 128].astype(F32)
         ).astype(BF16)
 
 
@@ -378,8 +429,9 @@
 
     fine_one = shift(after(fine_weights, packet), "y", 1)
     fine_three = shift(after(fine_weights, packet), "y", 3)
-    packets, fine_one, fine_three = lax.optimization_barrier((packets, fine_one, fine_three))
-    packets = gather(packets, "x").reshape(X, Z, ROWS, half + 128)
+    packets, fine_one = lax.optimization_barrier((packets, fine_one))
+    packets = kernel_call(repack_kernel, [VMEM], bf16(X, Z * ROWS + ROWS, half))(packets)
+    packets = exchange(packets, "x")
     split = fine_owned // 2
     fine_rows = [
         fine_weights,
@@ -388,7 +440,7 @@
         fine_three,
         shift(fine_three[split:], "y", 3),
     ]
-    ids = packets[:, :, 0, half : half + LANES * C].astype(I32)
+    ids = packets[:, Z * ROWS : Z * ROWS + Z, : LANES * C].astype(I32)
     extra = kernel_call(
         pick_other_kernel, [SMEM] * 2 + [VMEM] * 5, bf16(MEMBERS, ROWS, fine_width)
     )(where, ids, *fine_rows)
@@ -404,10 +456,11 @@
     both = jnp.concatenate([after(tokens, send), cotangent], axis=0)
     other_both = shift(both, "c", 1)
 
-    numbers = kernel_call(numbers_kernel, [VMEM], bf16(1, ROWS, 2 * fine_width))(
-        after(packets, send)
+    lines = after(packets, send)[:, Z * ROWS :]
+    numbers = kernel_call(numbers_kernel, [VMEM] * X, bf16(1, ROWS, 2 * fine_width))(
+        *[lines[x] for x in range(X)]
     )
-    block = after(packets, send)[:, :, :, :half].reshape(depth, half)
+    block = after(packets, send)[:, : Z * ROWS].reshape(depth, half)
     one, three = shift(block, "y", 1), shift(block, "y", 3)
     middle_row = depth // 2
     halves = [
@@ -421,7 +474,12 @@
     slots = kernel_call(
         coarse_kernel,
         [SMEM, SMEM] + [VMEM] * 9,
-        tuple([bf16(depth, half)] * Y + [f32(length, depth)] * 2),
+        tuple(
+            [bf16(depth, half)] * 2
+            + [bf16(middle_row, half)] * 2
+            + [bf16(depth, half)]
+            + [f32(length, depth)] * 2
+        ),
         [
             pltpu.VMEM((depth, half), BF16),
             pltpu.VMEM((depth, half), F32),
@@ -431,8 +489,9 @@
     )(
         where, ids, tokens, cotangent, other_both[:length], other_both[length:], *halves
     )
-    mine, numbers, *slots = lax.optimization_barrier([mine, numbers] + list(slots))
-    slots, coarse_back, other_back = slots[:Y], slots[Y], slots[Y + 1]
+    near, ahead, far_low, far_high, behind, coarse_back, other_back = slots
+    up, down = shift(far_low, "y", 1), shift(far_high, "y", 3)
+    mine, numbers, up, down = lax.optimization_barrier((mine, numbers, up, down))
 
     terms, back = kernel_call(
         levels_kernel,
@@ -442,17 +501,17 @@
     )(tokens, cotangent, mine)
     parts = exchange(terms.reshape(MEMBERS, ROWS, -1), ("x", "z"))
 
-    up = shift(slots[2][:middle_row], "y", 1).astype(F32)
-    down = shift(slots[2][middle_row:], "y", 3).astype(F32)
-    up = (slots[1][:middle_row].astype(F32) + up).astype(BF16)
-    down = (slots[3][middle_row:].astype(F32) + down).astype(BF16)
-    up = shift(jnp.concatenate([up, slots[1][middle_row:]]), "y", 1).astype(F32)
-    down = shift(jnp.concatenate([slots[3][:middle_row], down]), "y", 3).astype(F32)
-    summed = (slots[0].astype(F32) + up + down).astype(BF16).reshape(X, Z * ROWS, half)
-    column_sum = lax.dynamic_index_in_dim(summed, x_index, 0, keepdims=False).astype(F32)
+    up, down = kernel_call(coarse_relay_kernel, [VMEM] * 4, (bf16(depth, half),) * 2)(
+        ahead, behind, up, down
+    )
+    up, down = shift(after(up, terms), "y", 1), shift(after(down, terms), "y", 3)
+    column_sum, *leaving = kernel_call(
+        coarse_sum_kernel,
+        [SMEM] + [VMEM] * 3,
+        tuple([f32(Z * ROWS, half)] + [bf16(Z * ROWS, half)] * (X - 1)),
+    )(where, near, up, down)
     for s in range(1, X):
-        leaving = lax.dynamic_index_in_dim(summed, (x_index + s) % X, 0, keepdims=False)
-        column_sum = column_sum + shift(leaving, "x", s).astype(F32)
+        column_sum = column_sum + shift(leaving[s - 1], "x", s).astype(F32)
     column_sum = column_sum.astype(BF16).reshape(Z, ROWS, half)
     parts, column_sum = lax.optimization_barrier((parts, column_sum))
 
@@ -490,27 +549,29 @@
     fine_sums, q1, q3, coarse_four = lax.optimization_barrier(
         (fine_sums, q1, q3, coarse_four)
     )
-    leave, middle_done, fine_kept = kernel_call(
+    middle_kept, middle_leave = kernel_call(
+        middle_kernel,
+        [SMEM] + [VMEM] * 3,
+        (f32(share, ROWS, middle_width), bf16(share, ROWS, middle_width)),
+    )(where, s0, q1, q3)
+    middle_arrived = shift(middle_leave, "c", 1)
+    fine_leave, fine_kept = kernel_call(
         last_fine_kernel,
-        [SMEM, SMEM] + [VMEM] * 4,
-        (
-            bf16(share + fine_owned // 2, ROWS, middle_width),
-            f32(share, ROWS, middle_width),
-            f32(fine_owned, ROWS, fine_width),
-        ),
+        [SMEM, SMEM] + [VMEM] * 3,
+        (bf16(fine_owned // 2, ROWS, 2 * fine_width), f32(fine_owned, ROWS, fine_width)),
         [pltpu.VMEM((C * fine_owned + 8, ROWS, fine_width), F32)],
-    )(where, q1[lower, :Z, : LANES * C * X].astype(I32)[None], fine_sums, s0, q1, q3)
-    arrived = shift(leave, "c", 1)
-    coarse_done = jnp.sum(coarse_four, axis=0, dtype=F32).astype(BF16)
-    middle_done = (middle_done + arrived[:share].astype(F32)).astype(BF16)
-    done = jnp.concatenate([middle_done, coarse_done[None]], axis=0)
-    total = gather(done, ("y", "c")).reshape((Y * C,) + done.shape)
+    )(where, q1[lower, :Z, : LANES * C * X].astype(I32)[None], fine_sums, q1, q3)
+    done = kernel_call(
+        done_kernel, [VMEM] * 3, bf16(Y * C, share + 1, ROWS, middle_width)
+    )(middle_kept, middle_arrived, coarse_four)
+    total = exchange(done, ("y", "c"))
+    fine_arrived = shift(after(fine_leave, done), "c", 1)
     coarse_total, middle_total = kernel_call(
         spread_kernel, [VMEM], (bf16(*coarse_weights.shape), bf16(*middle_weights.shape))
     )(total)
     fine_total = kernel_call(
         finish_kernel, [VMEM] * 2, bf16(fine_owned, ROWS, fine_width)
-    )(fine_kept, arrived)
+    )(fine_kept, fine_arrived)
     other_back = shift(after(other_back, second[0]), "c", 1)
     tokens_grad = (coarse_back + other_back + back).astype(BF16)
     return (tokens_grad, coarse_total, middle_total, fine_total)

time: 249 us -> 246 us (0.988)
  Pallas kernels: 23.6 us -> 27.5 us
  other arithmetic: 5.98 us -> 2.68 us
  local copies, waits for them, and re-layouts: 10.9 us -> 7.69 us
    pallas_call x2 -> x7, Pallas kernels: 3.32 us -> 7.2 us  [the longest x1 2.87 us: on_device(): kernel_call(last_fine_kernel, [SMEM, SMEM] + [VMEM] * 3, (bf16(fine_owned...]
    ppermute x24 -> x25, starting transfers between devices: 88.3 us -> 90.2 us  [shift(): lax.ppermute(array, axis, [(i, (i + step) % count) for i in range(count)])]
    unnamed x32 -> x40, local copies, waits for them, and re-layouts: 7.18 us -> 6.08 us
    ppermute x24 -> x25, waiting for transfers between devices: 45.2 us -> 44.2 us  [shift(): lax.ppermute(array, axis, [(i, (i + step) % count) for i in range(count)])]
  transfers between devices with their start and end apart: 30 -> 31, of which waited for: 15 -> 17; matrix products, arithmetic and copies ran while one was open for 4% -> 2% of each run, Pallas kernels for 5% -> 8%
where the time goes in v6:
time: 246 us; the launch traced here: 245 us
  starting transfers between devices  144 us (59%)
  waiting for transfers between devices  61.8 us (25%)
  Pallas kernels  27.5 us (11%)
  local copies, waits for them, and re-layouts  7.69 us (3%)
  other arithmetic  2.68 us (1%)
    ppermute x25, starting transfers between devices, shift(): lax.ppermute(array, axis, [(i, (i + step) % count) for i in range(count)])  90.2 us
    all_to_all x6, starting transfers between devices, exchange(): return lax.all_to_all(array, axes, split_axis=0, concat_axis=0, tiled=True)  53.8 us
    ppermute x25, waiting for transfers between devices, shift(): lax.ppermute(array, axis, [(i, (i + step) % count) for i in range(count)])  44.2 us
    all_to_all x6, waiting for transfers between devices, exchange(): return lax.all_to_all(array, axes, split_axis=0, concat_axis=0, tiled=True)  17.5 us
    unnamed x40, local copies, waits for them, and re-layouts  6.08 us
  transfers between devices with their start and end apart: 31, of which 17 were waited for; matrix products, arithmetic and copies ran while one was open for 2% of the time, Pallas kernels for 8%

profile of v6, /device:TPU:1, one launch (start us, length us, event | category | flops | bytes accessed | tf_op | source)
XLA Modules:
  0.0 244.9 jit_solution(3958324123464429919)
XLA Ops:
  0.6 8.9 %collective-permute-start = (s32[1,3]{1,0:T(1,128)}, s32[1,3]{1,0:T(1,128)S(1)}, u32[]{:S(2)}, u32[]{:S(2)}) collective-permute-start(s32[1,3]{1,0:T(1,128)} %own_ref.1), channel_id=1, source_target_pairs={{0,64},{64,0},{1,65},{65,1},{2,66},{66,2},{3,67},{67,3},{4,68},{68... | collective-permute-start | bytes 44 | tf_op jit(solution)/shard_map/ppermute | solution.py:33
  13.3 9.5 %all-to-all-start = ((bf16[16,16,384]{2,1,0:T(8,128)(2,1)}), bf16[16,16,384]{2,1,0:T(8,128)(2,1)S(1)}, u32[]{:S(2)}, u32[]{:S(2)}) async-start(bf16[16,16,384]{2,1,0:T(8,128)(2,1)} %shard_map.93), calls=%async_computation | async-start | bytes 393216 | tf_op jit(solution)/shard_map/all_to_all | solution.py:23
  29.4 9.8 %collective-permute-done.1.f1 = bf16[128,16,128]{2,1,0:T(8,128)(2,1)S(1)} collective-permute-done((bf16[128,16,128]{2,1,0:T(8,128)(2,1)}, bf16[128,16,128]{2,1,0:T(8,128)(2,1)S(1)}, u32[]{:S(2)}, u32[]{:S(2)}) %collective-permute-start.1) | collective-permute-done | bytes 524320 | tf_op jit(solution)/shard_map/ppermute | solution.py:33
  40.1 4.1 %all-to-all-start.1 = ((bf16[4,272,256]{2,1,0:T(8,128)(2,1)}), bf16[4,272,256]{2,1,0:T(8,128)(2,1)S(1)}, u32[]{:S(2)}, u32[]{:S(2)}) async-start(bf16[4,272,256]{2,1,0:T(8,128)(2,1)} %shard_map.94), calls=%async_computation.1 | async-start | bytes 1114112 | tf_op jit(solution)/shard_map/all_to_all | solution.py:23
  52.3 5.1 %collective-permute-done.2.f2a = bf16[64,16,128]{2,1,0:T(8,128)(2,1)S(1)} collective-permute-done((bf16[64,16,128]{2,1,0:T(8,128)(2,1)}, bf16[64,16,128]{2,1,0:T(8,128)(2,1)S(1)}, u32[]{:S(2)}, u32[]{:S(2)}) %collective-permute-start.2) | collective-permute-done | bytes 262176 | tf_op jit(solution)/shard_map/ppermute | solution.py:33
  59.5 4.8 %collective-permute-start.5 = (bf16[64,16,128]{2,1,0:T(8,128)(2,1)S(1)}, bf16[64,16,128]{2,1,0:T(8,128)(2,1)S(1)}, u32[]{:S(2)}, u32[]{:S(2)}) collective-permute-start(bf16[64,16,128]{2,1,0:T(8,128)(2,1)S(1)} %shard_map.96), channel_id=1, source_target_pairs={{0,64},{64,0},{1,65},{65,1},{2,66},{66,2},{3,67},{67,3},{4,68},{68... | collective-permute-start | bytes 786440 | tf_op jit(solution)/shard_map/ppermute | solution.py:33
  67.7 15.0 %all-to-all-start.2 = ((bf16[64,16,384]{2,1,0:T(8,128)(2,1)}), bf16[64,16,384]{2,1,0:T(8,128)(2,1)S(1)}, u32[]{:S(2)}, u32[]{:S(2)}) async-start(bf16[64,16,384]{2,1,0:T(8,128)(2,1)} %shard_map.97), calls=%async_computation.2 | async-start | bytes 1572864 | tf_op jit(solution)/shard_map/all_to_all | solution.py:23
  84.6 3.4 %collective-permute-start.7 = (bf16[1024,256]{1,0:T(8,128)(2,1)S(1)}, bf16[1024,256]{1,0:T(8,128)(2,1)S(1)}, u32[]{:S(2)}, u32[]{:S(2)}) collective-permute-start(bf16[1024,256]{1,0:T(8,128)(2,1)S(1)} %bitcast.18), channel_id=1, source_target_pairs={{0,128},{128,256},{256,384},{384,0},{1,129},{129,257},{257,385},{3... | collective-permute-start | bytes 1572872 | tf_op jit(solution)/shard_map/ppermute | solution.py:33
  90.8 7.0 %collective-permute-done.9.h3 = bf16[1024,256]{1,0:T(8,128)(2,1)S(1)} collective-permute-done((bf16[1024,256]{1,0:T(8,128)(2,1)S(1)}, bf16[1024,256]{1,0:T(8,128)(2,1)S(1)}, u32[]{:S(2)}, u32[]{:S(2)}) %collective-permute-start.9) | collective-permute-done | bytes 524320 | tf_op jit(solution)/shard_map/ppermute | solution.py:33
  97.8 3.4 %collective-permute-start.10 = (bf16[512,256]{1,0:T(8,128)(2,1)S(1)}, bf16[512,256]{1,0:T(8,128)(2,1)S(1)}, u32[]{:S(2)}, u32[]{:S(2)}) collective-permute-start(bf16[512,256]{1,0:T(8,128)(2,1)S(1)} %slice.74), channel_id=1, source_target_pairs={{0,384},{128,0},{256,128},{384,256},{1,385},{129,1},{257,129},{385... | collective-permute-start | bytes 786440 | tf_op jit(solution)/shard_map/ppermute | solution.py:33
  106.4 4.7 %collective-permute-done.8.h2a = bf16[512,256]{1,0:T(8,128)(2,1)S(1)} collective-permute-done((bf16[512,256]{1,0:T(8,128)(2,1)S(1)}, bf16[512,256]{1,0:T(8,128)(2,1)S(1)}, u32[]{:S(2)}, u32[]{:S(2)}) %collective-permute-start.8) | collective-permute-done | bytes 262176 | tf_op jit(solution)/shard_map/ppermute | solution.py:33
  117.4 4.6 %collective-permute-start.12 = (bf16[512,256]{1,0:T(8,128)(2,1)S(1)}, bf16[512,256]{1,0:T(8,128)(2,1)S(1)}, u32[]{:S(2)}, u32[]{:S(2)}) collective-permute-start(bf16[512,256]{1,0:T(8,128)(2,1)S(1)} %get-tuple-element.59), channel_id=1, source_target_pairs={{0,384},{128,0},{256,128},{384,256},{1,385},{129,1},{257,129},{385... | collective-permute-start | bytes 786440 | tf_op jit(solution)/shard_map/ppermute | solution.py:33
  127.1 14.0 %all-to-all-start.3 = ((bf16[64,16,384]{2,1,0:T(8,128)(2,1)}), bf16[64,16,384]{2,1,0:T(8,128)(2,1)S(1)}, u32[]{:S(2)}, u32[]{:S(2)}) async-start(bf16[64,16,384]{2,1,0:T(8,128)(2,1)} %bitcast.10), calls=%async_computation.3 | async-start | bytes 1572864 | tf_op jit(solution)/shard_map/all_to_all | solution.py:23
  143.2 5.0 %collective-permute-start.14 = (bf16[1024,256]{1,0:T(8,128)(2,1)S(1)}, bf16[1024,256]{1,0:T(8,128)(2,1)S(1)}, u32[]{:S(2)}, u32[]{:S(2)}) collective-permute-start(bf16[1024,256]{1,0:T(8,128)(2,1)S(1)} %get-tuple-element.71), channel_id=1, source_target_pairs={{0,384},{128,0},{256,128},{384,256},{1,385},{129,1},{257,129},{385... | collective-permute-start | bytes 1572872 | tf_op jit(solution)/shard_map/ppermute | solution.py:33
  148.2 6.3 %collective-permute-done.13.up_ref = bf16[1024,256]{1,0:T(8,128)(2,1)S(1)} collective-permute-done((bf16[1024,256]{1,0:T(8,128)(2,1)S(1)}, bf16[1024,256]{1,0:T(8,128)(2,1)S(1)}, u32[]{:S(2)}, u32[]{:S(2)}) %collective-permute-start.13) | collective-permute-done | bytes 524320 | tf_op jit(solution)/shard_map/ppermute | solution.py:33
  158.8 4.5 %collective-permute-start.16 = (bf16[256,256]{1,0:T(8,128)(2,1)S(1)}, bf16[256,256]{1,0:T(8,128)(2,1)S(1)}, u32[]{:S(2)}, u32[]{:S(2)}) collective-permute-start(bf16[256,256]{1,0:T(8,128)(2,1)S(1)} %get-tuple-element.74), channel_id=1, source_target_pairs={{0,32},{16,48},{32,0},{48,16},{1,33},{17,49},{33,1},{49,17},{2,34}... | collective-permute-start | bytes 393224 | tf_op jit(solution)/shard_map/ppermute | solution.py:33
  170.7 7.4 %all-to-all-done.3.parts_ref = bf16[64,16,384]{2,1,0:T(8,128)(2,1)S(1)} async-done(((bf16[64,16,384]{2,1,0:T(8,128)(2,1)}), bf16[64,16,384]{2,1,0:T(8,128)(2,1)S(1)}, u32[]{:S(2)}, u32[]{:S(2)}) %all-to-all-start.3) | async-done | bytes 786464 | tf_op jit(solution)/shard_map/all_to_all | solution.py:23
  180.0 5.0 %collective-permute-start.19 = (bf16[49,16,256]{2,1,0:T(8,128)(2,1)S(1)}, bf16[49,16,256]{2,1,0:T(8,128)(2,1)S(1)}, u32[]{:S(2)}, u32[]{:S(2)}) collective-permute-start(bf16[49,16,256]{2,1,0:T(8,128)(2,1)S(1)} %get-tuple-element.77.p0), channel_id=1, source_target_pairs={{0,384},{128,0},{256,128},{384,256},{1,385},{129,1},{257,129},{385... | collective-permute-start | bytes 1204232 | tf_op jit(solution)/shard_map/ppermute | solution.py:33
  186.9 7.6 %all-to-all-start.4 = ((bf16[16,16,256]{2,1,0:T(8,128)(2,1)}), bf16[16,16,256]{2,1,0:T(8,128)(2,1)}, u32[]{:S(2)}, u32[]{:S(2)}) async-start(bf16[16,16,256]{2,1,0:T(8,128)(2,1)} %bitcast.11), calls=%async_computation.4 | async-start | bytes 262144 | tf_op jit(solution)/shard_map/all_to_all | solution.py:23
  197.5 4.6 %collective-permute-start.22 = (bf16[32,16,256]{2,1,0:T(8,128)(2,1)}, bf16[32,16,256]{2,1,0:T(8,128)(2,1)S(1)}, u32[]{:S(2)}, u32[]{:S(2)}) collective-permute-start(bf16[32,16,256]{2,1,0:T(8,128)(2,1)} %get-tuple-element.84), channel_id=1, source_target_pairs={{0,384},{128,0},{256,128},{384,256},{1,385},{129,1},{257,129},{385... | collective-permute-start | bytes 786440 | tf_op jit(solution)/shard_map/ppermute | solution.py:33
  202.1 9.9 %collective-permute-start.20 = (f32[128,1024]{1,0:T(8,128)}, f32[128,1024]{1,0:T(8,128)}, u32[]{:S(2)}, u32[]{:S(2)}) collective-permute-start(f32[128,1024]{1,0:T(8,128)} %copy-done.18), channel_id=1, source_target_pairs={{0,64},{64,0},{1,65},{65,1},{2,66},{66,2},{3,67},{67,3},{4,68},{68... | collective-permute-start | bytes 1572872 | tf_op jit(solution)/shard_map/ppermute | solution.py:33
  213.1 4.6 %shard_map.105.before_ref = f32[264,16,128]{2,1,0:T(8,128)S(1)} custom-call(s32[4]{0:T(128)S(1)} %pad_add_fusion.where_ref, s32[3,16,64]{2,1,0:T(8,128)S(1)} %maximum_convert_fusion.ids_ref, bf16[49,16,256]{2,1,0:T(8,128)(2,1)S(1)} %copy-done.13, bf16[49,16,256]{2,1,0:T(8,128)(2,1)S(1)} %collective-permute-done.18.r1.p1, ...), custom_call_target="tpu_custom_call" | custom-call | flops 1000000 | bytes 1000000 | tf_op jit(solution)/shard_map/pallas_call | solution.py:544
  229.5 3.5 %all-to-all-start.5 = ((bf16[8,9,16,256]{3,2,1,0:T(8,128)(2,1)}), bf16[8,9,16,256]{3,2,1,0:T(8,128)(2,1)S(1)}, u32[]{:S(2)}, u32[]{:S(2)}) async-start(bf16[8,9,16,256]{3,2,1,0:T(8,128)(2,1)} %shard_map.107), calls=%async_computation.5 | async-start | bytes 1179648 | tf_op jit(solution)/shard_map/all_to_all | solution.py:23
  234.8 8.3 %all-to-all-done.5.total_ref = bf16[8,9,16,256]{3,2,1,0:T(8,128)(2,1)S(1)} async-done(((bf16[8,9,16,256]{3,2,1,0:T(8,128)(2,1)}), bf16[8,9,16,256]{3,2,1,0:T(8,128)(2,1)S(1)}, u32[]{:S(2)}, u32[]{:S(2)}) %all-to-all-start.5) | async-done | bytes 589856 | tf_op jit(solution)/shard_map/all_to_all | solution.py:23
  (113 shorter events, 82.6 us)
Async XLA Ops:
  0.6 9.9 %collective-permute-start = (s32[1,3]{1,0:T(1,128)}, s32[1,3]{1,0:T(1,128)S(1)}, u32[]{:S(2)}, u32[]{:S(2)}) collective-permute-start(s32[1,3]{1,0:T(1,128)} %own_ref.1), channel_id=1, source_target_pairs={{0,64},{64,0},{1,65},{65,1},{2,66},{66,2},{3,67},{67,3},{4,68},{68... | collective-permute-start | bytes 44 | tf_op jit(solution)/shard_map/ppermute | solution.py:33
  13.3 25.9 %all-to-all-start = ((bf16[16,16,384]{2,1,0:T(8,128)(2,1)}), bf16[16,16,384]{2,1,0:T(8,128)(2,1)S(1)}, u32[]{:S(2)}, u32[]{:S(2)}) async-start(bf16[16,16,384]{2,1,0:T(8,128)(2,1)} %shard_map.93), calls=%async_computation | async-start | bytes 393216 | tf_op jit(solution)/shard_map/all_to_all | solution.py:23
  22.8 16.4 %collective-permute-start.1 = (bf16[128,16,128]{2,1,0:T(8,128)(2,1)}, bf16[128,16,128]{2,1,0:T(8,128)(2,1)S(1)}, u32[]{:S(2)}, u32[]{:S(2)}) collective-permute-start(bf16[128,16,128]{2,1,0:T(8,128)(2,1)} %f0.3), channel_id=1, source_target_pairs={{0,128},{128,256},{256,384},{384,0},{1,129},{129,257},{257,385},{3... | collective-permute-start | bytes 1572872 | tf_op jit(solution)/shard_map/ppermute | solution.py:33
  26.1 18.2 %collective-permute-start.3 = (bf16[128,16,128]{2,1,0:T(8,128)(2,1)}, bf16[128,16,128]{2,1,0:T(8,128)(2,1)S(1)}, u32[]{:S(2)}, u32[]{:S(2)}) collective-permute-start(bf16[128,16,128]{2,1,0:T(8,128)(2,1)} %f0.3), channel_id=1, source_target_pairs={{0,384},{128,0},{256,128},{384,256},{1,385},{129,1},{257,129},{385... | collective-permute-start | bytes 1572872 | tf_op jit(solution)/shard_map/ppermute | solution.py:33
  40.1 12.1 %all-to-all-start.1 = ((bf16[4,272,256]{2,1,0:T(8,128)(2,1)}), bf16[4,272,256]{2,1,0:T(8,128)(2,1)S(1)}, u32[]{:S(2)}, u32[]{:S(2)}) async-start(bf16[4,272,256]{2,1,0:T(8,128)(2,1)} %shard_map.94), calls=%async_computation.1 | async-start | bytes 1114112 | tf_op jit(solution)/shard_map/all_to_all | solution.py:23
  48.2 9.1 %collective-permute-start.2 = (bf16[64,16,128]{2,1,0:T(8,128)(2,1)}, bf16[64,16,128]{2,1,0:T(8,128)(2,1)S(1)}, u32[]{:S(2)}, u32[]{:S(2)}) collective-permute-start(bf16[64,16,128]{2,1,0:T(8,128)(2,1)} %slice.54), channel_id=1, source_target_pairs={{0,128},{128,256},{256,384},{384,0},{1,129},{129,257},{257,385},{3... | collective-permute-start | bytes 786440 | tf_op jit(solution)/shard_map/ppermute | solution.py:33
  67.7 57.6 %all-to-all-start.2 = ((bf16[64,16,384]{2,1,0:T(8,128)(2,1)}), bf16[64,16,384]{2,1,0:T(8,128)(2,1)S(1)}, u32[]{:S(2)}, u32[]{:S(2)}) async-start(bf16[64,16,384]{2,1,0:T(8,128)(2,1)} %shard_map.97), calls=%async_computation.2 | async-start | bytes 1572864 | tf_op jit(solution)/shard_map/all_to_all | solution.py:23
  82.7 15.1 %collective-permute-start.9 = (bf16[1024,256]{1,0:T(8,128)(2,1)S(1)}, bf16[1024,256]{1,0:T(8,128)(2,1)S(1)}, u32[]{:S(2)}, u32[]{:S(2)}) collective-permute-start(bf16[1024,256]{1,0:T(8,128)(2,1)S(1)} %bitcast.17), channel_id=1, source_target_pairs={{0,384},{128,0},{256,128},{384,256},{1,385},{129,1},{257,129},{385... | collective-permute-start | bytes 1572872 | tf_op jit(solution)/shard_map/ppermute | solution.py:33
  84.6 16.7 %collective-permute-start.7 = (bf16[1024,256]{1,0:T(8,128)(2,1)S(1)}, bf16[1024,256]{1,0:T(8,128)(2,1)S(1)}, u32[]{:S(2)}, u32[]{:S(2)}) collective-permute-start(bf16[1024,256]{1,0:T(8,128)(2,1)S(1)} %bitcast.18), channel_id=1, source_target_pairs={{0,128},{128,256},{256,384},{384,0},{1,129},{129,257},{257,385},{3... | collective-permute-start | bytes 1572872 | tf_op jit(solution)/shard_map/ppermute | solution.py:33
  88.1 15.2 %collective-permute-start.6 = (bf16[256,1024]{1,0:T(8,128)(2,1)S(1)}, bf16[256,1024]{1,0:T(8,128)(2,1)S(1)}, u32[]{:S(2)}, u32[]{:S(2)}) collective-permute-start(bf16[256,1024]{1,0:T(8,128)(2,1)S(1)} %pad_maximum_fusion), channel_id=1, source_target_pairs={{0,64},{64,0},{1,65},{65,1},{2,66},{66,2},{3,67},{67,3},{4,68},{68... | collective-permute-start | bytes 1572872 | tf_op jit(solution)/shard_map/ppermute | solution.py:33
  101.3 9.8 %collective-permute-start.8 = (bf16[512,256]{1,0:T(8,128)(2,1)S(1)}, bf16[512,256]{1,0:T(8,128)(2,1)S(1)}, u32[]{:S(2)}, u32[]{:S(2)}) collective-permute-start(bf16[512,256]{1,0:T(8,128)(2,1)S(1)} %slice.73), channel_id=1, source_target_pairs={{0,128},{128,256},{256,384},{384,0},{1,129},{129,257},{257,385},{3... | collective-permute-start | bytes 786440 | tf_op jit(solution)/shard_map/ppermute | solution.py:33
  115.5 8.9 %collective-permute-start.11 = (bf16[512,256]{1,0:T(8,128)(2,1)S(1)}, bf16[512,256]{1,0:T(8,128)(2,1)S(1)}, u32[]{:S(2)}, u32[]{:S(2)}) collective-permute-start(bf16[512,256]{1,0:T(8,128)(2,1)S(1)} %get-tuple-element.58), channel_id=1, source_target_pairs={{0,128},{128,256},{256,384},{384,0},{1,129},{129,257},{257,385},{3... | collective-permute-start | bytes 786440 | tf_op jit(solution)/shard_map/ppermute | solution.py:33
  127.1 51.0 %all-to-all-start.3 = ((bf16[64,16,384]{2,1,0:T(8,128)(2,1)}), bf16[64,16,384]{2,1,0:T(8,128)(2,1)S(1)}, u32[]{:S(2)}, u32[]{:S(2)}) async-start(bf16[64,16,384]{2,1,0:T(8,128)(2,1)} %bitcast.10), calls=%async_computation.3 | async-start | bytes 1572864 | tf_op jit(solution)/shard_map/all_to_all | solution.py:23
  141.3 13.2 %collective-permute-start.13 = (bf16[1024,256]{1,0:T(8,128)(2,1)S(1)}, bf16[1024,256]{1,0:T(8,128)(2,1)S(1)}, u32[]{:S(2)}, u32[]{:S(2)}) collective-permute-start(bf16[1024,256]{1,0:T(8,128)(2,1)S(1)} %get-tuple-element.69), channel_id=1, source_target_pairs={{0,128},{128,256},{256,384},{384,0},{1,129},{129,257},{257,385},{3... | collective-permute-start | bytes 1572872 | tf_op jit(solution)/shard_map/ppermute | solution.py:33
  143.2 12.2 %collective-permute-start.14 = (bf16[1024,256]{1,0:T(8,128)(2,1)S(1)}, bf16[1024,256]{1,0:T(8,128)(2,1)S(1)}, u32[]{:S(2)}, u32[]{:S(2)}) collective-permute-start(bf16[1024,256]{1,0:T(8,128)(2,1)S(1)} %get-tuple-element.71), channel_id=1, source_target_pairs={{0,384},{128,0},{256,128},{384,256},{1,385},{129,1},{257,129},{385... | collective-permute-start | bytes 1572872 | tf_op jit(solution)/shard_map/ppermute | solution.py:33
  156.2 10.2 %collective-permute-start.15 = (bf16[256,256]{1,0:T(8,128)(2,1)S(1)}, bf16[256,256]{1,0:T(8,128)(2,1)S(1)}, u32[]{:S(2)}, u32[]{:S(2)}) collective-permute-start(bf16[256,256]{1,0:T(8,128)(2,1)S(1)} %get-tuple-element.73), channel_id=1, source_target_pairs={{0,16},{16,32},{32,48},{48,0},{1,17},{17,33},{33,49},{49,1},{2,18}... | collective-permute-start | bytes 393224 | tf_op jit(solution)/shard_map/ppermute | solution.py:33
  180.0 14.5 %collective-permute-start.19 = (bf16[49,16,256]{2,1,0:T(8,128)(2,1)S(1)}, bf16[49,16,256]{2,1,0:T(8,128)(2,1)S(1)}, u32[]{:S(2)}, u32[]{:S(2)}) collective-permute-start(bf16[49,16,256]{2,1,0:T(8,128)(2,1)S(1)} %get-tuple-element.77.p0), channel_id=1, source_target_pairs={{0,384},{128,0},{256,128},{384,256},{1,385},{129,1},{257,129},{385... | collective-permute-start | bytes 1204232 | tf_op jit(solution)/shard_map/ppermute | solution.py:33
  185.0 9.8 %collective-permute-start.18 = (bf16[49,16,256]{2,1,0:T(8,128)(2,1)S(1)}, bf16[49,16,256]{2,1,0:T(8,128)(2,1)S(1)}, u32[]{:S(2)}, u32[]{:S(2)}) collective-permute-start(bf16[49,16,256]{2,1,0:T(8,128)(2,1)S(1)} %get-tuple-element.77.p0), channel_id=1, source_target_pairs={{0,128},{128,256},{256,384},{384,0},{1,129},{129,257},{257,385},{3... | collective-permute-start | bytes 1204232 | tf_op jit(solution)/shard_map/ppermute | solution.py:33
  186.9 30.9 %all-to-all-start.4 = ((bf16[16,16,256]{2,1,0:T(8,128)(2,1)}), bf16[16,16,256]{2,1,0:T(8,128)(2,1)}, u32[]{:S(2)}, u32[]{:S(2)}) async-start(bf16[16,16,256]{2,1,0:T(8,128)(2,1)} %bitcast.11), calls=%async_computation.4 | async-start | bytes 262144 | tf_op jit(solution)/shard_map/all_to_all | solution.py:23
  195.6 22.1 %collective-permute-start.21 = (bf16[33,16,256]{2,1,0:T(8,128)(2,1)}, bf16[33,16,256]{2,1,0:T(8,128)(2,1)S(1)}, u32[]{:S(2)}, u32[]{:S(2)}) collective-permute-start(bf16[33,16,256]{2,1,0:T(8,128)(2,1)} %get-tuple-element.80), channel_id=1, source_target_pairs={{0,128},{128,256},{256,384},{384,0},{1,129},{129,257},{257,385},{3... | collective-permute-start | bytes 811016 | tf_op jit(solution)/shard_map/ppermute | solution.py:33
  197.5 20.2 %collective-permute-start.22 = (bf16[32,16,256]{2,1,0:T(8,128)(2,1)}, bf16[32,16,256]{2,1,0:T(8,128)(2,1)S(1)}, u32[]{:S(2)}, u32[]{:S(2)}) collective-permute-start(bf16[32,16,256]{2,1,0:T(8,128)(2,1)} %get-tuple-element.84), channel_id=1, source_target_pairs={{0,384},{128,0},{256,128},{384,256},{1,385},{129,1},{257,129},{385... | collective-permute-start | bytes 786440 | tf_op jit(solution)/shard_map/ppermute | solution.py:33
  202.1 30.9 %collective-permute-start.20 = (f32[128,1024]{1,0:T(8,128)}, f32[128,1024]{1,0:T(8,128)}, u32[]{:S(2)}, u32[]{:S(2)}) collective-permute-start(f32[128,1024]{1,0:T(8,128)} %copy-done.18), channel_id=1, source_target_pairs={{0,64},{64,0},{1,65},{65,1},{2,66},{66,2},{3,67},{67,3},{4,68},{68... | collective-permute-start | bytes 1572872 | tf_op jit(solution)/shard_map/ppermute | solution.py:33
  227.1 16.9 %collective-permute-start.24 = (bf16[64,16,256]{2,1,0:T(8,128)(2,1)}, bf16[64,16,256]{2,1,0:T(8,128)(2,1)S(1)}, u32[]{:S(2)}, u32[]{:S(2)}) collective-permute-start(bf16[64,16,256]{2,1,0:T(8,128)(2,1)} %get-tuple-element.97), channel_id=1, source_target_pairs={{0,64},{64,0},{1,65},{65,1},{2,66},{66,2},{3,67},{67,3},{4,68},{68... | collective-permute-start | bytes 1572872 | tf_op jit(solution)/shard_map/ppermute | solution.py:33
  229.5 13.7 %all-to-all-start.5 = ((bf16[8,9,16,256]{3,2,1,0:T(8,128)(2,1)}), bf16[8,9,16,256]{3,2,1,0:T(8,128)(2,1)S(1)}, u32[]{:S(2)}, u32[]{:S(2)}) async-start(bf16[8,9,16,256]{3,2,1,0:T(8,128)(2,1)} %shard_map.107), calls=%async_computation.5 | async-start | bytes 1179648 | tf_op jit(solution)/shard_map/all_to_all | solution.py:23
  (27 other events, 381.5 us)

commit v7 on v6

--- a/solution.py
+++ b/solution.py
@@ -374,13 +374,17 @@
     leave_ref[:, :, 128:] = sums_ref[owned + half : 2 * owned].astype(BF16)
 
 
+def coarse_done_kernel(coarse_ref, out_ref):
+    coarse = coarse_ref[0].astype(F32)
+    for z in range(1, Z):
+        coarse = coarse + coarse_ref[z].astype(F32)
+    out_ref[...] = coarse.astype(BF16)
+
+
 def done_kernel(kept_ref, arrived_ref, coarse_ref, out_ref):
     share = kept_ref.shape[0]
     middle = (kept_ref[...] + arrived_ref[...].astype(F32)).astype(BF16)
-    coarse = coarse_ref[0].astype(F32)
-    for z in range(1, Z):
-        coarse = coarse + coarse_ref[z].astype(F32)
-    coarse = coarse.astype(BF16)
+    coarse = coarse_ref[...]
     for g in range(out_ref.shape[0]):
         out_ref[g, :share] = middle
         out_ref[g, share] = coarse
@@ -427,16 +431,17 @@
     )(where, path, other_path, coarse_weights)
     packets = exchange(packet, "z")
 
-    fine_one = shift(after(fine_weights, packet), "y", 1)
+    fine_one = shift(fine_weights, "y", 1)
     fine_three = shift(after(fine_weights, packet), "y", 3)
-    packets, fine_one = lax.optimization_barrier((packets, fine_one))
+    split = fine_owned // 2
+    fine_two = shift(fine_one[:split], "y", 1)
+    packets, fine_one, fine_two, fine_three = lax.optimization_barrier((packets, fine_one, fine_two, fine_three))
     packets = kernel_call(repack_kernel, [VMEM], bf16(X, Z * ROWS + ROWS, half))(packets)
     packets = exchange(packets, "x")
-    split = fine_owned // 2
     fine_rows = [
         fine_weights,
         fine_one,
-        shift(fine_one[:split], "y", 1),
+        fine_two,
         fine_three,
         shift(fine_three[split:], "y", 3),
     ]
@@ -513,7 +518,8 @@
     for s in range(1, X):
         column_sum = column_sum + shift(leaving[s - 1], "x", s).astype(F32)
     column_sum = column_sum.astype(BF16).reshape(Z, ROWS, half)
-    parts, column_sum = lax.optimization_barrier((parts, column_sum))
+    other_back = shift(after(other_back, column_sum), "c", 1)
+    parts, column_sum, other_back = lax.optimization_barrier((parts, column_sum, other_back))
 
     middle_count = middle_weights.shape[0]
     pairs = MEMBERS // 2
@@ -561,9 +567,10 @@
         (bf16(fine_owned // 2, ROWS, 2 * fine_width), f32(fine_owned, ROWS, fine_width)),
         [pltpu.VMEM((C * fine_owned + 8, ROWS, fine_width), F32)],
     )(where, q1[lower, :Z, : LANES * C * X].astype(I32)[None], fine_sums, q1, q3)
+    coarse_done = kernel_call(coarse_done_kernel, [VMEM], bf16(ROWS, half))(coarse_four)
     done = kernel_call(
         done_kernel, [VMEM] * 3, bf16(Y * C, share + 1, ROWS, middle_width)
-    )(middle_kept, middle_arrived, coarse_four)
+    )(middle_kept, middle_arrived, coarse_done)
     total = exchange(done, ("y", "c"))
     fine_arrived = shift(after(fine_leave, done), "c", 1)
     coarse_total, middle_total = kernel_call(
@@ -572,7 +579,6 @@
     fine_total = kernel_call(
         finish_kernel, [VMEM] * 2, bf16(fine_owned, ROWS, fine_width)
     )(fine_kept, fine_arrived)
-    other_back = shift(after(other_back, second[0]), "c", 1)
     tokens_grad = (coarse_back + other_back + back).astype(BF16)
     return (tokens_grad, coarse_total, middle_total, fine_total)
 

time: 246 us -> 246 us (level)
  waiting for transfers between devices: 61.8 us -> 50.7 us
  starting transfers between devices: 144 us -> 154 us
    all_to_all x6, waiting for transfers between devices: 17.5 us -> 11.5 us  [exchange(): return lax.all_to_all(array, axes, split_axis=0, concat_axis=0, tiled=True)]
    all_to_all x6, starting transfers between devices: 53.8 us -> 59.7 us  [exchange(): return lax.all_to_all(array, axes, split_axis=0, concat_axis=0, tiled=True)]
    ppermute x25, waiting for transfers between devices: 44.2 us -> 39.2 us  [shift(): lax.ppermute(array, axis, [(i, (i + step) % count) for i in range(count)])]
    ppermute x25, starting transfers between devices: 90.2 us -> 94.5 us  [shift(): lax.ppermute(array, axis, [(i, (i + step) % count) for i in range(count)])]
    unnamed x40 -> x42, local copies, waits for them, and re-layouts: 6.08 us -> 6.88 us
  transfers between devices with their start and end apart: 31 -> 31, of which waited for: 17 -> 14; matrix products, arithmetic and copies ran while one was open for 2% -> 1% of each run, Pallas kernels for 8% -> 7%
where the time goes in v7:
time: 246 us; the launch traced here: 244 us
  starting transfers between devices  154 us (63%)
  waiting for transfers between devices  50.7 us (21%)
  Pallas kernels  27.4 us (11%)
  local copies, waits for them, and re-layouts  7.78 us (3%)
  other arithmetic  2.71 us (1%)
    ppermute x25, starting transfers between devices, shift(): lax.ppermute(array, axis, [(i, (i + step) % count) for i in range(count)])  94.5 us
    all_to_all x6, starting transfers between devices, exchange(): return lax.all_to_all(array, axes, split_axis=0, concat_axis=0, tiled=True)  59.7 us
    ppermute x25, waiting for transfers between devices, shift(): lax.ppermute(array, axis, [(i, (i + step) % count) for i in range(count)])  39.2 us
    all_to_all x6, waiting for transfers between devices, exchange(): return lax.all_to_all(array, axes, split_axis=0, concat_axis=0, tiled=True)  11.5 us
    unnamed x42, local copies, waits for them, and re-layouts  6.88 us
  transfers between devices with their start and end apart: 31, of which 14 were waited for; matrix products, arithmetic and copies ran while one was open for 1% of the time, Pallas kernels for 7%

profile of v7, /device:TPU:1, one launch (start us, length us, event | category | flops | bytes accessed | tf_op | source)
XLA Modules:
  0.0 244.1 jit_solution(12255223558278553211)
XLA Ops:
  0.6 8.9 %collective-permute-start = (s32[1,3]{1,0:T(1,128)}, s32[1,3]{1,0:T(1,128)S(1)}, u32[]{:S(2)}, u32[]{:S(2)}) collective-permute-start(s32[1,3]{1,0:T(1,128)} %own_ref.1), channel_id=1, source_target_pairs={{0,64},{64,0},{1,65},{65,1},{2,66},{66,2},{3,67},{67,3},{4,68},{68... | collective-permute-start | bytes 44 | tf_op jit(solution)/shard_map/ppermute | solution.py:33
  14.4 10.8 %all-to-all-start = ((bf16[16,16,384]{2,1,0:T(8,128)(2,1)}), bf16[16,16,384]{2,1,0:T(8,128)(2,1)S(1)}, u32[]{:S(2)}, u32[]{:S(2)}) async-start(bf16[16,16,384]{2,1,0:T(8,128)(2,1)} %shard_map.93), calls=%async_computation | async-start | bytes 393216 | tf_op jit(solution)/shard_map/all_to_all | solution.py:23
  30.6 9.7 %collective-permute-done.3.f3 = bf16[128,16,128]{2,1,0:T(8,128)(2,1)S(1)} collective-permute-done((bf16[128,16,128]{2,1,0:T(8,128)(2,1)}, bf16[128,16,128]{2,1,0:T(8,128)(2,1)S(1)}, u32[]{:S(2)}, u32[]{:S(2)}) %collective-permute-start.3) | collective-permute-done | bytes 524320 | tf_op jit(solution)/shard_map/ppermute | solution.py:33
  41.1 4.1 %all-to-all-start.1 = ((bf16[4,272,256]{2,1,0:T(8,128)(2,1)}), bf16[4,272,256]{2,1,0:T(8,128)(2,1)S(1)}, u32[]{:S(2)}, u32[]{:S(2)}) async-start(bf16[4,272,256]{2,1,0:T(8,128)(2,1)} %shard_map.94), calls=%async_computation.1 | async-start | bytes 1114112 | tf_op jit(solution)/shard_map/all_to_all | solution.py:23
  45.3 4.6 %collective-permute-start.4 = (bf16[64,16,128]{2,1,0:T(8,128)(2,1)S(1)}, bf16[64,16,128]{2,1,0:T(8,128)(2,1)S(1)}, u32[]{:S(2)}, u32[]{:S(2)}) collective-permute-start(bf16[64,16,128]{2,1,0:T(8,128)(2,1)S(1)} %slice.55), channel_id=1, source_target_pairs={{0,384},{128,0},{256,128},{384,256},{1,385},{129,1},{257,129},{385... | collective-permute-start | bytes 786440 | tf_op jit(solution)/shard_map/ppermute | solution.py:33
  56.0 4.5 %collective-permute-start.5 = (bf16[64,16,128]{2,1,0:T(8,128)(2,1)S(1)}, bf16[64,16,128]{2,1,0:T(8,128)(2,1)S(1)}, u32[]{:S(2)}, u32[]{:S(2)}) collective-permute-start(bf16[64,16,128]{2,1,0:T(8,128)(2,1)S(1)} %shard_map.96), channel_id=1, source_target_pairs={{0,64},{64,0},{1,65},{65,1},{2,66},{66,2},{3,67},{67,3},{4,68},{68... | collective-permute-start | bytes 786440 | tf_op jit(solution)/shard_map/ppermute | solution.py:33
  63.8 14.7 %all-to-all-start.2 = ((bf16[64,16,384]{2,1,0:T(8,128)(2,1)}), bf16[64,16,384]{2,1,0:T(8,128)(2,1)S(1)}, u32[]{:S(2)}, u32[]{:S(2)}) async-start(bf16[64,16,384]{2,1,0:T(8,128)(2,1)} %shard_map.97), calls=%async_computation.2 | async-start | bytes 1572864 | tf_op jit(solution)/shard_map/all_to_all | solution.py:23
  78.6 5.3 %collective-permute-start.9 = (bf16[1024,256]{1,0:T(8,128)(2,1)S(1)}, bf16[1024,256]{1,0:T(8,128)(2,1)S(1)}, u32[]{:S(2)}, u32[]{:S(2)}) collective-permute-start(bf16[1024,256]{1,0:T(8,128)(2,1)S(1)} %bitcast.17), channel_id=1, source_target_pairs={{0,384},{128,0},{256,128},{384,256},{1,385},{129,1},{257,129},{385... | collective-permute-start | bytes 1572872 | tf_op jit(solution)/shard_map/ppermute | solution.py:33
  88.4 6.5 %collective-permute-done.9.h3 = bf16[1024,256]{1,0:T(8,128)(2,1)S(1)} collective-permute-done((bf16[1024,256]{1,0:T(8,128)(2,1)S(1)}, bf16[1024,256]{1,0:T(8,128)(2,1)S(1)}, u32[]{:S(2)}, u32[]{:S(2)}) %collective-permute-start.9) | collective-permute-done | bytes 524320 | tf_op jit(solution)/shard_map/ppermute | solution.py:33
  95.0 5.3 %collective-permute-start.10 = (bf16[512,256]{1,0:T(8,128)(2,1)S(1)}, bf16[512,256]{1,0:T(8,128)(2,1)S(1)}, u32[]{:S(2)}, u32[]{:S(2)}) collective-permute-start(bf16[512,256]{1,0:T(8,128)(2,1)S(1)} %slice.74), channel_id=1, source_target_pairs={{0,384},{128,0},{256,128},{384,256},{1,385},{129,1},{257,129},{385... | collective-permute-start | bytes 786440 | tf_op jit(solution)/shard_map/ppermute | solution.py:33
  104.7 5.1 %collective-permute-done.8.h2a = bf16[512,256]{1,0:T(8,128)(2,1)S(1)} collective-permute-done((bf16[512,256]{1,0:T(8,128)(2,1)S(1)}, bf16[512,256]{1,0:T(8,128)(2,1)S(1)}, u32[]{:S(2)}, u32[]{:S(2)}) %collective-permute-start.8) | collective-permute-done | bytes 262176 | tf_op jit(solution)/shard_map/ppermute | solution.py:33
  116.8 4.6 %collective-permute-start.12 = (bf16[512,256]{1,0:T(8,128)(2,1)S(1)}, bf16[512,256]{1,0:T(8,128)(2,1)S(1)}, u32[]{:S(2)}, u32[]{:S(2)}) collective-permute-start(bf16[512,256]{1,0:T(8,128)(2,1)S(1)} %get-tuple-element.63), channel_id=1, source_target_pairs={{0,384},{128,0},{256,128},{384,256},{1,385},{129,1},{257,129},{385... | collective-permute-start | bytes 786440 | tf_op jit(solution)/shard_map/ppermute | solution.py:33
  126.5 14.1 %all-to-all-start.3 = ((bf16[64,16,384]{2,1,0:T(8,128)(2,1)}), bf16[64,16,384]{2,1,0:T(8,128)(2,1)S(1)}, u32[]{:S(2)}, u32[]{:S(2)}) async-start(bf16[64,16,384]{2,1,0:T(8,128)(2,1)} %bitcast.10), calls=%async_computation.3 | async-start | bytes 1572864 | tf_op jit(solution)/shard_map/all_to_all | solution.py:23
  142.7 5.0 %collective-permute-start.14 = (bf16[1024,256]{1,0:T(8,128)(2,1)S(1)}, bf16[1024,256]{1,0:T(8,128)(2,1)S(1)}, u32[]{:S(2)}, u32[]{:S(2)}) collective-permute-start(bf16[1024,256]{1,0:T(8,128)(2,1)S(1)} %get-tuple-element.74), channel_id=1, source_target_pairs={{0,384},{128,0},{256,128},{384,256},{1,385},{129,1},{257,129},{385... | collective-permute-start | bytes 1572872 | tf_op jit(solution)/shard_map/ppermute | solution.py:33
  147.7 5.9 %collective-permute-done.13.up_ref = bf16[1024,256]{1,0:T(8,128)(2,1)S(1)} collective-permute-done((bf16[1024,256]{1,0:T(8,128)(2,1)S(1)}, bf16[1024,256]{1,0:T(8,128)(2,1)S(1)}, u32[]{:S(2)}, u32[]{:S(2)}) %collective-permute-start.13) | collective-permute-done | bytes 524320 | tf_op jit(solution)/shard_map/ppermute | solution.py:33
  158.0 4.5 %collective-permute-start.16 = (bf16[256,256]{1,0:T(8,128)(2,1)S(1)}, bf16[256,256]{1,0:T(8,128)(2,1)S(1)}, u32[]{:S(2)}, u32[]{:S(2)}) collective-permute-start(bf16[256,256]{1,0:T(8,128)(2,1)S(1)} %get-tuple-element.77), channel_id=1, source_target_pairs={{0,32},{16,48},{32,0},{48,16},{1,33},{17,49},{33,1},{49,17},{2,34}... | collective-permute-start | bytes 393224 | tf_op jit(solution)/shard_map/ppermute | solution.py:33
  169.9 8.6 %collective-permute-start.18 = (f32[128,1024]{1,0:T(8,128)S(1)}, f32[128,1024]{1,0:T(8,128)}, u32[]{:S(2)}, u32[]{:S(2)}) collective-permute-start(f32[128,1024]{1,0:T(8,128)S(1)} %copy-done.19), channel_id=1, source_target_pairs={{0,64},{64,0},{1,65},{65,1},{2,66},{66,2},{3,67},{67,3},{4,68},{68... | collective-permute-start | bytes 1572872 | tf_op jit(solution)/shard_map/ppermute | solution.py:33
  182.1 5.3 %collective-permute-start.20 = (bf16[49,16,256]{2,1,0:T(8,128)(2,1)S(1)}, bf16[49,16,256]{2,1,0:T(8,128)(2,1)S(1)}, u32[]{:S(2)}, u32[]{:S(2)}) collective-permute-start(bf16[49,16,256]{2,1,0:T(8,128)(2,1)S(1)} %get-tuple-element.86.p0), channel_id=1, source_target_pairs={{0,384},{128,0},{256,128},{384,256},{1,385},{129,1},{257,129},{385... | collective-permute-start | bytes 1204232 | tf_op jit(solution)/shard_map/ppermute | solution.py:33
  189.4 11.4 %all-to-all-start.4 = ((bf16[16,16,256]{2,1,0:T(8,128)(2,1)}), bf16[16,16,256]{2,1,0:T(8,128)(2,1)}, u32[]{:S(2)}, u32[]{:S(2)}) async-start(bf16[16,16,256]{2,1,0:T(8,128)(2,1)} %bitcast.11), calls=%async_computation.4 | async-start | bytes 262144 | tf_op jit(solution)/shard_map/all_to_all | solution.py:23
  203.6 4.6 %collective-permute-start.22 = (bf16[32,16,256]{2,1,0:T(8,128)(2,1)}, bf16[32,16,256]{2,1,0:T(8,128)(2,1)S(1)}, u32[]{:S(2)}, u32[]{:S(2)}) collective-permute-start(bf16[32,16,256]{2,1,0:T(8,128)(2,1)} %get-tuple-element.90), channel_id=1, source_target_pairs={{0,384},{128,0},{256,128},{384,256},{1,385},{129,1},{257,129},{385... | collective-permute-start | bytes 786440 | tf_op jit(solution)/shard_map/ppermute | solution.py:33
  209.2 4.6 %shard_map.104.before_ref = f32[264,16,128]{2,1,0:T(8,128)S(1)} custom-call(s32[4]{0:T(128)S(1)} %pad_add_fusion.where_ref, s32[3,16,64]{2,1,0:T(8,128)S(1)} %maximum_convert_fusion.ids_ref, bf16[49,16,256]{2,1,0:T(8,128)(2,1)S(1)} %copy-done.13, bf16[49,16,256]{2,1,0:T(8,128)(2,1)S(1)} %collective-permute-done.19.p1.r1, ...), custom_call_target="tpu_custom_call" | custom-call | flops 1000000 | bytes 1000000 | tf_op jit(solution)/shard_map/pallas_call | solution.py:550
  215.4 4.5 %collective-permute-start.23 = (bf16[8,16,256]{2,1,0:T(8,128)(2,1)S(1)}, bf16[8,16,256]{2,1,0:T(8,128)(2,1)S(1)}, u32[]{:S(2)}, u32[]{:S(2)}) collective-permute-start(bf16[8,16,256]{2,1,0:T(8,128)(2,1)S(1)} %get-tuple-element.96), channel_id=1, source_target_pairs={{0,64},{64,0},{1,65},{65,1},{2,66},{66,2},{3,67},{67,3},{4,68},{68... | collective-permute-start | bytes 196616 | tf_op jit(solution)/shard_map/ppermute | solution.py:33
  227.6 4.6 %all-to-all-start.5 = ((bf16[8,9,16,256]{3,2,1,0:T(8,128)(2,1)}), bf16[8,9,16,256]{3,2,1,0:T(8,128)(2,1)S(1)}, u32[]{:S(2)}, u32[]{:S(2)}) async-start(bf16[8,9,16,256]{3,2,1,0:T(8,128)(2,1)} %shard_map.108), calls=%async_computation.5 | async-start | bytes 1179648 | tf_op jit(solution)/shard_map/all_to_all | solution.py:23
  234.1 8.3 %all-to-all-done.5.total_ref = bf16[8,9,16,256]{3,2,1,0:T(8,128)(2,1)S(1)} async-done(((bf16[8,9,16,256]{3,2,1,0:T(8,128)(2,1)}), bf16[8,9,16,256]{3,2,1,0:T(8,128)(2,1)S(1)}, u32[]{:S(2)}, u32[]{:S(2)}) %all-to-all-start.5) | async-done | bytes 589856 | tf_op jit(solution)/shard_map/all_to_all | solution.py:23
  (116 shorter events, 77.2 us)
Async XLA Ops:
  0.6 10.9 %collective-permute-start = (s32[1,3]{1,0:T(1,128)}, s32[1,3]{1,0:T(1,128)S(1)}, u32[]{:S(2)}, u32[]{:S(2)}) collective-permute-start(s32[1,3]{1,0:T(1,128)} %own_ref.1), channel_id=1, source_target_pairs={{0,64},{64,0},{1,65},{65,1},{2,66},{66,2},{3,67},{67,3},{4,68},{68... | collective-permute-start | bytes 44 | tf_op jit(solution)/shard_map/ppermute | solution.py:33
  9.6 19.0 %collective-permute-start.1 = (bf16[128,16,128]{2,1,0:T(8,128)(2,1)}, bf16[128,16,128]{2,1,0:T(8,128)(2,1)S(1)}, u32[]{:S(2)}, u32[]{:S(2)}) collective-permute-start(bf16[128,16,128]{2,1,0:T(8,128)(2,1)} %f0.3), channel_id=1, source_target_pairs={{0,128},{128,256},{256,384},{384,0},{1,129},{129,257},{257,385},{3... | collective-permute-start | bytes 1572872 | tf_op jit(solution)/shard_map/ppermute | solution.py:33
  14.4 25.9 %all-to-all-start = ((bf16[16,16,384]{2,1,0:T(8,128)(2,1)}), bf16[16,16,384]{2,1,0:T(8,128)(2,1)S(1)}, u32[]{:S(2)}, u32[]{:S(2)}) async-start(bf16[16,16,384]{2,1,0:T(8,128)(2,1)} %shard_map.93), calls=%async_computation | async-start | bytes 393216 | tf_op jit(solution)/shard_map/all_to_all | solution.py:23
  25.2 15.0 %collective-permute-start.3 = (bf16[128,16,128]{2,1,0:T(8,128)(2,1)}, bf16[128,16,128]{2,1,0:T(8,128)(2,1)S(1)}, u32[]{:S(2)}, u32[]{:S(2)}) collective-permute-start(bf16[128,16,128]{2,1,0:T(8,128)(2,1)} %f0.3), channel_id=1, source_target_pairs={{0,384},{128,0},{256,128},{384,256},{1,385},{129,1},{257,129},{385... | collective-permute-start | bytes 1572872 | tf_op jit(solution)/shard_map/ppermute | solution.py:33
  28.6 11.6 %collective-permute-start.2 = (bf16[64,16,128]{2,1,0:T(8,128)(2,1)S(1)}, bf16[64,16,128]{2,1,0:T(8,128)(2,1)S(1)}, u32[]{:S(2)}, u32[]{:S(2)}) collective-permute-start(bf16[64,16,128]{2,1,0:T(8,128)(2,1)S(1)} %slice.69), channel_id=1, source_target_pairs={{0,128},{128,256},{256,384},{384,0},{1,129},{129,257},{257,385},{3... | collective-permute-start | bytes 786440 | tf_op jit(solution)/shard_map/ppermute | solution.py:33
  41.1 12.0 %all-to-all-start.1 = ((bf16[4,272,256]{2,1,0:T(8,128)(2,1)}), bf16[4,272,256]{2,1,0:T(8,128)(2,1)S(1)}, u32[]{:S(2)}, u32[]{:S(2)}) async-start(bf16[4,272,256]{2,1,0:T(8,128)(2,1)} %shard_map.94), calls=%async_computation.1 | async-start | bytes 1114112 | tf_op jit(solution)/shard_map/all_to_all | solution.py:23
  63.8 60.9 %all-to-all-start.2 = ((bf16[64,16,384]{2,1,0:T(8,128)(2,1)}), bf16[64,16,384]{2,1,0:T(8,128)(2,1)S(1)}, u32[]{:S(2)}, u32[]{:S(2)}) async-start(bf16[64,16,384]{2,1,0:T(8,128)(2,1)} %shard_map.97), calls=%async_computation.2 | async-start | bytes 1572864 | tf_op jit(solution)/shard_map/all_to_all | solution.py:23
  78.6 16.3 %collective-permute-start.9 = (bf16[1024,256]{1,0:T(8,128)(2,1)S(1)}, bf16[1024,256]{1,0:T(8,128)(2,1)S(1)}, u32[]{:S(2)}, u32[]{:S(2)}) collective-permute-start(bf16[1024,256]{1,0:T(8,128)(2,1)S(1)} %bitcast.17), channel_id=1, source_target_pairs={{0,384},{128,0},{256,128},{384,256},{1,385},{129,1},{257,129},{385... | collective-permute-start | bytes 1572872 | tf_op jit(solution)/shard_map/ppermute | solution.py:33
  83.9 16.4 %collective-permute-start.7 = (bf16[1024,256]{1,0:T(8,128)(2,1)S(1)}, bf16[1024,256]{1,0:T(8,128)(2,1)S(1)}, u32[]{:S(2)}, u32[]{:S(2)}) collective-permute-start(bf16[1024,256]{1,0:T(8,128)(2,1)S(1)} %bitcast.18), channel_id=1, source_target_pairs={{0,128},{128,256},{256,384},{384,0},{1,129},{129,257},{257,385},{3... | collective-permute-start | bytes 1572872 | tf_op jit(solution)/shard_map/ppermute | solution.py:33
  85.9 16.3 %collective-permute-start.6 = (bf16[256,1024]{1,0:T(8,128)(2,1)S(1)}, bf16[256,1024]{1,0:T(8,128)(2,1)S(1)}, u32[]{:S(2)}, u32[]{:S(2)}) collective-permute-start(bf16[256,1024]{1,0:T(8,128)(2,1)S(1)} %pad_maximum_fusion), channel_id=1, source_target_pairs={{0,64},{64,0},{1,65},{65,1},{2,66},{66,2},{3,67},{67,3},{4,68},{68... | collective-permute-start | bytes 1572872 | tf_op jit(solution)/shard_map/ppermute | solution.py:33
  95.0 9.8 %collective-permute-start.10 = (bf16[512,256]{1,0:T(8,128)(2,1)S(1)}, bf16[512,256]{1,0:T(8,128)(2,1)S(1)}, u32[]{:S(2)}, u32[]{:S(2)}) collective-permute-start(bf16[512,256]{1,0:T(8,128)(2,1)S(1)} %slice.74), channel_id=1, source_target_pairs={{0,384},{128,0},{256,128},{384,256},{1,385},{129,1},{257,129},{385... | collective-permute-start | bytes 786440 | tf_op jit(solution)/shard_map/ppermute | solution.py:33
  100.3 9.5 %collective-permute-start.8 = (bf16[512,256]{1,0:T(8,128)(2,1)S(1)}, bf16[512,256]{1,0:T(8,128)(2,1)S(1)}, u32[]{:S(2)}, u32[]{:S(2)}) collective-permute-start(bf16[512,256]{1,0:T(8,128)(2,1)S(1)} %slice.73), channel_id=1, source_target_pairs={{0,128},{128,256},{256,384},{384,0},{1,129},{129,257},{257,385},{3... | collective-permute-start | bytes 786440 | tf_op jit(solution)/shard_map/ppermute | solution.py:33
  126.5 53.7 %all-to-all-start.3 = ((bf16[64,16,384]{2,1,0:T(8,128)(2,1)}), bf16[64,16,384]{2,1,0:T(8,128)(2,1)S(1)}, u32[]{:S(2)}, u32[]{:S(2)}) async-start(bf16[64,16,384]{2,1,0:T(8,128)(2,1)} %bitcast.10), calls=%async_computation.3 | async-start | bytes 1572864 | tf_op jit(solution)/shard_map/all_to_all | solution.py:23
  140.7 12.9 %collective-permute-start.13 = (bf16[1024,256]{1,0:T(8,128)(2,1)S(1)}, bf16[1024,256]{1,0:T(8,128)(2,1)S(1)}, u32[]{:S(2)}, u32[]{:S(2)}) collective-permute-start(bf16[1024,256]{1,0:T(8,128)(2,1)S(1)} %get-tuple-element.72), channel_id=1, source_target_pairs={{0,128},{128,256},{256,384},{384,0},{1,129},{129,257},{257,385},{3... | collective-permute-start | bytes 1572872 | tf_op jit(solution)/shard_map/ppermute | solution.py:33
  142.7 11.9 %collective-permute-start.14 = (bf16[1024,256]{1,0:T(8,128)(2,1)S(1)}, bf16[1024,256]{1,0:T(8,128)(2,1)S(1)}, u32[]{:S(2)}, u32[]{:S(2)}) collective-permute-start(bf16[1024,256]{1,0:T(8,128)(2,1)S(1)} %get-tuple-element.74), channel_id=1, source_target_pairs={{0,384},{128,0},{256,128},{384,256},{1,385},{129,1},{257,129},{385... | collective-permute-start | bytes 1572872 | tf_op jit(solution)/shard_map/ppermute | solution.py:33
  155.3 10.2 %collective-permute-start.15 = (bf16[256,256]{1,0:T(8,128)(2,1)S(1)}, bf16[256,256]{1,0:T(8,128)(2,1)S(1)}, u32[]{:S(2)}, u32[]{:S(2)}) collective-permute-start(bf16[256,256]{1,0:T(8,128)(2,1)S(1)} %get-tuple-element.76), channel_id=1, source_target_pairs={{0,16},{16,32},{32,48},{48,0},{1,17},{17,33},{33,49},{49,1},{2,18}... | collective-permute-start | bytes 393224 | tf_op jit(solution)/shard_map/ppermute | solution.py:33
  169.9 10.3 %collective-permute-start.18 = (f32[128,1024]{1,0:T(8,128)S(1)}, f32[128,1024]{1,0:T(8,128)}, u32[]{:S(2)}, u32[]{:S(2)}) collective-permute-start(f32[128,1024]{1,0:T(8,128)S(1)} %copy-done.19), channel_id=1, source_target_pairs={{0,64},{64,0},{1,65},{65,1},{2,66},{66,2},{3,67},{67,3},{4,68},{68... | collective-permute-start | bytes 1572872 | tf_op jit(solution)/shard_map/ppermute | solution.py:33
  182.1 18.7 %collective-permute-start.20 = (bf16[49,16,256]{2,1,0:T(8,128)(2,1)S(1)}, bf16[49,16,256]{2,1,0:T(8,128)(2,1)S(1)}, u32[]{:S(2)}, u32[]{:S(2)}) collective-permute-start(bf16[49,16,256]{2,1,0:T(8,128)(2,1)S(1)} %get-tuple-element.86.p0), channel_id=1, source_target_pairs={{0,384},{128,0},{256,128},{384,256},{1,385},{129,1},{257,129},{385... | collective-permute-start | bytes 1204232 | tf_op jit(solution)/shard_map/ppermute | solution.py:33
  187.4 13.3 %collective-permute-start.19 = (bf16[49,16,256]{2,1,0:T(8,128)(2,1)S(1)}, bf16[49,16,256]{2,1,0:T(8,128)(2,1)S(1)}, u32[]{:S(2)}, u32[]{:S(2)}) collective-permute-start(bf16[49,16,256]{2,1,0:T(8,128)(2,1)S(1)} %get-tuple-element.86.p0), channel_id=1, source_target_pairs={{0,128},{128,256},{256,384},{384,0},{1,129},{129,257},{257,385},{3... | collective-permute-start | bytes 1204232 | tf_op jit(solution)/shard_map/ppermute | solution.py:33
  189.4 24.5 %all-to-all-start.4 = ((bf16[16,16,256]{2,1,0:T(8,128)(2,1)}), bf16[16,16,256]{2,1,0:T(8,128)(2,1)}, u32[]{:S(2)}, u32[]{:S(2)}) async-start(bf16[16,16,256]{2,1,0:T(8,128)(2,1)} %bitcast.11), calls=%async_computation.4 | async-start | bytes 262144 | tf_op jit(solution)/shard_map/all_to_all | solution.py:23
  201.7 12.2 %collective-permute-start.21 = (bf16[33,16,256]{2,1,0:T(8,128)(2,1)}, bf16[33,16,256]{2,1,0:T(8,128)(2,1)S(1)}, u32[]{:S(2)}, u32[]{:S(2)}) collective-permute-start(bf16[33,16,256]{2,1,0:T(8,128)(2,1)} %get-tuple-element.89), channel_id=1, source_target_pairs={{0,128},{128,256},{256,384},{384,0},{1,129},{129,257},{257,385},{3... | collective-permute-start | bytes 811016 | tf_op jit(solution)/shard_map/ppermute | solution.py:33
  203.6 10.3 %collective-permute-start.22 = (bf16[32,16,256]{2,1,0:T(8,128)(2,1)}, bf16[32,16,256]{2,1,0:T(8,128)(2,1)S(1)}, u32[]{:S(2)}, u32[]{:S(2)}) collective-permute-start(bf16[32,16,256]{2,1,0:T(8,128)(2,1)} %get-tuple-element.90), channel_id=1, source_target_pairs={{0,384},{128,0},{256,128},{384,256},{1,385},{129,1},{257,129},{385... | collective-permute-start | bytes 786440 | tf_op jit(solution)/shard_map/ppermute | solution.py:33
  225.7 17.5 %collective-permute-start.24 = (bf16[64,16,256]{2,1,0:T(8,128)(2,1)}, bf16[64,16,256]{2,1,0:T(8,128)(2,1)S(1)}, u32[]{:S(2)}, u32[]{:S(2)}) collective-permute-start(bf16[64,16,256]{2,1,0:T(8,128)(2,1)} %get-tuple-element.103), channel_id=1, source_target_pairs={{0,64},{64,0},{1,65},{65,1},{2,66},{66,2},{3,67},{67,3},{4,68},{68... | collective-permute-start | bytes 1572872 | tf_op jit(solution)/shard_map/ppermute | solution.py:33
  227.6 14.8 %all-to-all-start.5 = ((bf16[8,9,16,256]{3,2,1,0:T(8,128)(2,1)}), bf16[8,9,16,256]{3,2,1,0:T(8,128)(2,1)S(1)}, u32[]{:S(2)}, u32[]{:S(2)}) async-start(bf16[8,9,16,256]{3,2,1,0:T(8,128)(2,1)} %shard_map.108), calls=%async_computation.5 | async-start | bytes 1179648 | tf_op jit(solution)/shard_map/all_to_all | solution.py:23
  (28 other events, 382.3 us)

commit v8 on v7

--- a/solution.py
+++ b/solution.py
@@ -198,7 +198,7 @@
         hidden, before_grad = gelu_pair(before, hidden_grad)
         term_ref[:, :width] = dot(tokens, before_grad, 0, 0)
         term_ref[:, width:] = dot(cotangent, hidden, 0, 0)
-        into_ref[...] = dot(before_grad, half_ref[:, :width], 1, 1)
+        into_ref[...] = dot(before_grad, half_ref[:, :width], 1, 1).astype(into_ref.dtype)
 
     level(own_id, x_ref, g_ref, own_term, back_ref)
     level(other_id, ox_ref, og_ref, other_term, other_back_ref)
@@ -483,7 +483,7 @@
             [bf16(depth, half)] * 2
             + [bf16(middle_row, half)] * 2
             + [bf16(depth, half)]
-            + [f32(length, depth)] * 2
+            + [bf16(length, depth)] * 2
         ),
         [
             pltpu.VMEM((depth, half), BF16),
@@ -496,7 +496,7 @@
     )
     near, ahead, far_low, far_high, behind, coarse_back, other_back = slots
     up, down = shift(far_low, "y", 1), shift(far_high, "y", 3)
-    mine, numbers, up, down = lax.optimization_barrier((mine, numbers, up, down))
+    mine, numbers, up = lax.optimization_barrier((mine, numbers, up))
 
     terms, back = kernel_call(
         levels_kernel,
@@ -518,7 +518,7 @@
     for s in range(1, X):
         column_sum = column_sum + shift(leaving[s - 1], "x", s).astype(F32)
     column_sum = column_sum.astype(BF16).reshape(Z, ROWS, half)
-    other_back = shift(after(other_back, column_sum), "c", 1)
+    other_back = shift(after(other_back, terms), "c", 1)
     parts, column_sum, other_back = lax.optimization_barrier((parts, column_sum, other_back))
 
     middle_count = middle_weights.shape[0]
@@ -579,7 +579,7 @@
     fine_total = kernel_call(
         finish_kernel, [VMEM] * 2, bf16(fine_owned, ROWS, fine_width)
     )(fine_kept, fine_arrived)
-    tokens_grad = (coarse_back + other_back + back).astype(BF16)
+    tokens_grad = (coarse_back.astype(F32) + other_back.astype(F32) + back).astype(BF16)
     return (tokens_grad, coarse_total, middle_total, fine_total)
 
 

time: 246 us -> 246 us (level)
  waiting for transfers between devices: 50.7 us -> 54 us
    ppermute x25, waiting for transfers between devices: 39.2 us -> 42.4 us  [shift(): lax.ppermute(array, axis, [(i, (i + step) % count) for i in range(count)])]
    unnamed x42 -> x40, local copies, waits for them, and re-layouts: 6.88 us -> 6 us
  transfers between devices with their start and end apart: 31 -> 31, of which waited for: 14 -> 12; matrix products, arithmetic and copies ran while one was open for 1% -> 1% of each run, Pallas kernels for 7% -> 7%
where the time goes in v8:
time: 246 us; the launch traced here: 245 us
  starting transfers between devices  152 us (62%)
  waiting for transfers between devices  54 us (22%)
  Pallas kernels  27.4 us (11%)
  local copies, waits for them, and re-layouts  6.91 us (3%)
  other arithmetic  2.6 us (1%)
    ppermute x25, starting transfers between devices, shift(): lax.ppermute(array, axis, [(i, (i + step) % count) for i in range(count)])  92.4 us
    all_to_all x6, starting transfers between devices, exchange(): return lax.all_to_all(array, axes, split_axis=0, concat_axis=0, tiled=True)  59.9 us
    ppermute x25, waiting for transfers between devices, shift(): lax.ppermute(array, axis, [(i, (i + step) % count) for i in range(count)])  42.4 us
    all_to_all x6, waiting for transfers between devices, exchange(): return lax.all_to_all(array, axes, split_axis=0, concat_axis=0, tiled=True)  11.6 us
    unnamed x40, local copies, waits for them, and re-layouts  6 us
  transfers between devices with their start and end apart: 31, of which 12 were waited for; matrix products, arithmetic and copies ran while one was open for 1% of the time, Pallas kernels for 7%

profile of v8, /device:TPU:1, one launch (start us, length us, event | category | flops | bytes accessed | tf_op | source)
XLA Modules:
  0.0 244.5 jit_solution(17932812128809403369)
XLA Ops:
  0.6 8.9 %collective-permute-start = (s32[1,3]{1,0:T(1,128)}, s32[1,3]{1,0:T(1,128)S(1)}, u32[]{:S(2)}, u32[]{:S(2)}) collective-permute-start(s32[1,3]{1,0:T(1,128)} %own_ref.1), channel_id=1, source_target_pairs={{0,64},{64,0},{1,65},{65,1},{2,66},{66,2},{3,67},{67,3},{4,68},{68... | collective-permute-start | bytes 44 | tf_op jit(solution)/shard_map/ppermute | solution.py:33
  14.4 10.8 %all-to-all-start = ((bf16[16,16,384]{2,1,0:T(8,128)(2,1)}), bf16[16,16,384]{2,1,0:T(8,128)(2,1)S(1)}, u32[]{:S(2)}, u32[]{:S(2)}) async-start(bf16[16,16,384]{2,1,0:T(8,128)(2,1)} %shard_map.93), calls=%async_computation | async-start | bytes 393216 | tf_op jit(solution)/shard_map/all_to_all | solution.py:23
  30.6 9.7 %collective-permute-done.3.f3 = bf16[128,16,128]{2,1,0:T(8,128)(2,1)S(1)} collective-permute-done((bf16[128,16,128]{2,1,0:T(8,128)(2,1)}, bf16[128,16,128]{2,1,0:T(8,128)(2,1)S(1)}, u32[]{:S(2)}, u32[]{:S(2)}) %collective-permute-start.3) | collective-permute-done | bytes 524320 | tf_op jit(solution)/shard_map/ppermute | solution.py:33
  45.3 4.6 %collective-permute-start.4 = (bf16[64,16,128]{2,1,0:T(8,128)(2,1)S(1)}, bf16[64,16,128]{2,1,0:T(8,128)(2,1)S(1)}, u32[]{:S(2)}, u32[]{:S(2)}) collective-permute-start(bf16[64,16,128]{2,1,0:T(8,128)(2,1)S(1)} %slice.55), channel_id=1, source_target_pairs={{0,384},{128,0},{256,128},{384,256},{1,385},{129,1},{257,129},{385... | collective-permute-start | bytes 786440 | tf_op jit(solution)/shard_map/ppermute | solution.py:33
  56.0 4.5 %collective-permute-start.5 = (bf16[64,16,128]{2,1,0:T(8,128)(2,1)S(1)}, bf16[64,16,128]{2,1,0:T(8,128)(2,1)S(1)}, u32[]{:S(2)}, u32[]{:S(2)}) collective-permute-start(bf16[64,16,128]{2,1,0:T(8,128)(2,1)S(1)} %shard_map.96), channel_id=1, source_target_pairs={{0,64},{64,0},{1,65},{65,1},{2,66},{66,2},{3,67},{67,3},{4,68},{68... | collective-permute-start | bytes 786440 | tf_op jit(solution)/shard_map/ppermute | solution.py:33
  63.8 14.7 %all-to-all-start.2 = ((bf16[64,16,384]{2,1,0:T(8,128)(2,1)}), bf16[64,16,384]{2,1,0:T(8,128)(2,1)S(1)}, u32[]{:S(2)}, u32[]{:S(2)}) async-start(bf16[64,16,384]{2,1,0:T(8,128)(2,1)} %shard_map.97), calls=%async_computation.2 | async-start | bytes 1572864 | tf_op jit(solution)/shard_map/all_to_all | solution.py:23
  78.6 5.3 %collective-permute-start.9 = (bf16[1024,256]{1,0:T(8,128)(2,1)S(1)}, bf16[1024,256]{1,0:T(8,128)(2,1)S(1)}, u32[]{:S(2)}, u32[]{:S(2)}) collective-permute-start(bf16[1024,256]{1,0:T(8,128)(2,1)S(1)} %bitcast.17), channel_id=1, source_target_pairs={{0,384},{128,0},{256,128},{384,256},{1,385},{129,1},{257,129},{385... | collective-permute-start | bytes 1572872 | tf_op jit(solution)/shard_map/ppermute | solution.py:33
  88.4 6.5 %collective-permute-done.9.h3 = bf16[1024,256]{1,0:T(8,128)(2,1)S(1)} collective-permute-done((bf16[1024,256]{1,0:T(8,128)(2,1)S(1)}, bf16[1024,256]{1,0:T(8,128)(2,1)S(1)}, u32[]{:S(2)}, u32[]{:S(2)}) %collective-permute-start.9) | collective-permute-done | bytes 524320 | tf_op jit(solution)/shard_map/ppermute | solution.py:33
  94.9 5.3 %collective-permute-start.10 = (bf16[512,256]{1,0:T(8,128)(2,1)S(1)}, bf16[512,256]{1,0:T(8,128)(2,1)S(1)}, u32[]{:S(2)}, u32[]{:S(2)}) collective-permute-start(bf16[512,256]{1,0:T(8,128)(2,1)S(1)} %slice.74), channel_id=1, source_target_pairs={{0,384},{128,0},{256,128},{384,256},{1,385},{129,1},{257,129},{385... | collective-permute-start | bytes 786440 | tf_op jit(solution)/shard_map/ppermute | solution.py:33
  104.7 5.1 %collective-permute-done.8.h2a = bf16[512,256]{1,0:T(8,128)(2,1)S(1)} collective-permute-done((bf16[512,256]{1,0:T(8,128)(2,1)S(1)}, bf16[512,256]{1,0:T(8,128)(2,1)S(1)}, u32[]{:S(2)}, u32[]{:S(2)}) %collective-permute-start.8) | collective-permute-done | bytes 262176 | tf_op jit(solution)/shard_map/ppermute | solution.py:33
  116.0 5.9 %collective-permute-done.11.r1 = bf16[512,256]{1,0:T(8,128)(2,1)S(1)} collective-permute-done((bf16[512,256]{1,0:T(8,128)(2,1)S(1)}, bf16[512,256]{1,0:T(8,128)(2,1)S(1)}, u32[]{:S(2)}, u32[]{:S(2)}) %collective-permute-start.11) | collective-permute-done | bytes 262176 | tf_op jit(solution)/shard_map/ppermute | solution.py:33
  124.4 13.7 %all-to-all-start.3 = ((bf16[64,16,384]{2,1,0:T(8,128)(2,1)}), bf16[64,16,384]{2,1,0:T(8,128)(2,1)S(1)}, u32[]{:S(2)}, u32[]{:S(2)}) async-start(bf16[64,16,384]{2,1,0:T(8,128)(2,1)} %bitcast.10), calls=%async_computation.3 | async-start | bytes 1572864 | tf_op jit(solution)/shard_map/all_to_all | solution.py:23
  140.1 5.4 %collective-permute-done.12.r3 = bf16[512,256]{1,0:T(8,128)(2,1)S(1)} collective-permute-done((bf16[512,256]{1,0:T(8,128)(2,1)}, bf16[512,256]{1,0:T(8,128)(2,1)S(1)}, u32[]{:S(2)}, u32[]{:S(2)}) %collective-permute-start.12) | collective-permute-done | bytes 262176 | tf_op jit(solution)/shard_map/ppermute | solution.py:33
  147.6 4.6 %collective-permute-start.14 = (bf16[1024,256]{1,0:T(8,128)(2,1)S(1)}, bf16[1024,256]{1,0:T(8,128)(2,1)S(1)}, u32[]{:S(2)}, u32[]{:S(2)}) collective-permute-start(bf16[1024,256]{1,0:T(8,128)(2,1)S(1)} %get-tuple-element.72), channel_id=1, source_target_pairs={{0,384},{128,0},{256,128},{384,256},{1,385},{129,1},{257,129},{385... | collective-permute-start | bytes 1572872 | tf_op jit(solution)/shard_map/ppermute | solution.py:33
  152.2 4.9 %collective-permute-done.13.up_ref = bf16[1024,256]{1,0:T(8,128)(2,1)S(1)} collective-permute-done((bf16[1024,256]{1,0:T(8,128)(2,1)S(1)}, bf16[1024,256]{1,0:T(8,128)(2,1)S(1)}, u32[]{:S(2)}, u32[]{:S(2)}) %collective-permute-start.13) | collective-permute-done | bytes 524320 | tf_op jit(solution)/shard_map/ppermute | solution.py:33
  162.0 4.5 %collective-permute-start.16 = (bf16[256,256]{1,0:T(8,128)(2,1)S(1)}, bf16[256,256]{1,0:T(8,128)(2,1)S(1)}, u32[]{:S(2)}, u32[]{:S(2)}) collective-permute-start(bf16[256,256]{1,0:T(8,128)(2,1)S(1)} %get-tuple-element.75), channel_id=1, source_target_pairs={{0,32},{16,48},{32,0},{48,16},{1,33},{17,49},{33,1},{49,17},{2,34}... | collective-permute-start | bytes 393224 | tf_op jit(solution)/shard_map/ppermute | solution.py:33
  169.5 9.4 %collective-permute-start.18 = (bf16[128,1024]{1,0:T(8,128)(2,1)S(1)}, bf16[128,1024]{1,0:T(8,128)(2,1)}, u32[]{:S(2)}, u32[]{:S(2)}) collective-permute-start(bf16[128,1024]{1,0:T(8,128)(2,1)S(1)} %copy-done.17), channel_id=1, source_target_pairs={{0,64},{64,0},{1,65},{65,1},{2,66},{66,2},{3,67},{67,3},{4,68},{68... | collective-permute-start | bytes 786440 | tf_op jit(solution)/shard_map/ppermute | solution.py:33
  182.1 5.3 %collective-permute-start.20 = (bf16[49,16,256]{2,1,0:T(8,128)(2,1)S(1)}, bf16[49,16,256]{2,1,0:T(8,128)(2,1)S(1)}, u32[]{:S(2)}, u32[]{:S(2)}) collective-permute-start(bf16[49,16,256]{2,1,0:T(8,128)(2,1)S(1)} %get-tuple-element.84.p0), channel_id=1, source_target_pairs={{0,384},{128,0},{256,128},{384,256},{1,385},{129,1},{257,129},{385... | collective-permute-start | bytes 1204232 | tf_op jit(solution)/shard_map/ppermute | solution.py:33
  189.4 11.4 %all-to-all-start.4 = ((bf16[16,16,256]{2,1,0:T(8,128)(2,1)}), bf16[16,16,256]{2,1,0:T(8,128)(2,1)}, u32[]{:S(2)}, u32[]{:S(2)}) async-start(bf16[16,16,256]{2,1,0:T(8,128)(2,1)} %bitcast.11), calls=%async_computation.4 | async-start | bytes 262144 | tf_op jit(solution)/shard_map/all_to_all | solution.py:23
  203.6 4.6 %collective-permute-start.22 = (bf16[32,16,256]{2,1,0:T(8,128)(2,1)}, bf16[32,16,256]{2,1,0:T(8,128)(2,1)S(1)}, u32[]{:S(2)}, u32[]{:S(2)}) collective-permute-start(bf16[32,16,256]{2,1,0:T(8,128)(2,1)} %get-tuple-element.88), channel_id=1, source_target_pairs={{0,384},{128,0},{256,128},{384,256},{1,385},{129,1},{257,129},{385... | collective-permute-start | bytes 786440 | tf_op jit(solution)/shard_map/ppermute | solution.py:33
  209.2 4.6 %shard_map.104.before_ref = f32[264,16,128]{2,1,0:T(8,128)S(1)} custom-call(s32[4]{0:T(128)S(1)} %pad_add_fusion.where_ref, s32[3,16,64]{2,1,0:T(8,128)S(1)} %maximum_convert_fusion.ids_ref, bf16[49,16,256]{2,1,0:T(8,128)(2,1)S(1)} %copy-done.9, bf16[49,16,256]{2,1,0:T(8,128)(2,1)S(1)} %collective-permute-done.19.p1.r1, ...), custom_call_target="tpu_custom_call" | custom-call | flops 1000000 | bytes 1000000 | tf_op jit(solution)/shard_map/pallas_call | solution.py:550
  215.4 4.5 %collective-permute-start.23 = (bf16[8,16,256]{2,1,0:T(8,128)(2,1)S(1)}, bf16[8,16,256]{2,1,0:T(8,128)(2,1)S(1)}, u32[]{:S(2)}, u32[]{:S(2)}) collective-permute-start(bf16[8,16,256]{2,1,0:T(8,128)(2,1)S(1)} %get-tuple-element.94), channel_id=1, source_target_pairs={{0,64},{64,0},{1,65},{65,1},{2,66},{66,2},{3,67},{67,3},{4,68},{68... | collective-permute-start | bytes 196616 | tf_op jit(solution)/shard_map/ppermute | solution.py:33
  227.5 5.1 %all-to-all-start.5 = ((bf16[8,9,16,256]{3,2,1,0:T(8,128)(2,1)}), bf16[8,9,16,256]{3,2,1,0:T(8,128)(2,1)S(1)}, u32[]{:S(2)}, u32[]{:S(2)}) async-start(bf16[8,9,16,256]{3,2,1,0:T(8,128)(2,1)} %shard_map.108), calls=%async_computation.5 | async-start | bytes 1179648 | tf_op jit(solution)/shard_map/all_to_all | solution.py:23
  234.4 8.4 %all-to-all-done.5.total_ref = bf16[8,9,16,256]{3,2,1,0:T(8,128)(2,1)S(1)} async-done(((bf16[8,9,16,256]{3,2,1,0:T(8,128)(2,1)}), bf16[8,9,16,256]{3,2,1,0:T(8,128)(2,1)S(1)}, u32[]{:S(2)}, u32[]{:S(2)}) %all-to-all-start.5) | async-done | bytes 589856 | tf_op jit(solution)/shard_map/all_to_all | solution.py:23
  (114 shorter events, 75.5 us)
Async XLA Ops:
  0.6 10.9 %collective-permute-start = (s32[1,3]{1,0:T(1,128)}, s32[1,3]{1,0:T(1,128)S(1)}, u32[]{:S(2)}, u32[]{:S(2)}) collective-permute-start(s32[1,3]{1,0:T(1,128)} %own_ref.1), channel_id=1, source_target_pairs={{0,64},{64,0},{1,65},{65,1},{2,66},{66,2},{3,67},{67,3},{4,68},{68... | collective-permute-start | bytes 44 | tf_op jit(solution)/shard_map/ppermute | solution.py:33
  9.6 19.0 %collective-permute-start.1 = (bf16[128,16,128]{2,1,0:T(8,128)(2,1)}, bf16[128,16,128]{2,1,0:T(8,128)(2,1)S(1)}, u32[]{:S(2)}, u32[]{:S(2)}) collective-permute-start(bf16[128,16,128]{2,1,0:T(8,128)(2,1)} %f0.3), channel_id=1, source_target_pairs={{0,128},{128,256},{256,384},{384,0},{1,129},{129,257},{257,385},{3... | collective-permute-start | bytes 1572872 | tf_op jit(solution)/shard_map/ppermute | solution.py:33
  14.4 25.9 %all-to-all-start = ((bf16[16,16,384]{2,1,0:T(8,128)(2,1)}), bf16[16,16,384]{2,1,0:T(8,128)(2,1)S(1)}, u32[]{:S(2)}, u32[]{:S(2)}) async-start(bf16[16,16,384]{2,1,0:T(8,128)(2,1)} %shard_map.93), calls=%async_computation | async-start | bytes 393216 | tf_op jit(solution)/shard_map/all_to_all | solution.py:23
  25.2 15.0 %collective-permute-start.3 = (bf16[128,16,128]{2,1,0:T(8,128)(2,1)}, bf16[128,16,128]{2,1,0:T(8,128)(2,1)S(1)}, u32[]{:S(2)}, u32[]{:S(2)}) collective-permute-start(bf16[128,16,128]{2,1,0:T(8,128)(2,1)} %f0.3), channel_id=1, source_target_pairs={{0,384},{128,0},{256,128},{384,256},{1,385},{129,1},{257,129},{385... | collective-permute-start | bytes 1572872 | tf_op jit(solution)/shard_map/ppermute | solution.py:33
  28.6 11.6 %collective-permute-start.2 = (bf16[64,16,128]{2,1,0:T(8,128)(2,1)S(1)}, bf16[64,16,128]{2,1,0:T(8,128)(2,1)S(1)}, u32[]{:S(2)}, u32[]{:S(2)}) collective-permute-start(bf16[64,16,128]{2,1,0:T(8,128)(2,1)S(1)} %slice.69), channel_id=1, source_target_pairs={{0,128},{128,256},{256,384},{384,0},{1,129},{129,257},{257,385},{3... | collective-permute-start | bytes 786440 | tf_op jit(solution)/shard_map/ppermute | solution.py:33
  41.1 12.0 %all-to-all-start.1 = ((bf16[4,272,256]{2,1,0:T(8,128)(2,1)}), bf16[4,272,256]{2,1,0:T(8,128)(2,1)S(1)}, u32[]{:S(2)}, u32[]{:S(2)}) async-start(bf16[4,272,256]{2,1,0:T(8,128)(2,1)} %shard_map.94), calls=%async_computation.1 | async-start | bytes 1114112 | tf_op jit(solution)/shard_map/all_to_all | solution.py:23
  63.8 58.0 %all-to-all-start.2 = ((bf16[64,16,384]{2,1,0:T(8,128)(2,1)}), bf16[64,16,384]{2,1,0:T(8,128)(2,1)S(1)}, u32[]{:S(2)}, u32[]{:S(2)}) async-start(bf16[64,16,384]{2,1,0:T(8,128)(2,1)} %shard_map.97), calls=%async_computation.2 | async-start | bytes 1572864 | tf_op jit(solution)/shard_map/all_to_all | solution.py:23
  78.6 16.3 %collective-permute-start.9 = (bf16[1024,256]{1,0:T(8,128)(2,1)S(1)}, bf16[1024,256]{1,0:T(8,128)(2,1)S(1)}, u32[]{:S(2)}, u32[]{:S(2)}) collective-permute-start(bf16[1024,256]{1,0:T(8,128)(2,1)S(1)} %bitcast.17), channel_id=1, source_target_pairs={{0,384},{128,0},{256,128},{384,256},{1,385},{129,1},{257,129},{385... | collective-permute-start | bytes 1572872 | tf_op jit(solution)/shard_map/ppermute | solution.py:33
  83.9 16.4 %collective-permute-start.7 = (bf16[1024,256]{1,0:T(8,128)(2,1)S(1)}, bf16[1024,256]{1,0:T(8,128)(2,1)S(1)}, u32[]{:S(2)}, u32[]{:S(2)}) collective-permute-start(bf16[1024,256]{1,0:T(8,128)(2,1)S(1)} %bitcast.18), channel_id=1, source_target_pairs={{0,128},{128,256},{256,384},{384,0},{1,129},{129,257},{257,385},{3... | collective-permute-start | bytes 1572872 | tf_op jit(solution)/shard_map/ppermute | solution.py:33
  85.9 16.3 %collective-permute-start.6 = (bf16[256,1024]{1,0:T(8,128)(2,1)S(1)}, bf16[256,1024]{1,0:T(8,128)(2,1)S(1)}, u32[]{:S(2)}, u32[]{:S(2)}) collective-permute-start(bf16[256,1024]{1,0:T(8,128)(2,1)S(1)} %pad_maximum_fusion), channel_id=1, source_target_pairs={{0,64},{64,0},{1,65},{65,1},{2,66},{66,2},{3,67},{67,3},{4,68},{68... | collective-permute-start | bytes 1572872 | tf_op jit(solution)/shard_map/ppermute | solution.py:33
  124.4 55.7 %all-to-all-start.3 = ((bf16[64,16,384]{2,1,0:T(8,128)(2,1)}), bf16[64,16,384]{2,1,0:T(8,128)(2,1)S(1)}, u32[]{:S(2)}, u32[]{:S(2)}) async-start(bf16[64,16,384]{2,1,0:T(8,128)(2,1)} %bitcast.10), calls=%async_computation.3 | async-start | bytes 1572864 | tf_op jit(solution)/shard_map/all_to_all | solution.py:23
  145.7 11.4 %collective-permute-start.13 = (bf16[1024,256]{1,0:T(8,128)(2,1)S(1)}, bf16[1024,256]{1,0:T(8,128)(2,1)S(1)}, u32[]{:S(2)}, u32[]{:S(2)}) collective-permute-start(bf16[1024,256]{1,0:T(8,128)(2,1)S(1)} %get-tuple-element.70), channel_id=1, source_target_pairs={{0,128},{128,256},{256,384},{384,0},{1,129},{129,257},{257,385},{3... | collective-permute-start | bytes 1572872 | tf_op jit(solution)/shard_map/ppermute | solution.py:33
  147.6 10.7 %collective-permute-start.14 = (bf16[1024,256]{1,0:T(8,128)(2,1)S(1)}, bf16[1024,256]{1,0:T(8,128)(2,1)S(1)}, u32[]{:S(2)}, u32[]{:S(2)}) collective-permute-start(bf16[1024,256]{1,0:T(8,128)(2,1)S(1)} %get-tuple-element.72), channel_id=1, source_target_pairs={{0,384},{128,0},{256,128},{384,256},{1,385},{129,1},{257,129},{385... | collective-permute-start | bytes 1572872 | tf_op jit(solution)/shard_map/ppermute | solution.py:33
  159.0 19.9 %collective-permute-start.15 = (bf16[256,256]{1,0:T(8,128)(2,1)S(1)}, bf16[256,256]{1,0:T(8,128)(2,1)S(1)}, u32[]{:S(2)}, u32[]{:S(2)}) collective-permute-start(bf16[256,256]{1,0:T(8,128)(2,1)S(1)} %get-tuple-element.74), channel_id=1, source_target_pairs={{0,16},{16,32},{32,48},{48,0},{1,17},{17,33},{33,49},{49,1},{2,18}... | collective-permute-start | bytes 393224 | tf_op jit(solution)/shard_map/ppermute | solution.py:33
  162.0 16.9 %collective-permute-start.16 = (bf16[256,256]{1,0:T(8,128)(2,1)S(1)}, bf16[256,256]{1,0:T(8,128)(2,1)S(1)}, u32[]{:S(2)}, u32[]{:S(2)}) collective-permute-start(bf16[256,256]{1,0:T(8,128)(2,1)S(1)} %get-tuple-element.75), channel_id=1, source_target_pairs={{0,32},{16,48},{32,0},{48,16},{1,33},{17,49},{33,1},{49,17},{2,34}... | collective-permute-start | bytes 393224 | tf_op jit(solution)/shard_map/ppermute | solution.py:33
  166.5 12.4 %collective-permute-start.17 = (bf16[256,256]{1,0:T(8,128)(2,1)S(1)}, bf16[256,256]{1,0:T(8,128)(2,1)S(1)}, u32[]{:S(2)}, u32[]{:S(2)}) collective-permute-start(bf16[256,256]{1,0:T(8,128)(2,1)S(1)} %get-tuple-element.76), channel_id=1, source_target_pairs={{0,48},{16,0},{32,16},{48,32},{1,49},{17,1},{33,17},{49,33},{2,50}... | collective-permute-start | bytes 393224 | tf_op jit(solution)/shard_map/ppermute | solution.py:33
  169.5 10.7 %collective-permute-start.18 = (bf16[128,1024]{1,0:T(8,128)(2,1)S(1)}, bf16[128,1024]{1,0:T(8,128)(2,1)}, u32[]{:S(2)}, u32[]{:S(2)}) collective-permute-start(bf16[128,1024]{1,0:T(8,128)(2,1)S(1)} %copy-done.17), channel_id=1, source_target_pairs={{0,64},{64,0},{1,65},{65,1},{2,66},{66,2},{3,67},{67,3},{4,68},{68... | collective-permute-start | bytes 786440 | tf_op jit(solution)/shard_map/ppermute | solution.py:33
  182.1 18.7 %collective-permute-start.20 = (bf16[49,16,256]{2,1,0:T(8,128)(2,1)S(1)}, bf16[49,16,256]{2,1,0:T(8,128)(2,1)S(1)}, u32[]{:S(2)}, u32[]{:S(2)}) collective-permute-start(bf16[49,16,256]{2,1,0:T(8,128)(2,1)S(1)} %get-tuple-element.84.p0), channel_id=1, source_target_pairs={{0,384},{128,0},{256,128},{384,256},{1,385},{129,1},{257,129},{385... | collective-permute-start | bytes 1204232 | tf_op jit(solution)/shard_map/ppermute | solution.py:33
  187.4 13.3 %collective-permute-start.19 = (bf16[49,16,256]{2,1,0:T(8,128)(2,1)S(1)}, bf16[49,16,256]{2,1,0:T(8,128)(2,1)S(1)}, u32[]{:S(2)}, u32[]{:S(2)}) collective-permute-start(bf16[49,16,256]{2,1,0:T(8,128)(2,1)S(1)} %get-tuple-element.84.p0), channel_id=1, source_target_pairs={{0,128},{128,256},{256,384},{384,0},{1,129},{129,257},{257,385},{3... | collective-permute-start | bytes 1204232 | tf_op jit(solution)/shard_map/ppermute | solution.py:33
  189.4 24.5 %all-to-all-start.4 = ((bf16[16,16,256]{2,1,0:T(8,128)(2,1)}), bf16[16,16,256]{2,1,0:T(8,128)(2,1)}, u32[]{:S(2)}, u32[]{:S(2)}) async-start(bf16[16,16,256]{2,1,0:T(8,128)(2,1)} %bitcast.11), calls=%async_computation.4 | async-start | bytes 262144 | tf_op jit(solution)/shard_map/all_to_all | solution.py:23
  201.6 12.2 %collective-permute-start.21 = (bf16[33,16,256]{2,1,0:T(8,128)(2,1)}, bf16[33,16,256]{2,1,0:T(8,128)(2,1)S(1)}, u32[]{:S(2)}, u32[]{:S(2)}) collective-permute-start(bf16[33,16,256]{2,1,0:T(8,128)(2,1)} %get-tuple-element.87), channel_id=1, source_target_pairs={{0,128},{128,256},{256,384},{384,0},{1,129},{129,257},{257,385},{3... | collective-permute-start | bytes 811016 | tf_op jit(solution)/shard_map/ppermute | solution.py:33
  203.6 10.3 %collective-permute-start.22 = (bf16[32,16,256]{2,1,0:T(8,128)(2,1)}, bf16[32,16,256]{2,1,0:T(8,128)(2,1)S(1)}, u32[]{:S(2)}, u32[]{:S(2)}) collective-permute-start(bf16[32,16,256]{2,1,0:T(8,128)(2,1)} %get-tuple-element.88), channel_id=1, source_target_pairs={{0,384},{128,0},{256,128},{384,256},{1,385},{129,1},{257,129},{385... | collective-permute-start | bytes 786440 | tf_op jit(solution)/shard_map/ppermute | solution.py:33
  225.6 18.0 %collective-permute-start.24 = (bf16[64,16,256]{2,1,0:T(8,128)(2,1)}, bf16[64,16,256]{2,1,0:T(8,128)(2,1)S(1)}, u32[]{:S(2)}, u32[]{:S(2)}) collective-permute-start(bf16[64,16,256]{2,1,0:T(8,128)(2,1)} %get-tuple-element.101), channel_id=1, source_target_pairs={{0,64},{64,0},{1,65},{65,1},{2,66},{66,2},{3,67},{67,3},{4,68},{68... | collective-permute-start | bytes 1572872 | tf_op jit(solution)/shard_map/ppermute | solution.py:33
  227.5 15.3 %all-to-all-start.5 = ((bf16[8,9,16,256]{3,2,1,0:T(8,128)(2,1)}), bf16[8,9,16,256]{3,2,1,0:T(8,128)(2,1)S(1)}, u32[]{:S(2)}, u32[]{:S(2)}) async-start(bf16[8,9,16,256]{3,2,1,0:T(8,128)(2,1)} %shard_map.108), calls=%async_computation.5 | async-start | bytes 1179648 | tf_op jit(solution)/shard_map/all_to_all | solution.py:23
  (27 other events, 385.0 us)

commit v9 on v8

--- a/solution.py
+++ b/solution.py
@@ -496,7 +496,7 @@
     )
     near, ahead, far_low, far_high, behind, coarse_back, other_back = slots
     up, down = shift(far_low, "y", 1), shift(far_high, "y", 3)
-    mine, numbers, up = lax.optimization_barrier((mine, numbers, up))
+    mine, numbers, up, down = lax.optimization_barrier((mine, numbers, up, down))
 
     terms, back = kernel_call(
         levels_kernel,

time: 246 us -> 244 us (level)
  waiting for transfers between devices: 54 us -> 47.5 us
  starting transfers between devices: 152 us -> 155 us
    ppermute x25, waiting for transfers between devices: 42.4 us -> 34.3 us  [shift(): lax.ppermute(array, axis, [(i, (i + step) % count) for i in range(count)])]
    ppermute x25, starting transfers between devices: 92.4 us -> 97.4 us  [shift(): lax.ppermute(array, axis, [(i, (i + step) % count) for i in range(count)])]
    all_to_all x6, starting transfers between devices: 59.9 us -> 57.3 us  [exchange(): return lax.all_to_all(array, axes, split_axis=0, concat_axis=0, tiled=True)]
    unnamed x40 -> x42, local copies, waits for them, and re-layouts: 6 us -> 7.64 us
  transfers between devices with their start and end apart: 31 -> 31, of which waited for: 12 -> 13; matrix products, arithmetic and copies ran while one was open for 1% -> 1% of each run, Pallas kernels for 7% -> 7%
where the time goes in v9:
time: 244 us; the launch traced here: 242 us
  starting transfers between devices  155 us (64%)
  waiting for transfers between devices  47.5 us (19%)
  Pallas kernels  27.4 us (11%)
  local copies, waits for them, and re-layouts  8.55 us (4%)
  other arithmetic  2.61 us (1%)
    ppermute x25, starting transfers between devices, shift(): lax.ppermute(array, axis, [(i, (i + step) % count) for i in range(count)])  97.4 us
    all_to_all x6, starting transfers between devices, exchange(): return lax.all_to_all(array, axes, split_axis=0, concat_axis=0, tiled=True)  57.3 us
    ppermute x25, waiting for transfers between devices, shift(): lax.ppermute(array, axis, [(i, (i + step) % count) for i in range(count)])  34.3 us
    all_to_all x6, waiting for transfers between devices, exchange(): return lax.all_to_all(array, axes, split_axis=0, concat_axis=0, tiled=True)  13.2 us
    unnamed x42, local copies, waits for them, and re-layouts  7.64 us
  transfers between devices with their start and end apart: 31, of which 13 were waited for; matrix products, arithmetic and copies ran while one was open for 1% of the time, Pallas kernels for 7%

profile of v9, /device:TPU:1, one launch (start us, length us, event | category | flops | bytes accessed | tf_op | source)
XLA Modules:
  0.0 242.1 jit_solution(12747077249833344373)
XLA Ops:
  0.6 8.9 %collective-permute-start = (s32[1,3]{1,0:T(1,128)}, s32[1,3]{1,0:T(1,128)S(1)}, u32[]{:S(2)}, u32[]{:S(2)}) collective-permute-start(s32[1,3]{1,0:T(1,128)} %own_ref.1), channel_id=1, source_target_pairs={{0,64},{64,0},{1,65},{65,1},{2,66},{66,2},{3,67},{67,3},{4,68},{68... | collective-permute-start | bytes 44 | tf_op jit(solution)/shard_map/ppermute | solution.py:33
  14.4 10.8 %all-to-all-start = ((bf16[16,16,384]{2,1,0:T(8,128)(2,1)}), bf16[16,16,384]{2,1,0:T(8,128)(2,1)S(1)}, u32[]{:S(2)}, u32[]{:S(2)}) async-start(bf16[16,16,384]{2,1,0:T(8,128)(2,1)} %shard_map.93), calls=%async_computation | async-start | bytes 393216 | tf_op jit(solution)/shard_map/all_to_all | solution.py:23
  30.6 9.7 %collective-permute-done.3.f3 = bf16[128,16,128]{2,1,0:T(8,128)(2,1)S(1)} collective-permute-done((bf16[128,16,128]{2,1,0:T(8,128)(2,1)}, bf16[128,16,128]{2,1,0:T(8,128)(2,1)S(1)}, u32[]{:S(2)}, u32[]{:S(2)}) %collective-permute-start.3) | collective-permute-done | bytes 524320 | tf_op jit(solution)/shard_map/ppermute | solution.py:33
  41.1 4.1 %all-to-all-start.1 = ((bf16[4,272,256]{2,1,0:T(8,128)(2,1)}), bf16[4,272,256]{2,1,0:T(8,128)(2,1)S(1)}, u32[]{:S(2)}, u32[]{:S(2)}) async-start(bf16[4,272,256]{2,1,0:T(8,128)(2,1)} %shard_map.94), calls=%async_computation.1 | async-start | bytes 1114112 | tf_op jit(solution)/shard_map/all_to_all | solution.py:23
  45.3 4.6 %collective-permute-start.4 = (bf16[64,16,128]{2,1,0:T(8,128)(2,1)S(1)}, bf16[64,16,128]{2,1,0:T(8,128)(2,1)S(1)}, u32[]{:S(2)}, u32[]{:S(2)}) collective-permute-start(bf16[64,16,128]{2,1,0:T(8,128)(2,1)S(1)} %slice.55), channel_id=1, source_target_pairs={{0,384},{128,0},{256,128},{384,256},{1,385},{129,1},{257,129},{385... | collective-permute-start | bytes 786440 | tf_op jit(solution)/shard_map/ppermute | solution.py:33
  56.0 4.5 %collective-permute-start.5 = (bf16[64,16,128]{2,1,0:T(8,128)(2,1)S(1)}, bf16[64,16,128]{2,1,0:T(8,128)(2,1)S(1)}, u32[]{:S(2)}, u32[]{:S(2)}) collective-permute-start(bf16[64,16,128]{2,1,0:T(8,128)(2,1)S(1)} %shard_map.96), channel_id=1, source_target_pairs={{0,64},{64,0},{1,65},{65,1},{2,66},{66,2},{3,67},{67,3},{4,68},{68... | collective-permute-start | bytes 786440 | tf_op jit(solution)/shard_map/ppermute | solution.py:33
  63.8 14.7 %all-to-all-start.2 = ((bf16[64,16,384]{2,1,0:T(8,128)(2,1)}), bf16[64,16,384]{2,1,0:T(8,128)(2,1)S(1)}, u32[]{:S(2)}, u32[]{:S(2)}) async-start(bf16[64,16,384]{2,1,0:T(8,128)(2,1)} %shard_map.97), calls=%async_computation.2 | async-start | bytes 1572864 | tf_op jit(solution)/shard_map/all_to_all | solution.py:23
  78.6 5.3 %collective-permute-start.9 = (bf16[1024,256]{1,0:T(8,128)(2,1)S(1)}, bf16[1024,256]{1,0:T(8,128)(2,1)S(1)}, u32[]{:S(2)}, u32[]{:S(2)}) collective-permute-start(bf16[1024,256]{1,0:T(8,128)(2,1)S(1)} %bitcast.17), channel_id=1, source_target_pairs={{0,384},{128,0},{256,128},{384,256},{1,385},{129,1},{257,129},{385... | collective-permute-start | bytes 1572872 | tf_op jit(solution)/shard_map/ppermute | solution.py:33
  88.4 6.5 %collective-permute-done.9.h3 = bf16[1024,256]{1,0:T(8,128)(2,1)S(1)} collective-permute-done((bf16[1024,256]{1,0:T(8,128)(2,1)S(1)}, bf16[1024,256]{1,0:T(8,128)(2,1)S(1)}, u32[]{:S(2)}, u32[]{:S(2)}) %collective-permute-start.9) | collective-permute-done | bytes 524320 | tf_op jit(solution)/shard_map/ppermute | solution.py:33
  95.0 5.3 %collective-permute-start.10 = (bf16[512,256]{1,0:T(8,128)(2,1)S(1)}, bf16[512,256]{1,0:T(8,128)(2,1)S(1)}, u32[]{:S(2)}, u32[]{:S(2)}) collective-permute-start(bf16[512,256]{1,0:T(8,128)(2,1)S(1)} %slice.74), channel_id=1, source_target_pairs={{0,384},{128,0},{256,128},{384,256},{1,385},{129,1},{257,129},{385... | collective-permute-start | bytes 786440 | tf_op jit(solution)/shard_map/ppermute | solution.py:33
  104.7 5.1 %collective-permute-done.8.h2a = bf16[512,256]{1,0:T(8,128)(2,1)S(1)} collective-permute-done((bf16[512,256]{1,0:T(8,128)(2,1)S(1)}, bf16[512,256]{1,0:T(8,128)(2,1)S(1)}, u32[]{:S(2)}, u32[]{:S(2)}) %collective-permute-start.8) | collective-permute-done | bytes 262176 | tf_op jit(solution)/shard_map/ppermute | solution.py:33
  115.2 4.6 %collective-permute-start.12 = (bf16[512,256]{1,0:T(8,128)(2,1)S(1)}, bf16[512,256]{1,0:T(8,128)(2,1)S(1)}, u32[]{:S(2)}, u32[]{:S(2)}) collective-permute-start(bf16[512,256]{1,0:T(8,128)(2,1)S(1)} %get-tuple-element.63), channel_id=1, source_target_pairs={{0,384},{128,0},{256,128},{384,256},{1,385},{129,1},{257,129},{385... | collective-permute-start | bytes 786440 | tf_op jit(solution)/shard_map/ppermute | solution.py:33
  126.3 14.1 %all-to-all-start.3 = ((bf16[64,16,384]{2,1,0:T(8,128)(2,1)}), bf16[64,16,384]{2,1,0:T(8,128)(2,1)S(1)}, u32[]{:S(2)}, u32[]{:S(2)}) async-start(bf16[64,16,384]{2,1,0:T(8,128)(2,1)} %bitcast.10), calls=%async_computation.3 | async-start | bytes 1572864 | tf_op jit(solution)/shard_map/all_to_all | solution.py:23
  143.4 5.0 %collective-permute-start.14 = (bf16[1024,256]{1,0:T(8,128)(2,1)S(1)}, bf16[1024,256]{1,0:T(8,128)(2,1)S(1)}, u32[]{:S(2)}, u32[]{:S(2)}) collective-permute-start(bf16[1024,256]{1,0:T(8,128)(2,1)S(1)} %get-tuple-element.74), channel_id=1, source_target_pairs={{0,384},{128,0},{256,128},{384,256},{1,385},{129,1},{257,129},{385... | collective-permute-start | bytes 1572872 | tf_op jit(solution)/shard_map/ppermute | solution.py:33
  148.5 5.9 %collective-permute-done.13.up_ref = bf16[1024,256]{1,0:T(8,128)(2,1)S(1)} collective-permute-done((bf16[1024,256]{1,0:T(8,128)(2,1)S(1)}, bf16[1024,256]{1,0:T(8,128)(2,1)S(1)}, u32[]{:S(2)}, u32[]{:S(2)}) %collective-permute-start.13) | collective-permute-done | bytes 524320 | tf_op jit(solution)/shard_map/ppermute | solution.py:33
  158.7 4.5 %collective-permute-start.16 = (bf16[256,256]{1,0:T(8,128)(2,1)S(1)}, bf16[256,256]{1,0:T(8,128)(2,1)S(1)}, u32[]{:S(2)}, u32[]{:S(2)}) collective-permute-start(bf16[256,256]{1,0:T(8,128)(2,1)S(1)} %get-tuple-element.77), channel_id=1, source_target_pairs={{0,32},{16,48},{32,0},{48,16},{1,33},{17,49},{33,1},{49,17},{2,34}... | collective-permute-start | bytes 393224 | tf_op jit(solution)/shard_map/ppermute | solution.py:33
  166.2 8.3 %collective-permute-start.18 = (bf16[128,1024]{1,0:T(8,128)(2,1)S(1)}, bf16[128,1024]{1,0:T(8,128)(2,1)}, u32[]{:S(2)}, u32[]{:S(2)}) collective-permute-start(bf16[128,1024]{1,0:T(8,128)(2,1)S(1)} %copy-done.19), channel_id=1, source_target_pairs={{0,64},{64,0},{1,65},{65,1},{2,66},{66,2},{3,67},{67,3},{4,68},{68... | collective-permute-start | bytes 786440 | tf_op jit(solution)/shard_map/ppermute | solution.py:33
  179.3 5.6 %collective-permute-start.20 = (bf16[49,16,256]{2,1,0:T(8,128)(2,1)S(1)}, bf16[49,16,256]{2,1,0:T(8,128)(2,1)S(1)}, u32[]{:S(2)}, u32[]{:S(2)}) collective-permute-start(bf16[49,16,256]{2,1,0:T(8,128)(2,1)S(1)} %get-tuple-element.86.p0), channel_id=1, source_target_pairs={{0,384},{128,0},{256,128},{384,256},{1,385},{129,1},{257,129},{385... | collective-permute-start | bytes 1204232 | tf_op jit(solution)/shard_map/ppermute | solution.py:33
  186.8 9.6 %all-to-all-start.4 = ((bf16[16,16,256]{2,1,0:T(8,128)(2,1)}), bf16[16,16,256]{2,1,0:T(8,128)(2,1)}, u32[]{:S(2)}, u32[]{:S(2)}) async-start(bf16[16,16,256]{2,1,0:T(8,128)(2,1)} %bitcast.11), calls=%async_computation.4 | async-start | bytes 262144 | tf_op jit(solution)/shard_map/all_to_all | solution.py:23
  199.2 4.6 %collective-permute-start.22 = (bf16[32,16,256]{2,1,0:T(8,128)(2,1)}, bf16[32,16,256]{2,1,0:T(8,128)(2,1)S(1)}, u32[]{:S(2)}, u32[]{:S(2)}) collective-permute-start(bf16[32,16,256]{2,1,0:T(8,128)(2,1)} %get-tuple-element.90), channel_id=1, source_target_pairs={{0,384},{128,0},{256,128},{384,256},{1,385},{129,1},{257,129},{385... | collective-permute-start | bytes 786440 | tf_op jit(solution)/shard_map/ppermute | solution.py:33
  204.9 4.6 %shard_map.104.before_ref = f32[264,16,128]{2,1,0:T(8,128)S(1)} custom-call(s32[4]{0:T(128)S(1)} %pad_add_fusion.where_ref, s32[3,16,64]{2,1,0:T(8,128)S(1)} %maximum_convert_fusion.ids_ref, bf16[49,16,256]{2,1,0:T(8,128)(2,1)S(1)} %copy-done.9, bf16[49,16,256]{2,1,0:T(8,128)(2,1)S(1)} %collective-permute-done.19.p1.r1, ...), custom_call_target="tpu_custom_call" | custom-call | flops 1000000 | bytes 1000000 | tf_op jit(solution)/shard_map/pallas_call | solution.py:550
  211.1 7.5 %collective-permute-start.23 = (bf16[8,16,256]{2,1,0:T(8,128)(2,1)S(1)}, bf16[8,16,256]{2,1,0:T(8,128)(2,1)S(1)}, u32[]{:S(2)}, u32[]{:S(2)}) collective-permute-start(bf16[8,16,256]{2,1,0:T(8,128)(2,1)S(1)} %get-tuple-element.96), channel_id=1, source_target_pairs={{0,64},{64,0},{1,65},{65,1},{2,66},{66,2},{3,67},{67,3},{4,68},{68... | collective-permute-start | bytes 196616 | tf_op jit(solution)/shard_map/ppermute | solution.py:33
  226.2 3.9 %all-to-all-start.5 = ((bf16[8,9,16,256]{3,2,1,0:T(8,128)(2,1)}), bf16[8,9,16,256]{3,2,1,0:T(8,128)(2,1)S(1)}, u32[]{:S(2)}, u32[]{:S(2)}) async-start(bf16[8,9,16,256]{3,2,1,0:T(8,128)(2,1)} %shard_map.108), calls=%async_computation.5 | async-start | bytes 1179648 | tf_op jit(solution)/shard_map/all_to_all | solution.py:23
  231.9 8.4 %all-to-all-done.5.total_ref = bf16[8,9,16,256]{3,2,1,0:T(8,128)(2,1)S(1)} async-done(((bf16[8,9,16,256]{3,2,1,0:T(8,128)(2,1)}), bf16[8,9,16,256]{3,2,1,0:T(8,128)(2,1)S(1)}, u32[]{:S(2)}, u32[]{:S(2)}) %all-to-all-start.5) | async-done | bytes 589856 | tf_op jit(solution)/shard_map/all_to_all | solution.py:23
  (116 shorter events, 74.5 us)
Async XLA Ops:
  0.6 10.9 %collective-permute-start = (s32[1,3]{1,0:T(1,128)}, s32[1,3]{1,0:T(1,128)S(1)}, u32[]{:S(2)}, u32[]{:S(2)}) collective-permute-start(s32[1,3]{1,0:T(1,128)} %own_ref.1), channel_id=1, source_target_pairs={{0,64},{64,0},{1,65},{65,1},{2,66},{66,2},{3,67},{67,3},{4,68},{68... | collective-permute-start | bytes 44 | tf_op jit(solution)/shard_map/ppermute | solution.py:33
  9.6 19.0 %collective-permute-start.1 = (bf16[128,16,128]{2,1,0:T(8,128)(2,1)}, bf16[128,16,128]{2,1,0:T(8,128)(2,1)S(1)}, u32[]{:S(2)}, u32[]{:S(2)}) collective-permute-start(bf16[128,16,128]{2,1,0:T(8,128)(2,1)} %f0.3), channel_id=1, source_target_pairs={{0,128},{128,256},{256,384},{384,0},{1,129},{129,257},{257,385},{3... | collective-permute-start | bytes 1572872 | tf_op jit(solution)/shard_map/ppermute | solution.py:33
  14.4 25.9 %all-to-all-start = ((bf16[16,16,384]{2,1,0:T(8,128)(2,1)}), bf16[16,16,384]{2,1,0:T(8,128)(2,1)S(1)}, u32[]{:S(2)}, u32[]{:S(2)}) async-start(bf16[16,16,384]{2,1,0:T(8,128)(2,1)} %shard_map.93), calls=%async_computation | async-start | bytes 393216 | tf_op jit(solution)/shard_map/all_to_all | solution.py:23
  25.2 15.0 %collective-permute-start.3 = (bf16[128,16,128]{2,1,0:T(8,128)(2,1)}, bf16[128,16,128]{2,1,0:T(8,128)(2,1)S(1)}, u32[]{:S(2)}, u32[]{:S(2)}) collective-permute-start(bf16[128,16,128]{2,1,0:T(8,128)(2,1)} %f0.3), channel_id=1, source_target_pairs={{0,384},{128,0},{256,128},{384,256},{1,385},{129,1},{257,129},{385... | collective-permute-start | bytes 1572872 | tf_op jit(solution)/shard_map/ppermute | solution.py:33
  28.6 11.6 %collective-permute-start.2 = (bf16[64,16,128]{2,1,0:T(8,128)(2,1)S(1)}, bf16[64,16,128]{2,1,0:T(8,128)(2,1)S(1)}, u32[]{:S(2)}, u32[]{:S(2)}) collective-permute-start(bf16[64,16,128]{2,1,0:T(8,128)(2,1)S(1)} %slice.69), channel_id=1, source_target_pairs={{0,128},{128,256},{256,384},{384,0},{1,129},{129,257},{257,385},{3... | collective-permute-start | bytes 786440 | tf_op jit(solution)/shard_map/ppermute | solution.py:33
  41.1 12.0 %all-to-all-start.1 = ((bf16[4,272,256]{2,1,0:T(8,128)(2,1)}), bf16[4,272,256]{2,1,0:T(8,128)(2,1)S(1)}, u32[]{:S(2)}, u32[]{:S(2)}) async-start(bf16[4,272,256]{2,1,0:T(8,128)(2,1)} %shard_map.94), calls=%async_computation.1 | async-start | bytes 1114112 | tf_op jit(solution)/shard_map/all_to_all | solution.py:23
  63.8 59.9 %all-to-all-start.2 = ((bf16[64,16,384]{2,1,0:T(8,128)(2,1)}), bf16[64,16,384]{2,1,0:T(8,128)(2,1)S(1)}, u32[]{:S(2)}, u32[]{:S(2)}) async-start(bf16[64,16,384]{2,1,0:T(8,128)(2,1)} %shard_map.97), calls=%async_computation.2 | async-start | bytes 1572864 | tf_op jit(solution)/shard_map/all_to_all | solution.py:23
  78.6 16.3 %collective-permute-start.9 = (bf16[1024,256]{1,0:T(8,128)(2,1)S(1)}, bf16[1024,256]{1,0:T(8,128)(2,1)S(1)}, u32[]{:S(2)}, u32[]{:S(2)}) collective-permute-start(bf16[1024,256]{1,0:T(8,128)(2,1)S(1)} %bitcast.17), channel_id=1, source_target_pairs={{0,384},{128,0},{256,128},{384,256},{1,385},{129,1},{257,129},{385... | collective-permute-start | bytes 1572872 | tf_op jit(solution)/shard_map/ppermute | solution.py:33
  83.9 16.4 %collective-permute-start.7 = (bf16[1024,256]{1,0:T(8,128)(2,1)S(1)}, bf16[1024,256]{1,0:T(8,128)(2,1)S(1)}, u32[]{:S(2)}, u32[]{:S(2)}) collective-permute-start(bf16[1024,256]{1,0:T(8,128)(2,1)S(1)} %bitcast.18), channel_id=1, source_target_pairs={{0,128},{128,256},{256,384},{384,0},{1,129},{129,257},{257,385},{3... | collective-permute-start | bytes 1572872 | tf_op jit(solution)/shard_map/ppermute | solution.py:33
  85.9 16.3 %collective-permute-start.6 = (bf16[256,1024]{1,0:T(8,128)(2,1)S(1)}, bf16[256,1024]{1,0:T(8,128)(2,1)S(1)}, u32[]{:S(2)}, u32[]{:S(2)}) collective-permute-start(bf16[256,1024]{1,0:T(8,128)(2,1)S(1)} %pad_maximum_fusion), channel_id=1, source_target_pairs={{0,64},{64,0},{1,65},{65,1},{2,66},{66,2},{3,67},{67,3},{4,68},{68... | collective-permute-start | bytes 1572872 | tf_op jit(solution)/shard_map/ppermute | solution.py:33
  126.3 51.0 %all-to-all-start.3 = ((bf16[64,16,384]{2,1,0:T(8,128)(2,1)}), bf16[64,16,384]{2,1,0:T(8,128)(2,1)S(1)}, u32[]{:S(2)}, u32[]{:S(2)}) async-start(bf16[64,16,384]{2,1,0:T(8,128)(2,1)} %bitcast.10), calls=%async_computation.3 | async-start | bytes 1572864 | tf_op jit(solution)/shard_map/all_to_all | solution.py:23
  141.5 12.9 %collective-permute-start.13 = (bf16[1024,256]{1,0:T(8,128)(2,1)S(1)}, bf16[1024,256]{1,0:T(8,128)(2,1)S(1)}, u32[]{:S(2)}, u32[]{:S(2)}) collective-permute-start(bf16[1024,256]{1,0:T(8,128)(2,1)S(1)} %get-tuple-element.72), channel_id=1, source_target_pairs={{0,128},{128,256},{256,384},{384,0},{1,129},{129,257},{257,385},{3... | collective-permute-start | bytes 1572872 | tf_op jit(solution)/shard_map/ppermute | solution.py:33
  143.4 11.9 %collective-permute-start.14 = (bf16[1024,256]{1,0:T(8,128)(2,1)S(1)}, bf16[1024,256]{1,0:T(8,128)(2,1)S(1)}, u32[]{:S(2)}, u32[]{:S(2)}) collective-permute-start(bf16[1024,256]{1,0:T(8,128)(2,1)S(1)} %get-tuple-element.74), channel_id=1, source_target_pairs={{0,384},{128,0},{256,128},{384,256},{1,385},{129,1},{257,129},{385... | collective-permute-start | bytes 1572872 | tf_op jit(solution)/shard_map/ppermute | solution.py:33
  156.1 18.5 %collective-permute-start.15 = (bf16[256,256]{1,0:T(8,128)(2,1)S(1)}, bf16[256,256]{1,0:T(8,128)(2,1)S(1)}, u32[]{:S(2)}, u32[]{:S(2)}) collective-permute-start(bf16[256,256]{1,0:T(8,128)(2,1)S(1)} %get-tuple-element.76), channel_id=1, source_target_pairs={{0,16},{16,32},{32,48},{48,0},{1,17},{17,33},{33,49},{49,1},{2,18}... | collective-permute-start | bytes 393224 | tf_op jit(solution)/shard_map/ppermute | solution.py:33
  158.7 15.8 %collective-permute-start.16 = (bf16[256,256]{1,0:T(8,128)(2,1)S(1)}, bf16[256,256]{1,0:T(8,128)(2,1)S(1)}, u32[]{:S(2)}, u32[]{:S(2)}) collective-permute-start(bf16[256,256]{1,0:T(8,128)(2,1)S(1)} %get-tuple-element.77), channel_id=1, source_target_pairs={{0,32},{16,48},{32,0},{48,16},{1,33},{17,49},{33,1},{49,17},{2,34}... | collective-permute-start | bytes 393224 | tf_op jit(solution)/shard_map/ppermute | solution.py:33
  163.2 11.3 %collective-permute-start.17 = (bf16[256,256]{1,0:T(8,128)(2,1)S(1)}, bf16[256,256]{1,0:T(8,128)(2,1)S(1)}, u32[]{:S(2)}, u32[]{:S(2)}) collective-permute-start(bf16[256,256]{1,0:T(8,128)(2,1)S(1)} %get-tuple-element.78), channel_id=1, source_target_pairs={{0,48},{16,0},{32,16},{48,32},{1,49},{17,1},{33,17},{49,33},{2,50}... | collective-permute-start | bytes 393224 | tf_op jit(solution)/shard_map/ppermute | solution.py:33
  179.3 17.1 %collective-permute-start.20 = (bf16[49,16,256]{2,1,0:T(8,128)(2,1)S(1)}, bf16[49,16,256]{2,1,0:T(8,128)(2,1)S(1)}, u32[]{:S(2)}, u32[]{:S(2)}) collective-permute-start(bf16[49,16,256]{2,1,0:T(8,128)(2,1)S(1)} %get-tuple-element.86.p0), channel_id=1, source_target_pairs={{0,384},{128,0},{256,128},{384,256},{1,385},{129,1},{257,129},{385... | collective-permute-start | bytes 1204232 | tf_op jit(solution)/shard_map/ppermute | solution.py:33
  184.8 11.6 %collective-permute-start.19 = (bf16[49,16,256]{2,1,0:T(8,128)(2,1)S(1)}, bf16[49,16,256]{2,1,0:T(8,128)(2,1)S(1)}, u32[]{:S(2)}, u32[]{:S(2)}) collective-permute-start(bf16[49,16,256]{2,1,0:T(8,128)(2,1)S(1)} %get-tuple-element.86.p0), channel_id=1, source_target_pairs={{0,128},{128,256},{256,384},{384,0},{1,129},{129,257},{257,385},{3... | collective-permute-start | bytes 1204232 | tf_op jit(solution)/shard_map/ppermute | solution.py:33
  186.8 22.7 %all-to-all-start.4 = ((bf16[16,16,256]{2,1,0:T(8,128)(2,1)}), bf16[16,16,256]{2,1,0:T(8,128)(2,1)}, u32[]{:S(2)}, u32[]{:S(2)}) async-start(bf16[16,16,256]{2,1,0:T(8,128)(2,1)} %bitcast.11), calls=%async_computation.4 | async-start | bytes 262144 | tf_op jit(solution)/shard_map/all_to_all | solution.py:23
  197.3 12.2 %collective-permute-start.21 = (bf16[33,16,256]{2,1,0:T(8,128)(2,1)}, bf16[33,16,256]{2,1,0:T(8,128)(2,1)S(1)}, u32[]{:S(2)}, u32[]{:S(2)}) collective-permute-start(bf16[33,16,256]{2,1,0:T(8,128)(2,1)} %get-tuple-element.89), channel_id=1, source_target_pairs={{0,128},{128,256},{256,384},{384,0},{1,129},{129,257},{257,385},{3... | collective-permute-start | bytes 811016 | tf_op jit(solution)/shard_map/ppermute | solution.py:33
  199.2 10.3 %collective-permute-start.22 = (bf16[32,16,256]{2,1,0:T(8,128)(2,1)}, bf16[32,16,256]{2,1,0:T(8,128)(2,1)S(1)}, u32[]{:S(2)}, u32[]{:S(2)}) collective-permute-start(bf16[32,16,256]{2,1,0:T(8,128)(2,1)} %get-tuple-element.90), channel_id=1, source_target_pairs={{0,384},{128,0},{256,128},{384,256},{1,385},{129,1},{257,129},{385... | collective-permute-start | bytes 786440 | tf_op jit(solution)/shard_map/ppermute | solution.py:33
  211.1 12.3 %collective-permute-start.23 = (bf16[8,16,256]{2,1,0:T(8,128)(2,1)S(1)}, bf16[8,16,256]{2,1,0:T(8,128)(2,1)S(1)}, u32[]{:S(2)}, u32[]{:S(2)}) collective-permute-start(bf16[8,16,256]{2,1,0:T(8,128)(2,1)S(1)} %get-tuple-element.96), channel_id=1, source_target_pairs={{0,64},{64,0},{1,65},{65,1},{2,66},{66,2},{3,67},{67,3},{4,68},{68... | collective-permute-start | bytes 196616 | tf_op jit(solution)/shard_map/ppermute | solution.py:33
  224.3 16.9 %collective-permute-start.24 = (bf16[64,16,256]{2,1,0:T(8,128)(2,1)}, bf16[64,16,256]{2,1,0:T(8,128)(2,1)S(1)}, u32[]{:S(2)}, u32[]{:S(2)}) collective-permute-start(bf16[64,16,256]{2,1,0:T(8,128)(2,1)} %get-tuple-element.103), channel_id=1, source_target_pairs={{0,64},{64,0},{1,65},{65,1},{2,66},{66,2},{3,67},{67,3},{4,68},{68... | collective-permute-start | bytes 1572872 | tf_op jit(solution)/shard_map/ppermute | solution.py:33
  226.2 14.2 %all-to-all-start.5 = ((bf16[8,9,16,256]{3,2,1,0:T(8,128)(2,1)}), bf16[8,9,16,256]{3,2,1,0:T(8,128)(2,1)S(1)}, u32[]{:S(2)}, u32[]{:S(2)}) async-start(bf16[8,9,16,256]{3,2,1,0:T(8,128)(2,1)} %shard_map.108), calls=%async_computation.5 | async-start | bytes 1179648 | tf_op jit(solution)/shard_map/all_to_all | solution.py:23
  (28 other events, 369.1 us)
